TPU v7x, 256 devices: a whole 4x4x8 slice. The times are simulated.
256 devices in a mesh: gx: 2 (over x_hi), gy: 64 (over z, y, x_lo), gz: 2 (over core).
Axes of the slice: x: 4 (x_hi: 2, x_lo: 2; x = x_hi * 2 + x_lo), y: 4, z: 8, core: 2. Of those that a mesh axis runs over, the one named last changes fastest.
Arguments:
- adjoint_load: float32 [3, 16, 512, 256], P(None, 'gx', 'gy', 'gz'), may hold values from -6 to 6
- levels: int32 [8, 256, 128], P('gx', 'gy', 'gz'), may hold values from 0 to 15
- fine_stiffness: float32 [81, 81], replicated, may hold values from -0.025 to 2, as said below
- coarse_stiffness: float32 [24, 24], replicated, may hold values from -0.14 to 3.2, as said below
Outputs:
- preconditioned: float32 [3, 16, 512, 256], P(None, 'gx', 'gy', 'gz')
Inputs may be any that keep to these rules, and one draw needn't show every extreme that they name: `fine_stiffness`: symmetric; off-diagonal entries are at most zero; each diagonal entry exceeds the sum of the magnitudes of the other entries of its row by a positive margin. `coarse_stiffness`: symmetric; off-diagonal entries are at most zero; each diagonal entry exceeds the sum of the magnitudes of the other entries of its row by a positive margin.
All inputs are finite; a program needn't handle non-finite values.
Results may differ from a plain program's by a relative error of at most 0.0003.
Values sent between devices are 32-bit elements; how exact they have to be, the bound alone decides.
No kernel may reach another device: no remote copies, remote signals or barrier semaphores. Data moves between devices by JAX's collectives and lax.ppermute only.
A program may use at most 64 MiB of HBM per device.

v0:
```python
import functools

import jax
import jax.numpy as jnp
import numpy as np
from jax import lax
from jax.experimental import pallas as pl
from jax.experimental.pallas import tpu as pltpu
from jax.sharding import PartitionSpec as P

DEG = 4
DENSITY_LEVELS = 16
MID = 1.125
HALF = 0.875

F32 = jnp.float32
BF16 = jnp.bfloat16
EXACT = lax.Precision.HIGHEST

OWN = 4
REACH = 12
ROWS = OWN + 2 * REACH
LANES = 1024
WIDE = LANES + 128
PACK = 104


def node_row(group, row):
    px, py = ((0, 0), (1, 0), (0, 1))[group]
    if row < 6:
        return row % 3, px, py, row // 3
    return group, 1, 1, row - 6


FINE_IN = [(g, sx, sy) for sx, sy, groups in ((0, 0, (0, 1, 2)), (1, 0, (0, 2)), (0, 1, (0, 1)), (1, 1, (0,))) for g in groups]
SHIFTS = [(0, 0), (1, 0), (0, 1), (1, 1)]


def fine_place(group, row, sx, sy, sz):
    p, px, py, pz = node_row(group, row)
    if (sx and px) or (sy and py) or (sz and pz):
        return None
    return 27 * p + 9 * (px + 2 * sx) + 3 * (py + 2 * sy) + pz + 2 * sz


def coarse_place(row, sx, sy, sz):
    return 8 * row + 4 * sx + 2 * sy + sz if row < 3 else None


def fine_selectors():
    out_rows = np.zeros((128, 81), np.float32)
    in_rows = np.zeros((256, 81), np.float32)
    at = 0
    for sz in (0, 1):
        for g, sx, sy in FINE_IN:
            for row in range(8):
                place = fine_place(g, row, sx, sy, sz)
                if place is not None:
                    out_rows[at + row, place] = 1.0
            at += 8
    at = 0
    for g, sx, sy in FINE_IN:
        for sz in (0, 1):
            for row in range(8):
                place = fine_place(g, row, sx, sy, sz)
                if place is not None:
                    in_rows[at + row, place] = 1.0
                    in_rows[at + 8 + row, place] = 1.0
            at += 16
    return out_rows, in_rows


def coarse_selectors():
    out_rows = np.zeros((64, 24), np.float32)
    in_rows = np.zeros((128, 24), np.float32)
    at = 0
    for sz in (0, 1):
        for sx, sy in SHIFTS:
            for row in range(3):
                out_rows[at + row, coarse_place(row, sx, sy, sz)] = 1.0
            at += 8
    at = 0
    for sx, sy in SHIFTS:
        for sz in (0, 1):
            for row in range(3):
                in_rows[at + row, coarse_place(row, sx, sy, sz)] = 1.0
                in_rows[at + 8 + row, coarse_place(row, sx, sy, sz)] = 1.0
            at += 16
    return out_rows, in_rows


def weight_along(parity, shift):
    if parity == 0:
        return 1.0 if shift == 0 else 0.0
    return 0.5


def prolong_weights():
    weights = np.zeros((24, 128), np.float32)
    at = 0
    for sx, sy in SHIFTS:
        for sz in (0, 1):
            for g in range(3):
                for row in range(8):
                    p, px, py, pz = node_row(g, row)
                    w = weight_along(px, sx) * weight_along(py, sy) * weight_along(pz, sz)
                    weights[8 * g + row, at + p] = w
                    weights[8 * g + row, at + 8 + p] = w
            at += 16
    return weights


def restrict_weights():
    weights = np.zeros((64, 48), np.float32)
    at = 0
    for sz in (0, 1):
        for sx, sy in SHIFTS:
            for g in range(3):
                for row in range(8):
                    p, px, py, pz = node_row(g, row)
                    w = weight_along(px, sx) * weight_along(py, sy) * weight_along(pz, sz)
                    weights[at + p, 16 * g + row] = w
                    weights[at + p, 16 * g + 8 + row] = w
            at += 8
    return weights


def row_shuffle():
    shuffle = np.zeros((96, 96), np.float32)
    for y in range(4):
        for g in range(3):
            for row in range(8):
                p, px, py, pz = node_row(g, row)
                shuffle[24 * y + 8 * g + row, pz * 48 + p * 16 + px * 8 + 2 * y + py] = 1.0
    return shuffle


def exact_dot(a, b):
    return jnp.dot(a, b, precision=EXACT, preferred_element_type=F32)


def pack_kernel(place_ref, load_ref, load_other_ref, levels_ref, levels_other_ref, shuffle_ref, out_ref):
    gz = place_ref[2]

    def spread(half):
        row = lax.broadcasted_iota(jnp.int32, (128, 256), 0)
        col = lax.broadcasted_iota(jnp.int32, (128, 256), 1)
        source = 2 * (col % 128) + col // 128
        return (source == row + 128 * half).astype(F32)

    def widen(half):
        row = lax.broadcasted_iota(jnp.int32, (64, 128), 0)
        col = lax.broadcasted_iota(jnp.int32, (64, 128), 1)
        return (col == row + 64 * half).astype(F32)

    own_spread, other_spread = spread(gz), spread(1 - gz)
    own_widen, other_widen = widen(gz), widen(1 - gz)
    for x in range(4):
        lanes = slice(128 * x, 128 * x + 128)
        own = load_ref[:, 2 * x : 2 * x + 2].reshape(48, 128)
        other = load_other_ref[:, 2 * x : 2 * x + 2].reshape(48, 128)
        parted = exact_dot(own, own_spread) + exact_dot(other, other_spread)
        stacked = jnp.concatenate([parted[:, :128], parted[:, 128:]], axis=0)
        out_ref[0:96, lanes] = exact_dot(shuffle_ref[...], stacked)
        level = exact_dot(levels_ref[x].astype(F32), own_widen) + exact_dot(
            levels_other_ref[x].astype(F32), other_widen
        )
        ratio = level / (DENSITY_LEVELS - 1)
        out_ref[96:100, lanes] = 0.05 + 0.95 * ratio * ratio * ratio
        out_ref[100:104, lanes] = jnp.zeros((4, 128), F32)


def split(values):
    high = values.astype(BF16).astype(F32)
    return jnp.concatenate([high, values - high], axis=0).astype(BF16)


def roll_tiles(values, step):
    tiles = []
    for t in range(values.shape[1] // 128):
        tile = values[:, 128 * t : 128 * t + 128]
        lane = lax.broadcasted_iota(jnp.int32, tile.shape, 1)
        if step == 1:
            tiles.append(jnp.where(lane < 127, pltpu.roll(tile, 127, 1), 0.0))
        else:
            tiles.append(jnp.where(lane > 0, pltpu.roll(tile, 1, 1), 0.0))
    return tiles[0] if len(tiles) == 1 else jnp.concatenate(tiles, axis=1)


def hi_lo_weights(weights):
    high = weights.astype(BF16).astype(F32)
    col = lax.broadcasted_iota(jnp.int32, weights.shape, 1)
    low = jnp.where(col % 16 < 8, weights - high, 0.0)
    return jnp.concatenate([high, low], axis=0).astype(BF16)


def scaled(values, moduli):
    rows, lanes = values.shape
    return (values.reshape(rows // 8, 8, lanes) * moduli[None]).reshape(rows, lanes)


def cycle_kernel(place_ref, *refs):
    blocks = refs[:14]
    (fine_ref, coarse_ref, fine_diag_ref, coarse_diag_ref, prolong_ref, restrict_ref, shuffle_ref) = refs[14:21]
    out_ref = refs[21]
    (load, moduli, inverse, res, step, total, fine_x, carry,
     fine_w, coarse_w, c_inverse, c_res, c_step, c_total, coarse_x, c_carry) = refs[22:]
    gx, gy, gz = place_ref[0], place_ref[1], place_ref[2]
    y_first = gy * OWN - REACH
    y_count = lax.mul(place_ref[3], OWN)

    def valid(y):
        at = y_first + y
        return jnp.where((at >= 0) & (at < y_count), 1.0, 0.0).astype(F32)

    own, own_x = blocks[0], blocks[1]
    side = 1 - 2 * gz
    spots = [(own, 0, gx), (own_x, 0, 1 - gx)]
    for s in (1, 2, 3):
        a, ax, za, zax = blocks[4 * s - 2 : 4 * s + 2]
        spots += [(a, -s * side, gx), (ax, -s * side, 1 - gx), (za, s * side, gx), (zax, s * side, 1 - gx)]
    for ref, offset, half in spots:
        first = REACH + OWN * offset
        lanes = pl.ds(pl.multiple_of(half * 512, 512), 512)
        for y in range(OWN):
            load[first + y, :, lanes] = ref[24 * y : 24 * y + 24, :]
            moduli[first + y, :, lanes] = jnp.broadcast_to(ref[96 + y : 97 + y, :], (8, 512))

    fine_w[...] = hi_lo_weights(fine_ref[...])
    coarse_w[...] = hi_lo_weights(coarse_ref[...])

    def clear_tail(y, _):
        fine_x[y, :, LANES:] = jnp.zeros((96, 128), BF16)
        coarse_x[y, :, LANES:] = jnp.zeros((32, 128), BF16)
        return 0

    lax.fori_loop(0, ROWS, clear_tail, 0)

    def store_fine(y, lanes, values):
        for g in range(3):
            part = values[8 * g : 8 * g + 8]
            fine_x[y, 32 * g : 32 * g + 16, lanes] = split(part)
            fine_x[y, 32 * g + 16 : 32 * g + 32, lanes] = split(roll_tiles(part, 1))

    def store_coarse(y, lanes, values):
        coarse_x[y, 0:16, lanes] = split(values)
        coarse_x[y, 16:32, lanes] = split(roll_tiles(values, 1))

    def fine_products(y, low):
        here, there = slice(low, low + 256), slice(low + 128, low + 384)
        operand = jnp.concatenate(
            [
                fine_x[y, :, here],
                fine_x[y, 0:32, there],
                fine_x[y, 64:96, there],
                fine_x[y + 1, 0:64, here],
                fine_x[y + 1, 0:32, there],
            ],
            axis=0,
        )
        products = jnp.dot(fine_w[...], operand, preferred_element_type=F32)
        return products[:128] + products[128:]

    def coarse_products(y, low):
        here, there = slice(low, low + 256), slice(low + 128, low + 384)
        operand = jnp.concatenate(
            [coarse_x[y, :, here], coarse_x[y, :, there], coarse_x[y + 1, :, here], coarse_x[y + 1, :, there]],
            axis=0,
        )
        return operand

    def pushed(before, values):
        return jnp.concatenate([before, values[:, :128]], axis=1)

    def fine_sweep(first, last, products_of, finish):
        carry[...] = jnp.zeros_like(carry)

        def row(y, _):
            before = [(jnp.zeros((16, 128), F32), jnp.zeros((8, 128), F32))] * 2
            for n in range(4):
                lanes = slice(256 * n, 256 * n + 256)
                values = scaled(products_of(y, 256 * n), moduli[y, :, lanes])
                sums = []
                for z in range(2):
                    v = values[64 * z : 64 * z + 64]
                    old = carry[16 * z : 16 * z + 16, lanes]
                    along_x = pushed(before[z][0], v[24:40])
                    along_xy = pushed(before[z][1], v[56:64])
                    before[z] = (v[24:40, 128:], v[56:64, 128:])
                    sums.append(
                        jnp.concatenate(
                            [v[0:8] + along_x[0:8] + old[0:8], v[8:16] + old[8:16], v[16:24] + along_x[8:16]], axis=0
                        )
                    )
                    carry[16 * z : 16 * z + 16, lanes] = jnp.concatenate([v[40:48] + along_xy, v[48:56]], axis=0)
                finish(y, lanes, sums[0] + roll_tiles(sums[1], -1))
            return 0

        lax.fori_loop(first, last, row, 0)

    def coarse_sweep(first, last, products_of, scale, finish):
        c_carry[...] = jnp.zeros_like(c_carry)

        def row(y, _):
            before = [(jnp.zeros((8, 128), F32), jnp.zeros((8, 128), F32))] * 2
            for n in range(4):
                lanes = slice(256 * n, 256 * n + 256)
                values = products_of(y, 256 * n)
                if scale:
                    values = scaled(values, moduli[y, :, lanes])
                sums = []
                for z in range(2):
                    v = values[32 * z : 32 * z + 32]
                    old = c_carry[8 * z : 8 * z + 8, lanes]
                    sums.append(v[0:8] + pushed(before[z][0], v[8:16]) + old)
                    c_carry[8 * z : 8 * z + 8, lanes] = v[16:24] + pushed(before[z][1], v[24:32])
                    before[z] = (v[8:16, 128:], v[24:32, 128:])
                finish(y, lanes, sums[0] + roll_tiles(sums[1], -1))
            return 0

        lax.fori_loop(first, last, row, 0)

    def over_moduli(diag_ref):
        def products_of(y, low):
            diag = diag_ref[...]
            return jnp.concatenate([diag, diag], axis=1)

        return products_of

    def start_fine(y, lanes, diag):
        ok = valid(y)
        inv = ok / jnp.where(ok > 0, diag, 1.0)
        inverse[y, :, lanes] = inv
        r = load[y, :, lanes]
        d = inv * r * (1.0 / MID)
        res[y, :, lanes] = r
        step[y, :, lanes] = d
        total[y, :, lanes] = d
        store_fine(y, lanes, d)

    o = REACH
    fine_sweep(o - 12, o + 15, over_moduli(fine_diag_ref), start_fine)

    sigma = MID / HALF
    rhos = [1.0 / sigma]
    for _ in range(DEG - 1):
        rhos.append(1.0 / (2.0 * sigma - rhos[-1]))
    factors = [(rhos[s + 1] * rhos[s], 2.0 * rhos[s + 1] / HALF) for s in range(DEG - 1)]

    def smooth_fine(keep, gain, with_operand):
        def finish(y, lanes, sums):
            r = res[y, :, lanes] - sums
            d = keep * step[y, :, lanes] + gain * (inverse[y, :, lanes] * r)
            res[y, :, lanes] = r
            step[y, :, lanes] = d
            total[y, :, lanes] = total[y, :, lanes] + d
            if with_operand:
                store_fine(y, lanes, d)

        return finish

    for s in range(DEG - 1):
        fine_sweep(o - 11 + s, o + 14 - s, fine_products, smooth_fine(*factors[s], True))

    def leave(y, lanes, sums):
        left = (res[y, :, lanes] - sums) * valid(y)
        for g in range(3):
            fine_x[y, 16 * g : 16 * g + 16, lanes] = split(left[8 * g : 8 * g + 8])

    fine_sweep(o - 8, o + 11, fine_products, leave)

    def restricted(y, low):
        return jnp.dot(restrict_ref[...], fine_x[y, 0:48, low : low + 256], preferred_element_type=F32)

    def keep_load(y, lanes, sums):
        c_res[y, :, lanes] = sums

    coarse_sweep(o - 8, o + 11, restricted, False, keep_load)

    def start_coarse(y, lanes, diag):
        ok = valid(y)
        used = (lax.broadcasted_iota(jnp.int32, diag.shape, 0) < 3) & (ok > 0)
        inv = jnp.where(used, 1.0 / jnp.where(used, diag, 1.0), 0.0)
        c_inverse[y, :, lanes] = inv
        d = inv * c_res[y, :, lanes] * (1.0 / MID)
        c_step[y, :, lanes] = d
        c_total[y, :, lanes] = d
        store_coarse(y, lanes, d)

    coarse_sweep(o - 8, o + 11, over_moduli(coarse_diag_ref), True, start_coarse)

    def coarse_product(y, low):
        products = jnp.dot(coarse_w[...], coarse_products(y, low), preferred_element_type=F32)
        return products[:64] + products[64:]

    def smooth_coarse(keep, gain, last):
        def finish(y, lanes, sums):
            r = c_res[y, :, lanes] - sums
            d = keep * c_step[y, :, lanes] + gain * (c_inverse[y, :, lanes] * r)
            t = c_total[y, :, lanes] + d
            c_res[y, :, lanes] = r
            c_step[y, :, lanes] = d
            c_total[y, :, lanes] = t
            store_coarse(y, lanes, t if last else d)

        return finish

    for s in range(DEG - 1):
        coarse_sweep(o - 7 + s, o + 10 - s, coarse_product, True, smooth_coarse(*factors[s], s == DEG - 2))

    def correct(y, _):
        for n in range(4):
            lanes = slice(256 * n, 256 * n + 256)
            t = total[y, :, lanes] + jnp.dot(prolong_ref[...], coarse_products(y, 256 * n), preferred_element_type=F32)
            total[y, :, lanes] = t
            store_fine(y, lanes, t)
        return 0

    lax.fori_loop(o - 4, o + 8, correct, 0)

    def restart(y, lanes, sums):
        r = load[y, :, lanes] - sums
        d = inverse[y, :, lanes] * r * (1.0 / MID)
        res[y, :, lanes] = r
        step[y, :, lanes] = d
        total[y, :, lanes] = total[y, :, lanes] + d
        store_fine(y, lanes, d)

    fine_sweep(o - 4, o + 7, fine_products, restart)
    for s in range(DEG - 1):
        fine_sweep(o - 3 + s, o + 6 - s, fine_products, smooth_fine(*factors[s], s < DEG - 2))

    row = lax.broadcasted_iota(jnp.int32, (128, 128), 0)
    col = lax.broadcasted_iota(jnp.int32, (128, 128), 1)
    mine = row == 64 * gz + col // 2
    weave = [(mine & (col % 2 == pz)).astype(F32) for pz in (0, 1)]
    for x in range(4):
        lanes = pl.ds(pl.multiple_of(gx * 512 + 128 * x, 128), 128)
        rows = total[REACH : REACH + OWN, :, lanes].reshape(96, 128)
        back = lax.dot_general(
            shuffle_ref[...], rows, (((0,), (0,)), ((), ())), precision=EXACT, preferred_element_type=F32
        )
        woven = exact_dot(back[0:48], weave[0]) + exact_dot(back[48:96], weave[1])
        out_ref[:, 2 * x : 2 * x + 2] = woven.reshape(3, 2, 8, 128)


def per_device(adjoint_load, levels, fine_stiffness, coarse_stiffness):
    count = lax.axis_size("gy")
    place = jnp.stack(
        [lax.axis_index("gx"), lax.axis_index("gy"), lax.axis_index("gz"), jnp.int32(count)]
    ).astype(jnp.int32)

    def swap(value, axis):
        return lax.ppermute(value, axis, [(0, 1), (1, 0)])

    def sided(value, steps):
        pairs = [(2 * i, 2 * (i + steps)) for i in range(count - steps)]
        pairs += [(2 * (i + steps) + 1, 2 * i + 1) for i in range(count - steps)]
        return lax.ppermute(value, ("gy", "gz"), pairs)

    whole = pl.BlockSpec(memory_space=pltpu.VMEM)
    scalars = pl.BlockSpec(memory_space=pltpu.SMEM)
    shuffle = jnp.asarray(row_shuffle())
    own = pl.pallas_call(
        pack_kernel,
        out_shape=jax.ShapeDtypeStruct((PACK, 512), F32),
        in_specs=[scalars] + [whole] * 5,
        out_specs=whole,
        name="pack",
    )(place, adjoint_load, swap(adjoint_load, "gz"), levels, swap(levels, "gz"), shuffle)

    blocks = [own, swap(own, "gx")]
    for s in (1, 2, 3):
        a = sided(own, s)
        ax = swap(a, "gx")
        blocks += [a, ax, swap(a, "gz"), swap(ax, "gz")]

    fine_out, fine_in = fine_selectors()
    coarse_out, coarse_in = coarse_selectors()
    fine = exact_dot(exact_dot(jnp.asarray(fine_out), fine_stiffness), jnp.asarray(fine_in.T))
    coarse = exact_dot(exact_dot(jnp.asarray(coarse_out), coarse_stiffness), jnp.asarray(coarse_in.T))
    fine_diag = exact_dot(jnp.asarray(fine_out), jnp.broadcast_to(jnp.diagonal(fine_stiffness)[:, None], (81, 128)))
    coarse_diag = exact_dot(
        jnp.asarray(coarse_out), jnp.broadcast_to(jnp.diagonal(coarse_stiffness)[:, None], (24, 128))
    )

    scratch = [
        pltpu.VMEM((ROWS, 24, LANES), F32),
        pltpu.VMEM((ROWS, 8, LANES), F32),
        pltpu.VMEM((ROWS, 24, LANES), F32),
        pltpu.VMEM((ROWS, 24, LANES), F32),
        pltpu.VMEM((ROWS, 24, LANES), F32),
        pltpu.VMEM((ROWS, 24, LANES), F32),
        pltpu.VMEM((ROWS, 96, WIDE), BF16),
        pltpu.VMEM((32, LANES), F32),
        pltpu.VMEM((256, 256), BF16),
        pltpu.VMEM((128, 128), BF16),
        pltpu.VMEM((ROWS, 8, LANES), F32),
        pltpu.VMEM((ROWS, 8, LANES), F32),
        pltpu.VMEM((ROWS, 8, LANES), F32),
        pltpu.VMEM((ROWS, 8, LANES), F32),
        pltpu.VMEM((ROWS, 32, WIDE), BF16),
        pltpu.VMEM((16, LANES), F32),
    ]
    return pl.pallas_call(
        cycle_kernel,
        out_shape=jax.ShapeDtypeStruct(adjoint_load.shape, F32),
        in_specs=[scalars] + [whole] * 21,
        out_specs=whole,
        scratch_shapes=scratch,
        compiler_params=pltpu.CompilerParams(vmem_limit_bytes=56 * 1024 * 1024),
        name="cycle",
    )(
        place,
        *blocks,
        fine,
        coarse,
        fine_diag,
        coarse_diag,
        jnp.asarray(prolong_weights(), dtype=BF16),
        jnp.asarray(restrict_weights(), dtype=BF16),
        shuffle,
    )


def solution(mesh):
    return jax.shard_map(
        per_device,
        mesh=mesh,
        in_specs=(P(None, "gx", "gy", "gz"), P("gx", "gy", "gz"), P(), P()),
        out_specs=P(None, "gx", "gy", "gz"),
        check_vma=False,
    )
```

profile of v0, /device:TPU:129, one launch (start us, length us, event | category | flops | bytes accessed | tf_op | source)
XLA Modules:
  0.0 141.7 jit_solution(7000275728183101904)
XLA Ops:
  0.0 0.0 copy-start
  0.0 0.7 collective-permute-start.1
  0.7 0.1 collective-permute-start
  0.8 0.0 copy-done
  0.8 0.0 copy-start.2
  0.8 1.7 %gather_fusion = f32[81]{0:T(128)S(1)} fusion(f32[81,81]{1,0:T(8,128)S(1)} %copy-done, s32[81]{0:T(128)S(1)} %or_bitcast_fusion.1), kind=kCustom, calls=%fused_computation | custom fusion | bytes 1296 | tf_op jit(solution)/shard_map/jit(diagonal)/cond/branch_0_fun/gather | solution.py:482
  2.5 0.0 copy-done.2
  2.5 0.2 fusion.4
  2.7 0.0 copy-start.18
  2.7 0.9 fusion.refs_16_
  3.6 0.0 copy-done.18
  3.6 0.9 fusion.5.refs_14_
  4.5 0.7 pad_add_fusion.place_ref
  5.2 0.0 copy-done.1
  5.2 0.8 gather_fusion.1
  6.0 0.0 collective-permute-done.1.levels_other_ref
  6.0 0.0 collective-permute-done.load_other_ref
  6.0 0.6 copy-done.20
  6.6 0.6 copy-done.17
  7.2 3.8 %pack.1.refs_0_ = f32[104,512]{1,0:T(8,128)} custom-call(s32[4]{0:T(128)} %pad_add_fusion.place_ref, f32[3,8,8,128]{3,2,1,0:T(8,128)} %load_ref.1, f32[3,8,8,128]{3,2,1,0:T(8,128)} %copy-done.17, s32[4,4,64]{2,1,0:T(4,128)} %levels_ref.1, s32[4,4,64]{2,1,0:T(4,128)} %copy-done.20, f32[96,96]{1,0:T(8,128)} %constant.38.clone.shuffle_ref.refs_20_), custom_call_target="tpu_custom_call" | custom-call | tf_op jit(solution)/shard_map/pack/pallas_call | solution.py:464
  11.0 5.4 %collective-permute-start.11 = (f32[104,512]{1,0:T(8,128)}, f32[104,512]{1,0:T(8,128)S(1)}, u32[]{:S(2)}, u32[]{:S(2)}) collective-permute-start(f32[104,512]{1,0:T(8,128)} %pack.1.refs_0_), channel_id=1, source_target_pairs={{0,6},{2,8},{4,10},{6,12},{8,14},{10,16},{12,18},{14,20},{16,22},{... | collective-permute-start | bytes 638984 | tf_op jit(solution)/shard_map/ppermute | solution.py:459
  16.5 2.7 %collective-permute-start.7 = (f32[104,512]{1,0:T(8,128)}, f32[104,512]{1,0:T(8,128)S(1)}, u32[]{:S(2)}, u32[]{:S(2)}) collective-permute-start(f32[104,512]{1,0:T(8,128)} %pack.1.refs_0_), channel_id=1, source_target_pairs={{0,4},{2,6},{4,8},{6,10},{8,12},{10,14},{12,16},{14,18},{16,20},{1... | collective-permute-start | bytes 638984 | tf_op jit(solution)/shard_map/ppermute | solution.py:459
  19.2 1.9 %collective-permute-start.3 = (f32[104,512]{1,0:T(8,128)}, f32[104,512]{1,0:T(8,128)S(1)}, u32[]{:S(2)}, u32[]{:S(2)}) collective-permute-start(f32[104,512]{1,0:T(8,128)} %pack.1.refs_0_), channel_id=1, source_target_pairs={{0,2},{2,4},{4,6},{6,8},{8,10},{10,12},{12,14},{14,16},{16,18},{18... | collective-permute-start | bytes 638984 | tf_op jit(solution)/shard_map/ppermute | solution.py:459
  21.1 0.0 copy-done.16
  21.1 0.2 fusion.6
  21.3 2.5 %collective-permute-start.2 = (f32[104,512]{1,0:T(8,128)}, f32[104,512]{1,0:T(8,128)S(1)}, u32[]{:S(2)}, u32[]{:S(2)}) collective-permute-start(f32[104,512]{1,0:T(8,128)} %pack.1.refs_0_), channel_id=1, source_target_pairs={{0,128},{128,0},{1,129},{129,1},{2,130},{130,2},{3,131},{131,3},{4... | collective-permute-start | bytes 638984 | tf_op jit(solution)/shard_map/ppermute | solution.py:454
  23.8 0.0 collective-permute-done.11.refs_10_
  23.8 2.4 %collective-permute-start.13 = (f32[104,512]{1,0:T(8,128)S(1)}, f32[104,512]{1,0:T(8,128)S(1)}, u32[]{:S(2)}, u32[]{:S(2)}) collective-permute-start(f32[104,512]{1,0:T(8,128)S(1)} %collective-permute-done.11.refs_10_), channel_id=1, source_target_pairs={{0,1},{1,0},{2,3},{3,2},{4,5},{5,4},{6,7},{7,6},{8,9},{9,8},{10,11... | collective-permute-start | bytes 638984 | tf_op jit(solution)/shard_map/ppermute | solution.py:454
  26.2 0.9 collective-permute-start.12
  27.1 0.0 collective-permute-done.7.refs_6_
  27.1 2.0 %collective-permute-start.8 = (f32[104,512]{1,0:T(8,128)S(1)}, f32[104,512]{1,0:T(8,128)S(1)}, u32[]{:S(2)}, u32[]{:S(2)}) collective-permute-start(f32[104,512]{1,0:T(8,128)S(1)} %collective-permute-done.7.refs_6_), channel_id=1, source_target_pairs={{0,128},{128,0},{1,129},{129,1},{2,130},{130,2},{3,131},{131,3},{4... | collective-permute-start | bytes 638984 | tf_op jit(solution)/shard_map/ppermute | solution.py:454
  29.2 0.0 collective-permute-done.3.refs_2_
  29.2 0.9 collective-permute-start.4
  30.1 0.0 copy-done.19
  30.1 0.8 fusion.7.refs_15_
  30.9 0.6 collective-permute-done.2.refs_1_
  31.4 7.7 %collective-permute-start.9 = (f32[104,512]{1,0:T(8,128)S(1)}, f32[104,512]{1,0:T(8,128)S(1)}, u32[]{:S(2)}, u32[]{:S(2)}) collective-permute-start(f32[104,512]{1,0:T(8,128)S(1)} %collective-permute-done.7.refs_6_), channel_id=1, source_target_pairs={{0,1},{1,0},{2,3},{3,2},{4,5},{5,4},{6,7},{7,6},{8,9},{9,8},{10,11... | collective-permute-start | bytes 638984 | tf_op jit(solution)/shard_map/ppermute | solution.py:454
  39.1 0.0 collective-permute-done.13.refs_12_
  39.1 0.1 collective-permute-start.5
  39.2 0.0 collective-permute-done.12.refs_11_
  39.2 4.5 %collective-permute-start.14 = (f32[104,512]{1,0:T(8,128)S(1)}, f32[104,512]{1,0:T(8,128)S(1)}, u32[]{:S(2)}, u32[]{:S(2)}) collective-permute-start(f32[104,512]{1,0:T(8,128)S(1)} %collective-permute-done.12.refs_11_), channel_id=1, source_target_pairs={{0,1},{1,0},{2,3},{3,2},{4,5},{5,4},{6,7},{7,6},{8,9},{9,8},{10,11... | collective-permute-start | bytes 638984 | tf_op jit(solution)/shard_map/ppermute | solution.py:454
  43.7 0.0 collective-permute-done.8.refs_7_
  43.7 3.0 %collective-permute-start.10 = (f32[104,512]{1,0:T(8,128)S(1)}, f32[104,512]{1,0:T(8,128)S(1)}, u32[]{:S(2)}, u32[]{:S(2)}) collective-permute-start(f32[104,512]{1,0:T(8,128)S(1)} %collective-permute-done.8.refs_7_), channel_id=1, source_target_pairs={{0,1},{1,0},{2,3},{3,2},{4,5},{5,4},{6,7},{7,6},{8,9},{9,8},{10,11... | collective-permute-start | bytes 638984 | tf_op jit(solution)/shard_map/ppermute | solution.py:454
  46.7 0.0 collective-permute-done.4.refs_3_
  46.7 2.3 %collective-permute-start.6 = (f32[104,512]{1,0:T(8,128)S(1)}, f32[104,512]{1,0:T(8,128)S(1)}, u32[]{:S(2)}, u32[]{:S(2)}) collective-permute-start(f32[104,512]{1,0:T(8,128)S(1)} %collective-permute-done.4.refs_3_), channel_id=1, source_target_pairs={{0,1},{1,0},{2,3},{3,2},{4,5},{5,4},{6,7},{7,6},{8,9},{9,8},{10,11... | collective-permute-start | bytes 638984 | tf_op jit(solution)/shard_map/ppermute | solution.py:454
  49.0 0.8 fusion.2.refs_17_
  49.8 0.0 collective-permute-done.9.refs_8_
  49.8 0.0 collective-permute-done.5.refs_4_
  49.8 0.0 copy-start.12
  49.8 0.0 collective-permute-done.14.refs_13_
  49.9 0.0 copy-start.13
  49.9 0.0 collective-permute-done.10.refs_9_
  49.9 0.0 copy-start.14
  49.9 0.2 collective-permute-done.6.refs_5_
  50.1 0.0 copy-done.3
  50.1 0.0 copy-done.4
  50.1 0.0 copy-done.5
  50.1 0.0 copy-done.6
  50.1 0.4 copy-done.11
  50.5 0.1 copy-done.12
  50.6 0.1 copy-done.13
  50.7 0.1 copy-done.14
  50.7 0.7 copy-done.15
  51.4 90.2 %cycle.1 = f32[3,8,8,128]{3,2,1,0:T(8,128)} custom-call(s32[4]{0:T(128)} %pad_add_fusion.place_ref, f32[104,512]{1,0:T(8,128)} %pack.1.refs_0_, f32[104,512]{1,0:T(8,128)} %copy-done.6, f32[104,512]{1,0:T(8,128)} %copy-done.5, f32[104,512]{1,0:T(8,128)} %copy-done.10, f32[104,512]{1,0:T(8,128)} %copy-done.12, f32[104,512]{1,0:T(8,128)} %copy-done.15, ...), custom_call_target="tpu_custom_call" | custom-call | tf_op jit(solution)/shard_map/cycle/pallas_call | solution.py:505
  (21 shorter events, 0.0 us)
Async XLA Ops:
  0.0 0.8 copy-start
  0.0 6.0 %collective-permute-start.1 = (s32[4,4,64]{2,1,0:T(4,128)}, s32[4,4,64]{2,1,0:T(4,128)S(1)}, u32[]{:S(2)}, u32[]{:S(2)}) collective-permute-start(s32[4,4,64]{2,1,0:T(4,128)} %levels_ref.1), channel_id=1, source_target_pairs={{0,1},{1,0},{2,3},{3,2},{4,5},{5,4},{6,7},{7,6},{8,9},{9,8},{10,11... | collective-permute-start | bytes 12296 | tf_op jit(solution)/shard_map/ppermute | solution.py:454
  0.7 5.3 %collective-permute-start = (f32[3,8,8,128]{3,2,1,0:T(8,128)}, f32[3,8,8,128]{3,2,1,0:T(8,128)S(1)}, u32[]{:S(2)}, u32[]{:S(2)}) collective-permute-start(f32[3,8,8,128]{3,2,1,0:T(8,128)} %load_ref.1), channel_id=1, source_target_pairs={{0,1},{1,0},{2,3},{3,2},{4,5},{5,4},{6,7},{7,6},{8,9},{9,8},{10,11... | collective-permute-start | bytes 294920 | tf_op jit(solution)/shard_map/ppermute | solution.py:454
  0.8 1.7 %copy-start.2 = (f32[128,81]{1,0:T(8,128)S(1)}, f32[128,81]{1,0:T(8,128)}, u32[]{:S(2)}) copy-start(f32[128,81]{1,0:T(8,128)} %constant.39.clone) | copy-start | bytes 124420
  2.7 0.9 copy-start.18
  3.6 1.6 %copy-start.1 = (f32[24,24]{1,0:T(8,128)S(1)}, f32[24,24]{1,0:T(8,128)}, u32[]{:S(2)}) copy-start(f32[24,24]{1,0:T(8,128)} %param.14) | copy-start | bytes 6916
  6.0 15.1 %copy-start.16 = (f32[64,24]{1,0:T(8,128)S(1)}, f32[64,24]{1,0:T(8,128)}, u32[]{:S(2)}) copy-start(f32[64,24]{1,0:T(8,128)} %constant.41.clone) | copy-start | bytes 18436
  6.0 0.6 copy-start.20
  6.6 0.6 copy-start.17
  11.0 19.1 %copy-start.19 = (f32[24,128]{1,0:T(8,128)S(1)}, f32[24,128]{1,0:T(8,128)}, u32[]{:S(2)}) copy-start(f32[24,128]{1,0:T(8,128)} %constant.42.clone) | copy-start | bytes 36868
  11.0 12.7 %collective-permute-start.11 = (f32[104,512]{1,0:T(8,128)}, f32[104,512]{1,0:T(8,128)S(1)}, u32[]{:S(2)}, u32[]{:S(2)}) collective-permute-start(f32[104,512]{1,0:T(8,128)} %pack.1.refs_0_), channel_id=1, source_target_pairs={{0,6},{2,8},{4,10},{6,12},{8,14},{10,16},{12,18},{14,20},{16,22},{... | collective-permute-start | bytes 638984 | tf_op jit(solution)/shard_map/ppermute | solution.py:459
  16.5 10.7 %collective-permute-start.7 = (f32[104,512]{1,0:T(8,128)}, f32[104,512]{1,0:T(8,128)S(1)}, u32[]{:S(2)}, u32[]{:S(2)}) collective-permute-start(f32[104,512]{1,0:T(8,128)} %pack.1.refs_0_), channel_id=1, source_target_pairs={{0,4},{2,6},{4,8},{6,10},{8,12},{10,14},{12,16},{14,18},{16,20},{1... | collective-permute-start | bytes 638984 | tf_op jit(solution)/shard_map/ppermute | solution.py:459
  19.2 10.0 %collective-permute-start.3 = (f32[104,512]{1,0:T(8,128)}, f32[104,512]{1,0:T(8,128)S(1)}, u32[]{:S(2)}, u32[]{:S(2)}) collective-permute-start(f32[104,512]{1,0:T(8,128)} %pack.1.refs_0_), channel_id=1, source_target_pairs={{0,2},{2,4},{4,6},{6,8},{8,10},{10,12},{12,14},{14,16},{16,18},{18... | collective-permute-start | bytes 638984 | tf_op jit(solution)/shard_map/ppermute | solution.py:459
  21.3 10.2 %collective-permute-start.2 = (f32[104,512]{1,0:T(8,128)}, f32[104,512]{1,0:T(8,128)S(1)}, u32[]{:S(2)}, u32[]{:S(2)}) collective-permute-start(f32[104,512]{1,0:T(8,128)} %pack.1.refs_0_), channel_id=1, source_target_pairs={{0,128},{128,0},{1,129},{129,1},{2,130},{130,2},{3,131},{131,3},{4... | collective-permute-start | bytes 638984 | tf_op jit(solution)/shard_map/ppermute | solution.py:454
  23.8 26.3 %copy-start.3 = (f32[104,512]{1,0:T(8,128)}, f32[104,512]{1,0:T(8,128)S(1)}, u32[]{:S(2)}) copy-start(f32[104,512]{1,0:T(8,128)S(1)} %collective-permute-done.11.refs_10_) | copy-start | bytes 638980
  23.8 15.3 %collective-permute-start.13 = (f32[104,512]{1,0:T(8,128)S(1)}, f32[104,512]{1,0:T(8,128)S(1)}, u32[]{:S(2)}, u32[]{:S(2)}) collective-permute-start(f32[104,512]{1,0:T(8,128)S(1)} %collective-permute-done.11.refs_10_), channel_id=1, source_target_pairs={{0,1},{1,0},{2,3},{3,2},{4,5},{5,4},{6,7},{7,6},{8,9},{9,8},{10,11... | collective-permute-start | bytes 638984 | tf_op jit(solution)/shard_map/ppermute | solution.py:454
  26.2 13.0 %collective-permute-start.12 = (f32[104,512]{1,0:T(8,128)S(1)}, f32[104,512]{1,0:T(8,128)S(1)}, u32[]{:S(2)}, u32[]{:S(2)}) collective-permute-start(f32[104,512]{1,0:T(8,128)S(1)} %collective-permute-done.11.refs_10_), channel_id=1, source_target_pairs={{0,128},{128,0},{1,129},{129,1},{2,130},{130,2},{3,131},{131,3},{4... | collective-permute-start | bytes 638984 | tf_op jit(solution)/shard_map/ppermute | solution.py:454
  27.1 23.0 %copy-start.4 = (f32[104,512]{1,0:T(8,128)}, f32[104,512]{1,0:T(8,128)S(1)}, u32[]{:S(2)}) copy-start(f32[104,512]{1,0:T(8,128)S(1)} %collective-permute-done.7.refs_6_) | copy-start | bytes 638980
  27.1 16.6 %collective-permute-start.8 = (f32[104,512]{1,0:T(8,128)S(1)}, f32[104,512]{1,0:T(8,128)S(1)}, u32[]{:S(2)}, u32[]{:S(2)}) collective-permute-start(f32[104,512]{1,0:T(8,128)S(1)} %collective-permute-done.7.refs_6_), channel_id=1, source_target_pairs={{0,128},{128,0},{1,129},{129,1},{2,130},{130,2},{3,131},{131,3},{4... | collective-permute-start | bytes 638984 | tf_op jit(solution)/shard_map/ppermute | solution.py:454
  29.2 20.9 %copy-start.5 = (f32[104,512]{1,0:T(8,128)}, f32[104,512]{1,0:T(8,128)S(1)}, u32[]{:S(2)}) copy-start(f32[104,512]{1,0:T(8,128)S(1)} %collective-permute-done.3.refs_2_) | copy-start | bytes 638980
  29.2 17.5 %collective-permute-start.4 = (f32[104,512]{1,0:T(8,128)S(1)}, f32[104,512]{1,0:T(8,128)S(1)}, u32[]{:S(2)}, u32[]{:S(2)}) collective-permute-start(f32[104,512]{1,0:T(8,128)S(1)} %collective-permute-done.3.refs_2_), channel_id=1, source_target_pairs={{0,128},{128,0},{1,129},{129,1},{2,130},{130,2},{3,131},{131,3},{4... | collective-permute-start | bytes 638984 | tf_op jit(solution)/shard_map/ppermute | solution.py:454
  31.4 18.7 %copy-start.6 = (f32[104,512]{1,0:T(8,128)}, f32[104,512]{1,0:T(8,128)S(1)}, u32[]{:S(2)}) copy-start(f32[104,512]{1,0:T(8,128)S(1)} %collective-permute-done.2.refs_1_) | copy-start | bytes 638980
  31.4 18.4 %collective-permute-start.9 = (f32[104,512]{1,0:T(8,128)S(1)}, f32[104,512]{1,0:T(8,128)S(1)}, u32[]{:S(2)}, u32[]{:S(2)}) collective-permute-start(f32[104,512]{1,0:T(8,128)S(1)} %collective-permute-done.7.refs_6_), channel_id=1, source_target_pairs={{0,1},{1,0},{2,3},{3,2},{4,5},{5,4},{6,7},{7,6},{8,9},{9,8},{10,11... | collective-permute-start | bytes 638984 | tf_op jit(solution)/shard_map/ppermute | solution.py:454
  39.1 11.0 %copy-start.7 = (f32[104,512]{1,0:T(8,128)}, f32[104,512]{1,0:T(8,128)S(1)}, u32[]{:S(2)}) copy-start(f32[104,512]{1,0:T(8,128)S(1)} %collective-permute-done.13.refs_12_) | copy-start | bytes 638980
  39.1 10.7 %collective-permute-start.5 = (f32[104,512]{1,0:T(8,128)S(1)}, f32[104,512]{1,0:T(8,128)S(1)}, u32[]{:S(2)}, u32[]{:S(2)}) collective-permute-start(f32[104,512]{1,0:T(8,128)S(1)} %collective-permute-done.3.refs_2_), channel_id=1, source_target_pairs={{0,1},{1,0},{2,3},{3,2},{4,5},{5,4},{6,7},{7,6},{8,9},{9,8},{10,11... | collective-permute-start | bytes 638984 | tf_op jit(solution)/shard_map/ppermute | solution.py:454
  39.2 10.9 %copy-start.8 = (f32[104,512]{1,0:T(8,128)}, f32[104,512]{1,0:T(8,128)S(1)}, u32[]{:S(2)}) copy-start(f32[104,512]{1,0:T(8,128)S(1)} %collective-permute-done.12.refs_11_) | copy-start | bytes 638980
  39.2 10.6 %collective-permute-start.14 = (f32[104,512]{1,0:T(8,128)S(1)}, f32[104,512]{1,0:T(8,128)S(1)}, u32[]{:S(2)}, u32[]{:S(2)}) collective-permute-start(f32[104,512]{1,0:T(8,128)S(1)} %collective-permute-done.12.refs_11_), channel_id=1, source_target_pairs={{0,1},{1,0},{2,3},{3,2},{4,5},{5,4},{6,7},{7,6},{8,9},{9,8},{10,11... | collective-permute-start | bytes 638984 | tf_op jit(solution)/shard_map/ppermute | solution.py:454
  43.7 6.4 %copy-start.9 = (f32[104,512]{1,0:T(8,128)}, f32[104,512]{1,0:T(8,128)S(1)}, u32[]{:S(2)}) copy-start(f32[104,512]{1,0:T(8,128)S(1)} %collective-permute-done.8.refs_7_) | copy-start | bytes 638980
  43.7 6.2 %collective-permute-start.10 = (f32[104,512]{1,0:T(8,128)S(1)}, f32[104,512]{1,0:T(8,128)S(1)}, u32[]{:S(2)}, u32[]{:S(2)}) collective-permute-start(f32[104,512]{1,0:T(8,128)S(1)} %collective-permute-done.8.refs_7_), channel_id=1, source_target_pairs={{0,1},{1,0},{2,3},{3,2},{4,5},{5,4},{6,7},{7,6},{8,9},{9,8},{10,11... | collective-permute-start | bytes 638984 | tf_op jit(solution)/shard_map/ppermute | solution.py:454
  46.7 3.4 %copy-start.10 = (f32[104,512]{1,0:T(8,128)}, f32[104,512]{1,0:T(8,128)S(1)}, u32[]{:S(2)}) copy-start(f32[104,512]{1,0:T(8,128)S(1)} %collective-permute-done.4.refs_3_) | copy-start | bytes 638980
  46.7 3.4 %collective-permute-start.6 = (f32[104,512]{1,0:T(8,128)S(1)}, f32[104,512]{1,0:T(8,128)S(1)}, u32[]{:S(2)}, u32[]{:S(2)}) collective-permute-start(f32[104,512]{1,0:T(8,128)S(1)} %collective-permute-done.4.refs_3_), channel_id=1, source_target_pairs={{0,1},{1,0},{2,3},{3,2},{4,5},{5,4},{6,7},{7,6},{8,9},{9,8},{10,11... | collective-permute-start | bytes 638984 | tf_op jit(solution)/shard_map/ppermute | solution.py:454
  49.8 0.7 copy-start.11
  49.8 0.8 copy-start.12
  49.9 0.8 copy-start.13
  49.9 0.9 copy-start.14
  50.7 0.7 copy-start.15
where the time goes:
time: 143 us; the launch traced here: 142 us
  Pallas kernels  94 us (66%)
  starting transfers between devices  37.2 us (26%)
  local copies, waits for them, and re-layouts  5.03 us (4%)
  matrix products  3.73 us (3%)
    pallas_call x1, Pallas kernels, per_device(): pl.pallas_call(cycle_kernel, out_shape=jax.ShapeDtypeStruct(adjoint_load....  90.2 us
    ppermute x12, starting transfers between devices, swap(): return lax.ppermute(value, axis, [(0, 1), (1, 0)])  27.1 us
    ppermute x3, starting transfers between devices, sided(): return lax.ppermute(value, ('gy', 'gz'), pairs)  10 us
    pallas_call x1, Pallas kernels, per_device(): pl.pallas_call(pack_kernel, out_shape=jax.ShapeDtypeStruct((PACK, 512), F...  3.81 us
    dot_general x6, matrix products, exact_dot(): return jnp.dot(a, b, precision=EXACT, preferred_element_type=F32)  3.73 us
  transfers between devices with their start and end apart: 15, of which 2 were waited for; matrix products, arithmetic and copies ran while one was open for 5% of the time, Pallas kernels for 0%

commit v1 on v0

v1 whole, which is shorter than its diff:
```python
import jax
import jax.numpy as jnp
import numpy as np
from jax import lax
from jax.experimental import pallas as pl
from jax.experimental.pallas import tpu as pltpu
from jax.sharding import PartitionSpec as P

DEG = 4
DENSITY_LEVELS = 16
MID = 1.125
HALF = 0.875

F32 = jnp.float32
BF16 = jnp.bfloat16
EXACT = lax.Precision.HIGHEST

OWN = 4
SIDE = 4
FAR = 8
ROWS = OWN + 2 * SIDE
C_ROWS = OWN + 2 * FAR
LANES = 1024
WIDE = LANES + 128
AHEAD = 2
PACK = 104
NOTE = 24


def node_row(group, row):
    px, py = ((0, 0), (1, 0), (0, 1))[group]
    if row < 6:
        return row % 3, px, py, row // 3
    return group, 1, 1, row - 6


FINE_IN = [(g, sx, sy) for sx, sy, groups in ((0, 0, (0, 1, 2)), (1, 0, (0, 2)), (0, 1, (0, 1)), (1, 1, (0,))) for g in groups]
SHIFTS = [(0, 0), (1, 0), (0, 1), (1, 1)]


def fine_place(group, row, sx, sy, sz):
    p, px, py, pz = node_row(group, row)
    if (sx and px) or (sy and py) or (sz and pz):
        return None
    return 27 * p + 9 * (px + 2 * sx) + 3 * (py + 2 * sy) + pz + 2 * sz


def coarse_place(row, sx, sy, sz):
    return 8 * row + 4 * sx + 2 * sy + sz if row < 3 else None


def fine_selectors():
    out_rows = np.zeros((128, 81), np.float32)
    in_rows = np.zeros((256, 81), np.float32)
    at = 0
    for sz in (0, 1):
        for g, sx, sy in FINE_IN:
            for row in range(8):
                place = fine_place(g, row, sx, sy, sz)
                if place is not None:
                    out_rows[at + row, place] = 1.0
            at += 8
    at = 0
    for g, sx, sy in FINE_IN:
        for sz in (0, 1):
            for row in range(8):
                place = fine_place(g, row, sx, sy, sz)
                if place is not None:
                    in_rows[at + row, place] = 1.0
                    in_rows[at + 8 + row, place] = 1.0
            at += 16
    return out_rows, in_rows


def coarse_selectors():
    out_rows = np.zeros((64, 24), np.float32)
    in_rows = np.zeros((128, 24), np.float32)
    at = 0
    for sz in (0, 1):
        for sx, sy in SHIFTS:
            for row in range(3):
                out_rows[at + row, coarse_place(row, sx, sy, sz)] = 1.0
            at += 8
    at = 0
    for sx, sy in SHIFTS:
        for sz in (0, 1):
            for row in range(3):
                in_rows[at + row, coarse_place(row, sx, sy, sz)] = 1.0
                in_rows[at + 8 + row, coarse_place(row, sx, sy, sz)] = 1.0
            at += 16
    return out_rows, in_rows


def weight_along(parity, shift):
    if parity == 0:
        return 1.0 if shift == 0 else 0.0
    return 0.5


def prolong_weights():
    weights = np.zeros((24, 128), np.float32)
    at = 0
    for sx, sy in SHIFTS:
        for sz in (0, 1):
            for g in range(3):
                for row in range(8):
                    p, px, py, pz = node_row(g, row)
                    w = weight_along(px, sx) * weight_along(py, sy) * weight_along(pz, sz)
                    weights[8 * g + row, at + p] = w
                    weights[8 * g + row, at + 8 + p] = w
            at += 16
    return weights


def restrict_weights():
    weights = np.zeros((64, 48), np.float32)
    at = 0
    for sz in (0, 1):
        for sx, sy in SHIFTS:
            for g in range(3):
                for row in range(8):
                    p, px, py, pz = node_row(g, row)
                    w = weight_along(px, sx) * weight_along(py, sy) * weight_along(pz, sz)
                    weights[at + p, 16 * g + row] = w
                    weights[at + p, 16 * g + 8 + row] = w
            at += 8
    return weights


def row_shuffle():
    shuffle = np.zeros((96, 96), np.float32)
    for y in range(4):
        for g in range(3):
            for row in range(8):
                p, px, py, pz = node_row(g, row)
                shuffle[24 * y + 8 * g + row, pz * 48 + p * 16 + px * 8 + 2 * y + py] = 1.0
    return shuffle


def diag_selectors():
    fine = np.zeros((32, 16, 81), np.float32)
    coarse = np.zeros((32, 16, 24), np.float32)
    for at in range(8):
        sy, sx, sz = at // 4, at // 2 % 2, at % 2
        for half in (0, 8):
            for g in range(3):
                for row in range(8):
                    place = fine_place(g, row, sx, sy, sz)
                    if place is not None:
                        fine[8 * g + row, half + at, place] = 1.0
            for row in range(3):
                coarse[24 + row, half + at, coarse_place(row, sx, sy, sz)] = 1.0
    return fine.reshape(512, 81), coarse.reshape(512, 24)


def exact_dot(a, b):
    return jnp.dot(a, b, precision=EXACT, preferred_element_type=F32)


def pack_kernel(place_ref, load_ref, load_other_ref, levels_ref, levels_other_ref, shuffle_ref, out_ref):
    gz = place_ref[2]

    def spread(half):
        row = lax.broadcasted_iota(jnp.int32, (128, 256), 0)
        col = lax.broadcasted_iota(jnp.int32, (128, 256), 1)
        source = 2 * (col % 128) + col // 128
        return (source == row + 128 * half).astype(F32)

    def widen(half):
        row = lax.broadcasted_iota(jnp.int32, (64, 128), 0)
        col = lax.broadcasted_iota(jnp.int32, (64, 128), 1)
        return (col == row + 64 * half).astype(F32)

    own_spread, other_spread = spread(gz), spread(1 - gz)
    own_widen, other_widen = widen(gz), widen(1 - gz)
    for x in range(4):
        lanes = slice(128 * x, 128 * x + 128)
        own = load_ref[:, 2 * x : 2 * x + 2].reshape(48, 128)
        other = load_other_ref[:, 2 * x : 2 * x + 2].reshape(48, 128)
        parted = exact_dot(own, own_spread) + exact_dot(other, other_spread)
        stacked = jnp.concatenate([parted[:, :128], parted[:, 128:]], axis=0)
        out_ref[0:96, lanes] = exact_dot(shuffle_ref[...], stacked)
        level = exact_dot(levels_ref[x].astype(F32), own_widen) + exact_dot(
            levels_other_ref[x].astype(F32), other_widen
        )
        ratio = level / (DENSITY_LEVELS - 1)
        out_ref[96:100, lanes] = 0.05 + 0.95 * ratio * ratio * ratio
        out_ref[100:104, lanes] = jnp.zeros((4, 128), F32)


def split(values):
    high = values.astype(BF16).astype(F32)
    return jnp.concatenate([high, values - high], axis=0).astype(BF16)


def roll_tiles(values, step):
    tiles = []
    for t in range(values.shape[1] // 128):
        tile = values[:, 128 * t : 128 * t + 128]
        lane = lax.broadcasted_iota(jnp.int32, tile.shape, 1)
        if step == 1:
            tiles.append(jnp.where(lane < 127, pltpu.roll(tile, 127, 1), 0.0))
        else:
            tiles.append(jnp.where(lane > 0, pltpu.roll(tile, 1, 1), 0.0))
    return tiles[0] if len(tiles) == 1 else jnp.concatenate(tiles, axis=1)


def hi_lo_weights(weights):
    high = weights.astype(BF16).astype(F32)
    col = lax.broadcasted_iota(jnp.int32, weights.shape, 1)
    low = jnp.where(col % 16 < 8, weights - high, 0.0)
    return jnp.concatenate([high, low], axis=0).astype(BF16)


def scaled(values, moduli):
    rows, lanes = values.shape
    return (values.reshape(rows // 8, 8, lanes) * moduli[None]).reshape(rows, lanes)


def joined(sweeps):
    rows, factors = [], []
    for first, last, keep, gain, flag in sweeps:
        rows += list(range(first, last))
        factors += [(keep, gain, flag)] * (last - first)
    return rows, factors


def schedules():
    sigma = MID / HALF
    rhos = [1.0 / sigma]
    for _ in range(DEG - 1):
        rhos.append(1.0 / (2.0 * sigma - rhos[-1]))
    smooth = [(rhos[s + 1] * rhos[s], 2.0 * rhos[s + 1] / HALF) for s in range(DEG - 1)]
    o, c = SIDE, FAR
    runs = {
        "start": (joined([(0, ROWS, 0.0, 0.0, 0.0)]), 3),
        "before": (joined([(o - 3 + s, o + 7 - s, *smooth[s], 0.0) for s in range(DEG - 1)]), 6),
        "leave": (joined([(o, o + 4, 0.0, 0.0, 0.0)]), 4),
        "coarse_start": (joined([(c - 7, c + 11, 0.0, 0.0, 0.0)]), 3),
        "coarse": (joined([(c - 7 + s, c + 10 - s, *smooth[s], float(s == DEG - 2)) for s in range(DEG - 1)]), 9),
        "correct": (joined([(o - 4, o + 8, 0.0, 0.0, 0.0)]), 3),
        "after": (
            joined(
                [(o - 4, o + 7, 0.0, 1.0 / MID, 0.0)]
                + [(o - 3 + s, o + 6 - s + (s == DEG - 2), *smooth[s], 0.0) for s in range(DEG - 1)]
            ),
            3,
        ),
    }
    rows, factors, at = [], [], {}
    for name, ((run_rows, run_factors), together) in runs.items():
        assert len(run_rows) % together == 0
        assert together % (AHEAD + 1) == 0 or len(run_rows) == together
        at[name] = (len(rows), len(run_rows), together)
        rows += run_rows + [o] * AHEAD
        factors += run_factors + [(0.0, 0.0, 0.0)] * AHEAD
    return np.asarray(rows, np.int32), np.asarray(factors, np.float32).reshape(-1), at


CHUNKS = [(256 * n, slice(256 * n, 256 * n + 256)) for n in range(4)]


def pushed(before, values):
    return jnp.concatenate([before, values[:, :128]], axis=1)


def store_fine(fine_x, y, lanes, values):
    for g in range(3):
        part = values[8 * g : 8 * g + 8]
        fine_x[y, 32 * g : 32 * g + 16, lanes] = split(part)
        fine_x[y, 32 * g + 16 : 32 * g + 32, lanes] = split(roll_tiles(part, 1))


def store_coarse(coarse_x, y, lanes, values):
    coarse_x[y, 0:16, lanes] = split(values)
    coarse_x[y, 16:32, lanes] = split(roll_tiles(values, 1))


def pipeline(rows_ref, prods, name, issue, finish):
    first, count, together = schedules()[2][name]
    for u in range(AHEAD):
        issue(rows_ref[first + u], prods[u])

    def some(i, _):
        t = first + together * i
        for u in range(together):
            issue(rows_ref[t + u + AHEAD], prods[(u + AHEAD) % len(prods)])
            finish(t + u, rows_ref[t + u], prods[u % len(prods)])
        return 0

    lax.fori_loop(0, count // together, some, 0)


def fine_issue(fine_w, fine_x):
    def issue(y, prod):
        for low, lanes in CHUNKS:
            there = slice(low + 128, low + 384)
            operand = jnp.concatenate(
                [
                    fine_x[y, :, lanes],
                    fine_x[y, 0:32, there],
                    fine_x[y, 64:96, there],
                    fine_x[y + 1, 0:64, lanes],
                    fine_x[y + 1, 0:32, there],
                ],
                axis=0,
            )
            products = jnp.dot(fine_w[...], operand, preferred_element_type=F32)
            prod[:, lanes] = products[:128] + products[128:]

    return issue


def fine_finish(moduli, offset, carry, use):
    def finish(t, y, prod):
        before = [(jnp.zeros((16, 128), F32), jnp.zeros((8, 128), F32))] * 2
        for low, lanes in CHUNKS:
            m = moduli[y + offset, :, lanes]
            sums = []
            for z in range(2):
                v = scaled(prod[64 * z : 64 * z + 64, lanes], m)
                old = carry[16 * z : 16 * z + 16, lanes]
                along_x = pushed(before[z][0], v[24:40])
                along_xy = pushed(before[z][1], v[56:64])
                before[z] = (v[24:40, 128:], v[56:64, 128:])
                sums.append(
                    jnp.concatenate(
                        [v[0:8] + along_x[0:8] + old[0:8], v[8:16] + old[8:16], v[16:24] + along_x[8:16]], axis=0
                    )
                )
                carry[16 * z : 16 * z + 16, lanes] = jnp.concatenate([v[40:48] + along_xy, v[48:56]], axis=0)
            use(t, y, lanes, sums[0] + roll_tiles(sums[1], -1))

    return finish


def coarse_finish(moduli, carry, use):
    def finish(t, y, prod):
        before = [(jnp.zeros((8, 128), F32), jnp.zeros((8, 128), F32))] * 2
        for low, lanes in CHUNKS:
            sums = []
            for z in range(2):
                v = prod[32 * z : 32 * z + 32, lanes]
                if moduli is not None:
                    v = scaled(v, moduli[y, :, lanes])
                old = carry[8 * z : 8 * z + 8, lanes]
                sums.append(v[0:8] + pushed(before[z][0], v[8:16]) + old)
                carry[8 * z : 8 * z + 8, lanes] = v[16:24] + pushed(before[z][1], v[24:32])
                before[z] = (v[8:16, 128:], v[24:32, 128:])
            use(t, y, lanes, sums[0] + roll_tiles(sums[1], -1))

    return finish


def smooth_fine(factors_ref, inverse, res, step, total, fine_x):
    def use(t, y, lanes, sums):
        keep, gain = factors_ref[3 * t], factors_ref[3 * t + 1]
        r = res[y, :, lanes] - sums
        d = keep * step[y, :, lanes] + gain * (inverse[y, :, lanes] * r)
        res[y, :, lanes] = r
        step[y, :, lanes] = d
        total[y, :, lanes] = total[y, :, lanes] + d
        store_fine(fine_x, y, lanes, d)

    return use


def diag_issue(diag_w, moduli, count):
    def issue(y, prod):
        spot = lax.broadcasted_iota(jnp.int32, (8, 256), 0)
        before = jnp.zeros((8, 128), F32)
        for low, lanes in CHUNKS:
            near = jnp.where(spot < 4, moduli[y, :, lanes], moduli[jnp.maximum(y - 1, 0), :, lanes])
            moved = pushed(before, near)
            before = near[:, 128:]
            around = jnp.where(spot % 4 < 2, near, moved)
            around = jnp.where(spot % 2 < 1, around, roll_tiles(around, -1))
            products = jnp.dot(diag_w[...], split(around), preferred_element_type=F32)
            prod[0:count, lanes] = products[:count] + products[count:]

    return issue


def clear_tail(ref, rows):
    def clear(y, _):
        ref[y, :, LANES:] = jnp.zeros((ref.shape[1], 128), BF16)
        return 0

    lax.fori_loop(0, rows, clear, 0)


def validity(place_ref, ahead):
    first, count = place_ref[1] * OWN - ahead, place_ref[3] * OWN

    def valid(y):
        return jnp.where((first + y >= 0) & (first + y < count), 1.0, 0.0).astype(F32)

    return valid


def before_kernel(place_ref, rows_ref, factors_ref, *refs):
    blocks = refs[:6]
    fine_ref, diag_ref, restrict_ref = refs[6:9]
    load, moduli, inverse, smoothed, note = refs[9:14]
    res, step, total, fine_x, carry, fine_w, diag_w, c_carry, *prods = refs[14:]
    gx, gz = place_ref[0], place_ref[2]
    valid = validity(place_ref, SIDE)
    o = SIDE

    own, own_x, a, ax, za, zax = blocks
    side = 1 - 2 * gz
    for ref, offset, half in [
        (own, 0, gx), (own_x, 0, 1 - gx), (a, -side, gx), (ax, -side, 1 - gx), (za, side, gx), (zax, side, 1 - gx)
    ]:
        first = o + OWN * offset
        lanes = pl.ds(pl.multiple_of(half * 512, 512), 512)
        for y in range(OWN):
            load[first + y, :, lanes] = ref[24 * y : 24 * y + 24, :]
            moduli[first + y, :, lanes] = jnp.broadcast_to(ref[96 + y : 97 + y, :], (8, 512))

    fine_w[...] = hi_lo_weights(fine_ref[...])
    diag_w[...] = hi_lo_weights(diag_ref[0:24, :])
    clear_tail(fine_x, ROWS)
    carry[...] = jnp.zeros_like(carry)

    def start(t, y, prod):
        ok = valid(y)
        for low, lanes in CHUNKS:
            inv = ok / (prod[0:24, lanes] + (1.0 - ok))
            r = load[y, :, lanes]
            d = inv * r * (1.0 / MID)
            inverse[y, :, lanes] = inv
            res[y, :, lanes] = r
            step[y, :, lanes] = d
            total[y, :, lanes] = d
            store_fine(fine_x, y, lanes, d)

    pipeline(rows_ref, prods, "start", diag_issue(diag_w, moduli, 24), start)
    issue = fine_issue(fine_w, fine_x)
    use = smooth_fine(factors_ref, inverse, res, step, total, fine_x)
    pipeline(rows_ref, prods, "before", issue, fine_finish(moduli, 0, carry, use))
    for y in range(OWN):
        smoothed[24 * y : 24 * y + 24, :] = total[o + y]

    carry[...] = jnp.zeros_like(carry)

    def store_left(y, lanes, left):
        for g in range(3):
            fine_x[y, 16 * g : 16 * g + 16, lanes] = split(left[8 * g : 8 * g + 8])

    def leave(t, y, lanes, sums):
        store_left(y, lanes, res[y, :, lanes] - sums)

    pipeline(rows_ref, prods, "leave", issue, fine_finish(moduli, 0, carry, leave))
    for low, lanes in CHUNKS:
        last = carry[0:16, lanes] + roll_tiles(carry[16:32, lanes], -1)
        last = jnp.concatenate([last, jnp.zeros((8, 256), F32)], axis=0)
        store_left(o + OWN, lanes, -last * valid(o + OWN))

    c_carry[...] = jnp.zeros_like(c_carry)
    for j in range(OWN + 1):
        prod = prods[j % len(prods)]
        for low, lanes in CHUNKS:
            prod[0:64, lanes] = jnp.dot(
                restrict_ref[...], fine_x[o + j, 0:48, lanes], preferred_element_type=F32
            )

        def keep(t, y, lanes, sums, j=j):
            note[3 * j : 3 * j + 3, lanes] = sums[0:3]

        coarse_finish(None, c_carry, keep)(0, o + j, prod)
    for y in range(OWN):
        note[16 + y : 17 + y, :] = moduli[o + y, 0:1, :]


def after_kernel(place_ref, rows_ref, factors_ref, *refs):
    note, m1, zm1, m2, zm2, s0, s1, zs1, load, near_moduli, inverse = refs[:11]
    fine_ref, coarse_ref, diag_ref, prolong_ref, shuffle_ref = refs[11:16]
    out_ref = refs[16]
    (res, step, total, fine_x, carry, fine_w, moduli, coarse_w, diag_w,
     c_inverse, c_res, c_step, c_total, coarse_x, c_carry, *prods) = refs[17:]
    gx, gz = place_ref[0], place_ref[2]
    o, c = SIDE, FAR
    valid = validity(place_ref, FAR)
    side = 1 - 2 * gz

    for y in range(ROWS):
        moduli[c - o + y] = near_moduli[y]
    c_res[...] = jnp.zeros_like(c_res)
    for ref, offset in [(m2, -2 * side), (zm2, 2 * side)]:
        first = c + OWN * offset
        for y in range(OWN):
            moduli[first + y] = jnp.broadcast_to(ref[16 + y : 17 + y, :], (8, LANES))
    for ref, offset in [(note, 0), (m1, -side), (zm1, side), (m2, -2 * side), (zm2, 2 * side)]:
        first = c + OWN * offset
        for y in range(OWN + 1):
            at = jnp.minimum(first + y, C_ROWS)
            c_res[at, 0:3, :] = c_res[at, 0:3, :] + ref[3 * y : 3 * y + 3, :]
    for ref, offset in [(s0, 0), (s1, -side), (zs1, side)]:
        for y in range(OWN):
            total[o + OWN * offset + y] = ref[24 * y : 24 * y + 24, :]

    fine_w[...] = hi_lo_weights(fine_ref[...])
    coarse_w[...] = hi_lo_weights(coarse_ref[...])
    diag_w[...] = hi_lo_weights(diag_ref[24:32, :])
    clear_tail(fine_x, ROWS)
    clear_tail(coarse_x, C_ROWS)
    carry[...] = jnp.zeros_like(carry)
    c_carry[...] = jnp.zeros_like(c_carry)

    def start(t, y, prod):
        ok = valid(y)
        for low, lanes in CHUNKS:
            used = lax.broadcasted_iota(jnp.int32, (8, 256), 0) < 3
            inv = jnp.where(used, ok / (prod[0:8, lanes] + (1.0 - ok)), 0.0)
            d = inv * c_res[y, :, lanes] * (1.0 / MID)
            c_inverse[y, :, lanes] = inv
            c_step[y, :, lanes] = d
            c_total[y, :, lanes] = d
            store_coarse(coarse_x, y, lanes, d)

    pipeline(rows_ref, prods, "coarse_start", diag_issue(diag_w, moduli, 8), start)

    def coarse_operand(y, low, lanes):
        there = slice(low + 128, low + 384)
        return jnp.concatenate(
            [coarse_x[y, :, lanes], coarse_x[y, :, there], coarse_x[y + 1, :, lanes], coarse_x[y + 1, :, there]],
            axis=0,
        )

    def coarse_issue(y, prod):
        for low, lanes in CHUNKS:
            products = jnp.dot(coarse_w[...], coarse_operand(y, low, lanes), preferred_element_type=F32)
            prod[0:64, lanes] = products[:64] + products[64:]

    def smooth_coarse(t, y, lanes, sums):
        keep, gain, last = factors_ref[3 * t], factors_ref[3 * t + 1], factors_ref[3 * t + 2]
        r = c_res[y, :, lanes] - sums
        d = keep * c_step[y, :, lanes] + gain * (c_inverse[y, :, lanes] * r)
        so_far = c_total[y, :, lanes]
        c_res[y, :, lanes] = r
        c_step[y, :, lanes] = d
        c_total[y, :, lanes] = so_far + d
        store_coarse(coarse_x, y, lanes, d + last * so_far)

    pipeline(rows_ref, prods, "coarse", coarse_issue, coarse_finish(moduli, c_carry, smooth_coarse))

    def correct_issue(y, prod):
        for low, lanes in CHUNKS:
            prod[0:24, lanes] = jnp.dot(
                prolong_ref[...], coarse_operand(y + (c - o), low, lanes), preferred_element_type=F32
            )

    def correct(t, y, prod):
        for low, lanes in CHUNKS:
            corrected = total[y, :, lanes] + prod[0:24, lanes]
            total[y, :, lanes] = corrected
            res[y, :, lanes] = load[y, :, lanes]
            step[y, :, lanes] = jnp.zeros((24, 256), F32)
            store_fine(fine_x, y, lanes, corrected)

    pipeline(rows_ref, prods, "correct", correct_issue, correct)
    use = smooth_fine(factors_ref, inverse, res, step, total, fine_x)
    pipeline(rows_ref, prods, "after", fine_issue(fine_w, fine_x), fine_finish(moduli, c - o, carry, use))

    row = lax.broadcasted_iota(jnp.int32, (128, 128), 0)
    col = lax.broadcasted_iota(jnp.int32, (128, 128), 1)
    mine = row == 64 * gz + col // 2
    weave = [(mine & (col % 2 == pz)).astype(F32) for pz in (0, 1)]
    for x in range(4):
        lanes = pl.ds(pl.multiple_of(gx * 512 + 128 * x, 128), 128)
        rows = total[o : o + OWN, :, lanes].reshape(96, 128)
        back = lax.dot_general(
            shuffle_ref[...], rows, (((0,), (0,)), ((), ())), precision=EXACT, preferred_element_type=F32
        )
        woven = exact_dot(back[0:48], weave[0]) + exact_dot(back[48:96], weave[1])
        out_ref[:, 2 * x : 2 * x + 2] = woven.reshape(3, 2, 8, 128)


def per_device(adjoint_load, levels, fine_stiffness, coarse_stiffness):
    count = lax.axis_size("gy")
    place = jnp.stack(
        [lax.axis_index("gx"), lax.axis_index("gy"), lax.axis_index("gz"), jnp.int32(count)]
    ).astype(jnp.int32)

    def swap(value, axis):
        return lax.ppermute(value, axis, [(0, 1), (1, 0)])

    def sided(value, steps):
        pairs = [(2 * i, 2 * (i + steps)) for i in range(count - steps)]
        pairs += [(2 * (i + steps) + 1, 2 * i + 1) for i in range(count - steps)]
        return lax.ppermute(value, ("gy", "gz"), pairs)

    whole = pl.BlockSpec(memory_space=pltpu.VMEM)
    scalars = pl.BlockSpec(memory_space=pltpu.SMEM)
    shuffle = jnp.asarray(row_shuffle())
    own = pl.pallas_call(
        pack_kernel,
        out_shape=jax.ShapeDtypeStruct((PACK, 512), F32),
        in_specs=[scalars] + [whole] * 5,
        out_specs=whole,
        name="pack",
    )(place, adjoint_load, swap(adjoint_load, "gz"), levels, swap(levels, "gz"), shuffle)

    a = sided(own, 1)
    own_x = swap(own, "gx")
    ax = swap(a, "gx")
    blocks = [own, own_x, a, ax, swap(a, "gz"), swap(ax, "gz")]

    fine_out, fine_in = fine_selectors()
    coarse_out, coarse_in = coarse_selectors()
    fine = exact_dot(exact_dot(jnp.asarray(fine_out), fine_stiffness), jnp.asarray(fine_in.T))
    coarse = exact_dot(exact_dot(jnp.asarray(coarse_out), coarse_stiffness), jnp.asarray(coarse_in.T))
    fine_at, coarse_at = diag_selectors()
    diag = jnp.sum(jnp.asarray(fine_at) * jnp.diagonal(fine_stiffness), axis=1)
    diag = diag + jnp.sum(jnp.asarray(coarse_at) * jnp.diagonal(coarse_stiffness), axis=1)
    rows, factors, _ = schedules()

    rows, factors = jnp.asarray(rows), jnp.asarray(factors)
    diag = diag.reshape(32, 16)

    def held(count, height=24):
        return pltpu.VMEM((count, height, LANES), F32)

    fine_scratch = [
        held(ROWS),
        held(ROWS),
        held(ROWS),
        pltpu.VMEM((ROWS + 1, 96, WIDE), BF16),
        pltpu.VMEM((32, LANES), F32),
        pltpu.VMEM((256, 256), BF16),
    ]
    prods = [pltpu.VMEM((128, LANES), F32)] * (AHEAD + 1)
    limit = pltpu.CompilerParams(vmem_limit_bytes=56 * 1024 * 1024)
    load, moduli, inverse, smoothed, note = pl.pallas_call(
        before_kernel,
        out_shape=[
            jax.ShapeDtypeStruct(shape, F32)
            for shape in [(ROWS, 24, LANES), (ROWS, 8, LANES), (ROWS, 24, LANES), (24 * OWN, LANES), (NOTE, LANES)]
        ],
        in_specs=[scalars] * 3 + [whole] * 9,
        out_specs=[whole] * 5,
        scratch_shapes=fine_scratch
        + [
            pltpu.VMEM((48, 16), BF16),
            pltpu.VMEM((16, LANES), F32),
            *prods,
        ],
        compiler_params=limit,
        name="before",
    )(place, rows, factors, *blocks, fine, diag, jnp.asarray(restrict_weights(), dtype=BF16))

    m1, m2 = sided(note, 1), sided(note, 2)
    s1 = sided(smoothed, 1)
    notes = [note, m1, swap(m1, "gz"), m2, swap(m2, "gz")]
    return pl.pallas_call(
        after_kernel,
        out_shape=jax.ShapeDtypeStruct(adjoint_load.shape, F32),
        in_specs=[scalars] * 3 + [whole] * 16,
        out_specs=whole,
        scratch_shapes=fine_scratch
        + [
            held(C_ROWS, 8),
            pltpu.VMEM((128, 128), BF16),
            pltpu.VMEM((16, 16), BF16),
            held(C_ROWS, 8),
            held(C_ROWS + 1, 8),
            held(C_ROWS, 8),
            held(C_ROWS, 8),
            pltpu.VMEM((C_ROWS + 1, 32, WIDE), BF16),
            pltpu.VMEM((16, LANES), F32),
            *prods,
        ],
        compiler_params=limit,
        name="after",
    )(
        place,
        rows,
        factors,
        *notes,
        smoothed,
        s1,
        swap(s1, "gz"),
        load,
        moduli,
        inverse,
        fine,
        coarse,
        diag,
        jnp.asarray(prolong_weights(), dtype=BF16),
        shuffle,
    )


def solution(mesh):
    return jax.shard_map(
        per_device,
        mesh=mesh,
        in_specs=(P(None, "gx", "gy", "gz"), P("gx", "gy", "gz"), P(), P()),
        out_specs=P(None, "gx", "gy", "gz"),
        check_vma=False,
    )
```

time: 143 us -> 90 us (0.63)
  Pallas kernels: 94 us -> 39.7 us
  waiting for transfers between devices: 0.79 us -> 3.62 us
  local copies, waits for them, and re-layouts: 5.03 us -> 7.24 us
  starting transfers between devices: 37.2 us -> 35.7 us
    pallas_call x1 -> x2, Pallas kernels: 90.2 us -> 35.9 us  [the longest x1 23.6 us: per_device(): pl.pallas_call(after_kernel, out_shape=jax.ShapeDtypeStruct(adjoint_load....]
    ppermute x12 -> x9, starting transfers between devices: 27.1 us -> 19.5 us  [swap(): return lax.ppermute(value, axis, [(0, 1), (1, 0)])]
    ppermute x3 -> x4, starting transfers between devices: 10 us -> 16.2 us  [sided(): return lax.ppermute(value, ('gy', 'gz'), pairs)]
    ppermute x3 -> x4, waiting for transfers between devices: 0.01 us -> 3.4 us  [sided(): return lax.ppermute(value, ('gy', 'gz'), pairs)]
    dot_general x6 -> x4, matrix products: 3.73 us -> 2.31 us  [exact_dot(): return jnp.dot(a, b, precision=EXACT, preferred_element_type=F32)]
  transfers between devices with their start and end apart: 15 -> 13, of which waited for: 2 -> 4; matrix products, arithmetic and copies ran while one was open for 5% -> 8% of each run, Pallas kernels for 0% -> 0%
where the time goes in v1:
time: 90 us; the launch traced here: 89.6 us
  Pallas kernels  39.7 us (44%)
  starting transfers between devices  35.7 us (40%)
  local copies, waits for them, and re-layouts  7.24 us (8%)
  waiting for transfers between devices  3.62 us (4%)
  matrix products  2.31 us (3%)
    pallas_call x1, Pallas kernels, per_device(): pl.pallas_call(after_kernel, out_shape=jax.ShapeDtypeStruct(adjoint_load....  23.6 us
    ppermute x9, starting transfers between devices, swap(): return lax.ppermute(value, axis, [(0, 1), (1, 0)])  19.5 us
    ppermute x4, starting transfers between devices, sided(): return lax.ppermute(value, ('gy', 'gz'), pairs)  16.2 us
    pallas_call x1, Pallas kernels, per_device(): pl.pallas_call(before_kernel, out_shape=[jax.ShapeDtypeStruct(shape, F32)...  12.3 us
    pallas_call x1, Pallas kernels, per_device(): pl.pallas_call(pack_kernel, out_shape=jax.ShapeDtypeStruct((PACK, 512), F...  3.82 us
    ppermute x4, waiting for transfers between devices, sided(): return lax.ppermute(value, ('gy', 'gz'), pairs)  3.4 us
    unnamed x42, local copies, waits for them, and re-layouts  3.35 us
    dot_general x4, matrix products, exact_dot(): return jnp.dot(a, b, precision=EXACT, preferred_element_type=F32)  2.31 us
  transfers between devices with their start and end apart: 13, of which 4 were waited for; matrix products, arithmetic and copies ran while one was open for 8% of the time, Pallas kernels for 0%

profile of v1, /device:TPU:129, one launch (start us, length us, event | category | flops | bytes accessed | tf_op | source)
XLA Modules:
  0.0 89.6 jit_solution(7971293974318103563)
XLA Ops:
  0.0 0.0 copy-start
  0.0 0.0 copy-start.16
  0.0 0.0 copy-start.15
  0.0 0.8 collective-permute-start
  0.8 0.1 collective-permute-start.1
  0.9 0.6 pad_add_fusion.place_ref
  1.5 0.0 copy-done
  1.5 1.7 %gather_fusion = f32[81]{0:T(128)S(1)} fusion(f32[81,81]{1,0:T(8,128)S(1)} %copy-done, s32[81]{0:T(128)S(1)} %or_bitcast_fusion.1), kind=kCustom, calls=%fused_computation | custom fusion | bytes 1296 | tf_op jit(solution)/shard_map/jit(diagonal)/cond/branch_0_fun/gather | solution.py:615
  3.2 1.5 %gather_fusion.1 = f32[24]{0:T(128)S(1)} fusion(f32[24,24]{1,0:T(8,128)} %param.18, s32[24]{0:T(128)S(1)} %or_bitcast_fusion), kind=kCustom, calls=%fused_computation.1 | custom fusion | bytes 384 | tf_op jit(solution)/shard_map/jit(diagonal)/cond/branch_0_fun/gather | solution.py:616
  4.8 0.0 collective-permute-done.1.levels_other_ref
  4.8 0.0 collective-permute-done.load_other_ref
  4.8 0.6 copy-done.20
  5.4 0.6 copy-done.10
  6.0 3.8 %pack.1.refs_0_ = f32[104,512]{1,0:T(8,128)} custom-call(s32[4]{0:T(128)} %pad_add_fusion.place_ref, f32[3,8,8,128]{3,2,1,0:T(8,128)} %load_ref.1, f32[3,8,8,128]{3,2,1,0:T(8,128)} %copy-done.10, s32[4,4,64]{2,1,0:T(4,128)} %levels_ref.1, s32[4,4,64]{2,1,0:T(4,128)} %copy-done.20, f32[96,96]{1,0:T(8,128)} %constant.48.clone.shuffle_ref.refs_15_), custom_call_target="tpu_custom_call" | custom-call | tf_op jit(solution)/shard_map/pack/pallas_call | solution.py:597
  9.8 5.2 %collective-permute-start.3 = (f32[104,512]{1,0:T(8,128)}, f32[104,512]{1,0:T(8,128)S(1)}, u32[]{:S(2)}, u32[]{:S(2)}) collective-permute-start(f32[104,512]{1,0:T(8,128)} %pack.1.refs_0_), channel_id=1, source_target_pairs={{0,2},{2,4},{4,6},{6,8},{8,10},{10,12},{12,14},{14,16},{16,18},{18... | collective-permute-start | bytes 638984 | tf_op jit(solution)/shard_map/ppermute | solution.py:592
  15.1 0.0 copy-done.17
  15.1 0.1 multiply_reduce_fusion.1
  15.2 0.0 copy-done.9
  15.2 0.1 multiply_reduce_fusion
  15.3 0.7 add.16.refs_7_.refs_13_
  16.0 2.2 %collective-permute-done.3.refs_2_ = f32[104,512]{1,0:T(8,128)S(1)} collective-permute-done((f32[104,512]{1,0:T(8,128)}, f32[104,512]{1,0:T(8,128)S(1)}, u32[]{:S(2)}, u32[]{:S(2)}) %collective-permute-start.3) | collective-permute-done | bytes 213024 | tf_op jit(solution)/shard_map/ppermute | solution.py:592
  18.2 2.5 %collective-permute-start.4 = (f32[104,512]{1,0:T(8,128)S(1)}, f32[104,512]{1,0:T(8,128)S(1)}, u32[]{:S(2)}, u32[]{:S(2)}) collective-permute-start(f32[104,512]{1,0:T(8,128)S(1)} %collective-permute-done.3.refs_2_), channel_id=1, source_target_pairs={{0,128},{128,0},{1,129},{129,1},{2,130},{130,2},{3,131},{131,3},{4... | collective-permute-start | bytes 638984 | tf_op jit(solution)/shard_map/ppermute | solution.py:587
  20.6 0.0 copy-done.16
  20.6 0.3 fusion
  20.9 0.6 collective-permute-start.2
  21.5 4.9 %collective-permute-start.5 = (f32[104,512]{1,0:T(8,128)S(1)}, f32[104,512]{1,0:T(8,128)S(1)}, u32[]{:S(2)}, u32[]{:S(2)}) collective-permute-start(f32[104,512]{1,0:T(8,128)S(1)} %collective-permute-done.3.refs_2_), channel_id=1, source_target_pairs={{0,1},{1,0},{2,3},{3,2},{4,5},{5,4},{6,7},{7,6},{8,9},{9,8},{10,11... | collective-permute-start | bytes 638984 | tf_op jit(solution)/shard_map/ppermute | solution.py:587
  26.5 0.0 collective-permute-done.4.refs_3_
  26.5 3.9 %collective-permute-start.6 = (f32[104,512]{1,0:T(8,128)S(1)}, f32[104,512]{1,0:T(8,128)S(1)}, u32[]{:S(2)}, u32[]{:S(2)}) collective-permute-start(f32[104,512]{1,0:T(8,128)S(1)} %collective-permute-done.4.refs_3_), channel_id=1, source_target_pairs={{0,1},{1,0},{2,3},{3,2},{4,5},{5,4},{6,7},{7,6},{8,9},{9,8},{10,11... | collective-permute-start | bytes 638984 | tf_op jit(solution)/shard_map/ppermute | solution.py:587
  30.4 0.0 copy-done.15
  30.4 1.0 %fusion.1.refs_6_.refs_11_ = f32[128,256]{1,0:T(8,128)} fusion(f32[128,81]{0,1:T(8,128)S(1)} %fusion, f32[81,256]{1,0:T(8,128)S(1)} %copy-done.15), kind=kOutput, calls=%fused_computation.8 | convolution fusion | flops 31850496 | bytes 255488 | tf_op jit(solution)/shard_map/dot_general | solution.py:157
  31.4 0.0 collective-permute-done.2.refs_1_
  31.4 0.0 collective-permute-done.5.refs_4_
  31.4 0.0 copy-start.7
  31.4 0.1 collective-permute-done.6.refs_5_
  31.5 0.0 copy-done.4
  31.5 0.0 copy-done.5
  31.5 0.6 copy-done.6
  32.0 0.1 copy-done.7
  32.1 0.7 copy-done.8
  32.8 12.3 %before.1 = (f32[12,24,1024]{2,1,0:T(8,128)}, f32[12,8,1024]{2,1,0:T(8,128)}, f32[12,24,1024]{2,1,0:T(8,128)}, f32[96,1024]{1,0:T(8,128)}, f32[24,1024]{1,0:T(8,128)}) custom-call(s32[4]{0:T(128)} %pad_add_fusion.place_ref, s32[162]{0:T(256)} %constant.55.clone.rows_ref, f32[486]{0:T(512)} %constant.56.clone.factors_ref, f32[104,512]{1,0:T(8,128)} %pack.1.refs_0_, ...), custom_call_target="tpu_custom_call" | custom-call | tf_op jit(solution)/shard_map/before/pallas_call | solution.py:635
  45.1 7.2 %collective-permute-start.11 = (f32[96,1024]{1,0:T(8,128)}, f32[96,1024]{1,0:T(8,128)S(1)}, u32[]{:S(2)}, u32[]{:S(2)}) collective-permute-start(f32[96,1024]{1,0:T(8,128)} %get-tuple-element.11.refs_5_), channel_id=1, source_target_pairs={{0,2},{2,4},{4,6},{6,8},{8,10},{10,12},{12,14},{14,16},{16,18},{18... | collective-permute-start | bytes 1179656 | tf_op jit(solution)/shard_map/ppermute | solution.py:592
  52.2 1.9 %collective-permute-start.9 = (f32[24,1024]{1,0:T(8,128)}, f32[24,1024]{1,0:T(8,128)S(1)}, u32[]{:S(2)}, u32[]{:S(2)}) collective-permute-start(f32[24,1024]{1,0:T(8,128)} %get-tuple-element.10.refs_0_), channel_id=1, source_target_pairs={{0,4},{2,6},{4,8},{6,10},{8,12},{10,14},{12,16},{14,18},{16,20},{1... | collective-permute-start | bytes 294920 | tf_op jit(solution)/shard_map/ppermute | solution.py:592
  54.2 1.9 %collective-permute-start.7 = (f32[24,1024]{1,0:T(8,128)}, f32[24,1024]{1,0:T(8,128)S(1)}, u32[]{:S(2)}, u32[]{:S(2)}) collective-permute-start(f32[24,1024]{1,0:T(8,128)} %get-tuple-element.10.refs_0_), channel_id=1, source_target_pairs={{0,2},{2,4},{4,6},{6,8},{8,10},{10,12},{12,14},{14,16},{16,18},{18... | collective-permute-start | bytes 294920 | tf_op jit(solution)/shard_map/ppermute | solution.py:592
  56.1 1.2 %collective-permute-done.11.refs_6_ = f32[96,1024]{1,0:T(8,128)S(1)} collective-permute-done((f32[96,1024]{1,0:T(8,128)}, f32[96,1024]{1,0:T(8,128)S(1)}, u32[]{:S(2)}, u32[]{:S(2)}) %collective-permute-start.11) | collective-permute-done | bytes 393248 | tf_op jit(solution)/shard_map/ppermute | solution.py:592
  57.3 5.2 %collective-permute-start.12 = (f32[96,1024]{1,0:T(8,128)S(1)}, f32[96,1024]{1,0:T(8,128)S(1)}, u32[]{:S(2)}, u32[]{:S(2)}) collective-permute-start(f32[96,1024]{1,0:T(8,128)S(1)} %collective-permute-done.11.refs_6_), channel_id=1, source_target_pairs={{0,1},{1,0},{2,3},{3,2},{4,5},{5,4},{6,7},{7,6},{8,9},{9,8},{10,11... | collective-permute-start | bytes 1179656 | tf_op jit(solution)/shard_map/ppermute | solution.py:587
  62.5 0.0 copy-done.1
  62.5 0.0 copy-done.18
  62.5 0.2 fusion.2
  62.7 0.0 collective-permute-done.9.refs_3_
  62.7 0.0 copy-start.11
  62.7 0.1 collective-permute-start.10
  62.8 0.0 collective-permute-done.7.refs_1_
  62.8 0.0 copy-start.12
  62.9 1.4 %collective-permute-start.8 = (f32[24,1024]{1,0:T(8,128)S(1)}, f32[24,1024]{1,0:T(8,128)S(1)}, u32[]{:S(2)}, u32[]{:S(2)}) collective-permute-start(f32[24,1024]{1,0:T(8,128)S(1)} %collective-permute-done.7.refs_1_), channel_id=1, source_target_pairs={{0,1},{1,0},{2,3},{3,2},{4,5},{5,4},{6,7},{7,6},{8,9},{9,8},{10,11... | collective-permute-start | bytes 294920 | tf_op jit(solution)/shard_map/ppermute | solution.py:587
  64.3 0.0 copy-done.19
  64.3 0.8 fusion.3.refs_12_
  65.1 0.0 collective-permute-done.10.refs_4_
  65.1 0.1 collective-permute-done.8.refs_2_
  65.2 0.0 collective-permute-done.12.refs_7_
  65.2 0.0 copy-done.2
  65.2 0.5 copy-done.13
  65.7 0.1 copy-done.14
  65.8 0.1 copy-done.3
  66.0 23.6 %after.1 = f32[3,8,8,128]{3,2,1,0:T(8,128)} custom-call(s32[4]{0:T(128)} %pad_add_fusion.place_ref, s32[162]{0:T(256)} %constant.55.clone.rows_ref, f32[486]{0:T(512)} %constant.56.clone.factors_ref, f32[24,1024]{1,0:T(8,128)} %get-tuple-element.10.refs_0_, f32[24,1024]{1,0:T(8,128)} %copy-done.12, f32[24,1024]{1,0:T(8,128)} %copy-done.14, ...), custom_call_target="tpu_custom_call" | custom-call | tf_op jit(solution)/shard_map/after/pallas_call | solution.py:656
  (20 shorter events, 0.0 us)
Async XLA Ops:
  0.0 1.5 %copy-start = (f32[81,81]{1,0:T(8,128)S(1)}, f32[81,81]{1,0:T(8,128)}, u32[]{:S(2)}) copy-start(f32[81,81]{1,0:T(8,128)} %param.17) | copy-start | bytes 78736
  0.0 15.1 %copy-start.17 = (f32[512,24]{0,1:T(8,128)S(1)}, f32[512,24]{0,1:T(8,128)}, u32[]{:S(2)}) copy-start(f32[512,24]{0,1:T(8,128)} %constant.54.clone) | copy-start | bytes 147460
  0.0 15.2 %copy-start.9 = (f32[512,81]{0,1:T(8,128)S(1)}, f32[512,81]{0,1:T(8,128)}, u32[]{:S(2)}) copy-start(f32[512,81]{0,1:T(8,128)} %constant.53.clone) | copy-start | bytes 497668
  0.0 20.6 %copy-start.16 = (f32[128,81]{1,0:T(8,128)S(1)}, f32[128,81]{1,0:T(8,128)}, u32[]{:S(2)}) copy-start(f32[128,81]{1,0:T(8,128)} %constant.49.clone) | copy-start | bytes 124420
  0.0 30.4 %copy-start.15 = (f32[81,256]{1,0:T(8,128)S(1)}, f32[81,256]{1,0:T(8,128)}, u32[]{:S(2)}) copy-start(f32[81,256]{1,0:T(8,128)} %constant.50.clone) | copy-start | bytes 248836
  0.0 4.7 %collective-permute-start = (f32[3,8,8,128]{3,2,1,0:T(8,128)}, f32[3,8,8,128]{3,2,1,0:T(8,128)S(1)}, u32[]{:S(2)}, u32[]{:S(2)}) collective-permute-start(f32[3,8,8,128]{3,2,1,0:T(8,128)} %load_ref.1), channel_id=1, source_target_pairs={{0,1},{1,0},{2,3},{3,2},{4,5},{5,4},{6,7},{7,6},{8,9},{9,8},{10,11... | collective-permute-start | bytes 294920 | tf_op jit(solution)/shard_map/ppermute | solution.py:587
  0.8 4.0 %collective-permute-start.1 = (s32[4,4,64]{2,1,0:T(4,128)}, s32[4,4,64]{2,1,0:T(4,128)S(1)}, u32[]{:S(2)}, u32[]{:S(2)}) collective-permute-start(s32[4,4,64]{2,1,0:T(4,128)} %levels_ref.1), channel_id=1, source_target_pairs={{0,1},{1,0},{2,3},{3,2},{4,5},{5,4},{6,7},{7,6},{8,9},{9,8},{10,11... | collective-permute-start | bytes 12296 | tf_op jit(solution)/shard_map/ppermute | solution.py:587
  4.8 0.6 copy-start.20
  5.4 0.6 copy-start.10
  9.8 52.7 %copy-start.1 = (f32[24,24]{1,0:T(8,128)S(1)}, f32[24,24]{1,0:T(8,128)}, u32[]{:S(2)}) copy-start(f32[24,24]{1,0:T(8,128)} %param.18) | copy-start | bytes 6916
  9.8 52.7 %copy-start.18 = (f32[64,24]{1,0:T(8,128)S(1)}, f32[64,24]{1,0:T(8,128)}, u32[]{:S(2)}) copy-start(f32[64,24]{1,0:T(8,128)} %constant.51.clone) | copy-start | bytes 18436
  9.8 54.4 %copy-start.19 = (f32[24,128]{1,0:T(8,128)S(1)}, f32[24,128]{1,0:T(8,128)}, u32[]{:S(2)}) copy-start(f32[24,128]{1,0:T(8,128)} %constant.52.clone) | copy-start | bytes 36868
  9.8 8.3 %collective-permute-start.3 = (f32[104,512]{1,0:T(8,128)}, f32[104,512]{1,0:T(8,128)S(1)}, u32[]{:S(2)}, u32[]{:S(2)}) collective-permute-start(f32[104,512]{1,0:T(8,128)} %pack.1.refs_0_), channel_id=1, source_target_pairs={{0,2},{2,4},{4,6},{6,8},{8,10},{10,12},{12,14},{14,16},{16,18},{18... | collective-permute-start | bytes 638984 | tf_op jit(solution)/shard_map/ppermute | solution.py:592
  18.2 13.3 %copy-start.4 = (f32[104,512]{1,0:T(8,128)}, f32[104,512]{1,0:T(8,128)S(1)}, u32[]{:S(2)}) copy-start(f32[104,512]{1,0:T(8,128)S(1)} %collective-permute-done.3.refs_2_) | copy-start | bytes 638980
  18.2 8.3 %collective-permute-start.4 = (f32[104,512]{1,0:T(8,128)S(1)}, f32[104,512]{1,0:T(8,128)S(1)}, u32[]{:S(2)}, u32[]{:S(2)}) collective-permute-start(f32[104,512]{1,0:T(8,128)S(1)} %collective-permute-done.3.refs_2_), channel_id=1, source_target_pairs={{0,128},{128,0},{1,129},{129,1},{2,130},{130,2},{3,131},{131,3},{4... | collective-permute-start | bytes 638984 | tf_op jit(solution)/shard_map/ppermute | solution.py:587
  20.9 10.4 %collective-permute-start.2 = (f32[104,512]{1,0:T(8,128)}, f32[104,512]{1,0:T(8,128)S(1)}, u32[]{:S(2)}, u32[]{:S(2)}) collective-permute-start(f32[104,512]{1,0:T(8,128)} %pack.1.refs_0_), channel_id=1, source_target_pairs={{0,128},{128,0},{1,129},{129,1},{2,130},{130,2},{3,131},{131,3},{4... | collective-permute-start | bytes 638984 | tf_op jit(solution)/shard_map/ppermute | solution.py:587
  21.5 9.8 %collective-permute-start.5 = (f32[104,512]{1,0:T(8,128)S(1)}, f32[104,512]{1,0:T(8,128)S(1)}, u32[]{:S(2)}, u32[]{:S(2)}) collective-permute-start(f32[104,512]{1,0:T(8,128)S(1)} %collective-permute-done.3.refs_2_), channel_id=1, source_target_pairs={{0,1},{1,0},{2,3},{3,2},{4,5},{5,4},{6,7},{7,6},{8,9},{9,8},{10,11... | collective-permute-start | bytes 638984 | tf_op jit(solution)/shard_map/ppermute | solution.py:587
  26.5 5.0 %copy-start.5 = (f32[104,512]{1,0:T(8,128)}, f32[104,512]{1,0:T(8,128)S(1)}, u32[]{:S(2)}) copy-start(f32[104,512]{1,0:T(8,128)S(1)} %collective-permute-done.4.refs_3_) | copy-start | bytes 638980
  26.5 5.0 %collective-permute-start.6 = (f32[104,512]{1,0:T(8,128)S(1)}, f32[104,512]{1,0:T(8,128)S(1)}, u32[]{:S(2)}, u32[]{:S(2)}) collective-permute-start(f32[104,512]{1,0:T(8,128)S(1)} %collective-permute-done.4.refs_3_), channel_id=1, source_target_pairs={{0,1},{1,0},{2,3},{3,2},{4,5},{5,4},{6,7},{7,6},{8,9},{9,8},{10,11... | collective-permute-start | bytes 638984 | tf_op jit(solution)/shard_map/ppermute | solution.py:587
  31.4 0.7 copy-start.6
  31.4 0.8 copy-start.7
  32.1 0.7 copy-start.8
  45.1 12.2 %collective-permute-start.11 = (f32[96,1024]{1,0:T(8,128)}, f32[96,1024]{1,0:T(8,128)S(1)}, u32[]{:S(2)}, u32[]{:S(2)}) collective-permute-start(f32[96,1024]{1,0:T(8,128)} %get-tuple-element.11.refs_5_), channel_id=1, source_target_pairs={{0,2},{2,4},{4,6},{6,8},{8,10},{10,12},{12,14},{14,16},{16,18},{18... | collective-permute-start | bytes 1179656 | tf_op jit(solution)/shard_map/ppermute | solution.py:592
  52.2 10.5 %collective-permute-start.9 = (f32[24,1024]{1,0:T(8,128)}, f32[24,1024]{1,0:T(8,128)S(1)}, u32[]{:S(2)}, u32[]{:S(2)}) collective-permute-start(f32[24,1024]{1,0:T(8,128)} %get-tuple-element.10.refs_0_), channel_id=1, source_target_pairs={{0,4},{2,6},{4,8},{6,10},{8,12},{10,14},{12,16},{14,18},{16,20},{1... | collective-permute-start | bytes 294920 | tf_op jit(solution)/shard_map/ppermute | solution.py:592
  54.2 8.7 %collective-permute-start.7 = (f32[24,1024]{1,0:T(8,128)}, f32[24,1024]{1,0:T(8,128)S(1)}, u32[]{:S(2)}, u32[]{:S(2)}) collective-permute-start(f32[24,1024]{1,0:T(8,128)} %get-tuple-element.10.refs_0_), channel_id=1, source_target_pairs={{0,2},{2,4},{4,6},{6,8},{8,10},{10,12},{12,14},{14,16},{16,18},{18... | collective-permute-start | bytes 294920 | tf_op jit(solution)/shard_map/ppermute | solution.py:592
  57.3 7.9 %copy-start.2 = (f32[96,1024]{1,0:T(8,128)}, f32[96,1024]{1,0:T(8,128)S(1)}, u32[]{:S(2)}) copy-start(f32[96,1024]{1,0:T(8,128)S(1)} %collective-permute-done.11.refs_6_) | copy-start | bytes 1179652
  57.3 7.9 %collective-permute-start.12 = (f32[96,1024]{1,0:T(8,128)S(1)}, f32[96,1024]{1,0:T(8,128)S(1)}, u32[]{:S(2)}, u32[]{:S(2)}) collective-permute-start(f32[96,1024]{1,0:T(8,128)S(1)} %collective-permute-done.11.refs_6_), channel_id=1, source_target_pairs={{0,1},{1,0},{2,3},{3,2},{4,5},{5,4},{6,7},{7,6},{8,9},{9,8},{10,11... | collective-permute-start | bytes 1179656 | tf_op jit(solution)/shard_map/ppermute | solution.py:587
  62.7 2.5 %copy-start.11 = (f32[24,1024]{1,0:T(8,128)}, f32[24,1024]{1,0:T(8,128)S(1)}, u32[]{:S(2)}) copy-start(f32[24,1024]{1,0:T(8,128)S(1)} %collective-permute-done.9.refs_3_) | copy-start | bytes 294916
  62.7 2.4 %collective-permute-start.10 = (f32[24,1024]{1,0:T(8,128)S(1)}, f32[24,1024]{1,0:T(8,128)S(1)}, u32[]{:S(2)}, u32[]{:S(2)}) collective-permute-start(f32[24,1024]{1,0:T(8,128)S(1)} %collective-permute-done.9.refs_3_), channel_id=1, source_target_pairs={{0,1},{1,0},{2,3},{3,2},{4,5},{5,4},{6,7},{7,6},{8,9},{9,8},{10,11... | collective-permute-start | bytes 294920 | tf_op jit(solution)/shard_map/ppermute | solution.py:587
  62.8 2.4 %copy-start.12 = (f32[24,1024]{1,0:T(8,128)}, f32[24,1024]{1,0:T(8,128)S(1)}, u32[]{:S(2)}) copy-start(f32[24,1024]{1,0:T(8,128)S(1)} %collective-permute-done.7.refs_1_) | copy-start | bytes 294916
  62.9 2.3 %collective-permute-start.8 = (f32[24,1024]{1,0:T(8,128)S(1)}, f32[24,1024]{1,0:T(8,128)S(1)}, u32[]{:S(2)}, u32[]{:S(2)}) collective-permute-start(f32[24,1024]{1,0:T(8,128)S(1)} %collective-permute-done.7.refs_1_), channel_id=1, source_target_pairs={{0,1},{1,0},{2,3},{3,2},{4,5},{5,4},{6,7},{7,6},{8,9},{9,8},{10,11... | collective-permute-start | bytes 294920 | tf_op jit(solution)/shard_map/ppermute | solution.py:587
  65.1 0.6 copy-start.13
  65.2 0.6 copy-start.14
  65.2 0.8 copy-start.3

commit v2 on v1

v2 whole, which is shorter than its diff:
```python
import jax
import jax.numpy as jnp
import numpy as np
from jax import lax
from jax.experimental import pallas as pl
from jax.experimental.pallas import tpu as pltpu
from jax.sharding import PartitionSpec as P

DEG = 4
DENSITY_LEVELS = 16
MID = 1.125
HALF = 0.875

F32 = jnp.float32
BF16 = jnp.bfloat16

OWN = 4
SIDE = 4
FAR = 8
ROWS = OWN + 2 * SIDE
C_ROWS = OWN + 2 * FAR
LANES = 1024
WIDE = LANES + 128
AHEAD = 2
PART = 56
PACK = 104
NOTE = 24


def node_row(group, row):
    px, py = ((0, 0), (1, 0), (0, 1))[group]
    if row < 6:
        return row % 3, px, py, row // 3
    return group, 1, 1, row - 6


FINE_IN = [(g, sx, sy) for sx, sy, groups in ((0, 0, (0, 1, 2)), (1, 0, (0, 2)), (0, 1, (0, 1)), (1, 1, (0,))) for g in groups]
SHIFTS = [(0, 0), (1, 0), (0, 1), (1, 1)]


def fine_place(group, row, sx, sy, sz):
    p, px, py, pz = node_row(group, row)
    if (sx and px) or (sy and py) or (sz and pz):
        return None
    return 27 * p + 9 * (px + 2 * sx) + 3 * (py + 2 * sy) + pz + 2 * sz


def coarse_place(row, sx, sy, sz):
    return 8 * row + 4 * sx + 2 * sy + sz if row < 3 else None


def fine_selectors():
    out_rows = np.zeros((128, 81), np.float32)
    in_rows = np.zeros((256, 81), np.float32)
    at = 0
    for sz in (0, 1):
        for g, sx, sy in FINE_IN:
            for row in range(8):
                place = fine_place(g, row, sx, sy, sz)
                if place is not None:
                    out_rows[at + row, place] = 1.0
            at += 8
    at = 0
    for g, sx, sy in FINE_IN:
        for sz in (0, 1):
            for row in range(8):
                place = fine_place(g, row, sx, sy, sz)
                if place is not None:
                    in_rows[at + row, place] = 1.0
                    in_rows[at + 8 + row, place] = 1.0
            at += 16
    return out_rows, in_rows


def coarse_selectors():
    out_rows = np.zeros((32, 24), np.float32)
    in_rows = np.zeros((64, 24), np.float32)
    for at, (sx, sy) in enumerate(SHIFTS):
        for sz in (0, 1):
            for row in range(3):
                place = coarse_place(row, sx, sy, sz)
                out_rows[8 * at + 3 * sz + row, place] = 1.0
                in_rows[[16 * at + 3 * sz + row, 16 * at + 8 + 3 * sz + row], place] = 1.0
    return out_rows, in_rows


def weight_along(parity, shift):
    if parity == 0:
        return 1.0 if shift == 0 else 0.0
    return 0.5


def transfer_weights():
    prolong = np.zeros((24, 64), np.float32)
    restrict = np.zeros((32, 48), np.float32)
    for at, (sx, sy) in enumerate(SHIFTS):
        for sz in (0, 1):
            for g in range(3):
                for row in range(8):
                    p, px, py, pz = node_row(g, row)
                    w = weight_along(px, sx) * weight_along(py, sy) * weight_along(pz, sz)
                    prolong[8 * g + row, [16 * at + 3 * sz + p, 16 * at + 8 + 3 * sz + p]] = w
                    restrict[8 * at + 3 * sz + p, [16 * g + row, 16 * g + 8 + row]] = w
    return prolong, restrict


def row_shuffle():
    shuffle = np.zeros((96, 96), np.float32)
    for y in range(4):
        for g in range(3):
            for row in range(8):
                p, px, py, pz = node_row(g, row)
                shuffle[24 * y + 8 * g + row, pz * 48 + p * 16 + px * 8 + 2 * y + py] = 1.0
    return np.concatenate([shuffle, shuffle], axis=1)


def diag_selectors():
    fine_rows, fine_at = np.zeros((24, 81), np.float32), np.zeros((81, 16), np.float32)
    coarse_rows, coarse_at = np.zeros((8, 24), np.float32), np.zeros((24, 16), np.float32)
    for at in range(8):
        sy, sx, sz = at // 4, at // 2 % 2, at % 2
        for g in range(3):
            for row in range(8):
                place = fine_place(g, row, sx, sy, sz)
                if place is not None:
                    fine_rows[8 * g + row, place] = 1.0
                    fine_at[place, [at, at + 8]] = 1.0
        for row in range(3):
            place = coarse_place(row, sx, sy, sz)
            coarse_rows[row, place] = 1.0
            coarse_at[place, [at, at + 8]] = 1.0
    return fine_rows, fine_at, coarse_rows, coarse_at


def laid_out(parts):
    places, at = {}, 0
    for name, (rows, columns) in parts.items():
        places[name] = (at, rows, columns)
        at += -(-rows // 16) * 16
    return places, at


def constants():
    fine_out, fine_in = fine_selectors()
    coarse_out, coarse_in = coarse_selectors()
    fine_rows, fine_at, coarse_rows, coarse_at = diag_selectors()
    prolong, restrict = transfer_weights()
    return {
        "fine_out": fine_out, "fine_in": fine_in.T, "fine_rows": fine_rows, "fine_at": fine_at,
        "coarse_out": coarse_out, "coarse_in": coarse_in.T, "coarse_rows": coarse_rows, "coarse_at": coarse_at,
        "restrict": restrict, "prolong": prolong, "shuffle": row_shuffle(),
    }


CARDS, CARD_ROWS = laid_out({name: value.shape for name, value in constants().items()})
BOOKS = [
    laid_out({"fine": (256, 256), "fine_diag": (48, 16), "restrict": (32, 48)}),
    laid_out({"coarse": (64, 64), "coarse_diag": (16, 16)}),
    laid_out({"fine": (256, 256), "prolong": (24, 64), "shuffle": (96, 192)}),
]


def cards():
    sheet = np.zeros((CARD_ROWS, 256), np.float32)
    for name, value in constants().items():
        first, rows, columns = CARDS[name]
        sheet[first : first + rows, :columns] = value
    return jnp.asarray(sheet, dtype=BF16)


class Part:
    def __init__(self, ref, places, name):
        first, rows, columns = places[name]
        self.ref, self.at = ref, (slice(first, first + rows), slice(0, columns))

    def __getitem__(self, _):
        return self.ref[self.at]

    def __setitem__(self, _, values):
        self.ref[self.at] = values


def halves(values):
    high = values.astype(BF16).astype(F32)
    return high, (values - high).astype(BF16).astype(F32)


def fetched(copies, sems, first=0):
    started = [pltpu.make_async_copy(a, b, sems.at[first + i]) for i, (a, b) in enumerate(copies)]
    for copy in started:
        copy.start()
    return started


def wait_for(started):
    for copy in started:
        copy.wait()


def pack_kernel(place_ref, raw_sent, other_sent, out_ref, half_ref, raw, other, sems):
    gz = place_ref[2]
    copies = fetched([(raw_sent, raw), (other_sent, other)], sems)

    row = lax.broadcasted_iota(jnp.int32, (256, 256), 0)
    col = lax.broadcasted_iota(jnp.int32, (256, 256), 1)
    parter = jnp.where(2 * (col & 127) + (col >> 7) == ((row + 128 * gz) & 255), 1.0, 0.0).astype(BF16)
    row = lax.broadcasted_iota(jnp.int32, (256, 128), 0)
    col = lax.broadcasted_iota(jnp.int32, (256, 128), 1)
    half = jnp.where(row < 128, gz, 1 - gz)
    widen = jnp.where(((row & 127) < 64) & (col == (row & 127) + 64 * half), 1.0, 0.0).astype(BF16)

    row = lax.broadcasted_iota(jnp.int32, (96, 192), 0)
    col = lax.broadcasted_iota(jnp.int32, (96, 192), 1)
    y = sum(jnp.where(row >= 24 * i, 1, 0) for i in (1, 2, 3))
    group, at = (row >> 3) - 3 * y, row & 7
    back = jnp.where(at >= 3, 1, 0)
    corner = at >= 6
    component = jnp.where(corner, group, at - 3 * back)
    pz = jnp.where(corner, at - 6, back)
    px = jnp.where(corner | (group == 1), 1, 0)
    py = jnp.where(corner | (group == 2), 1, 0)
    source = 48 * pz + 16 * component + 8 * px + 2 * y + py
    shuffle = jnp.where(jnp.where(col >= 96, col - 96, col) == source, 1.0, 0.0).astype(BF16)

    wait_for(copies)
    high, low = halves(jnp.concatenate([raw[0:3].reshape(192, 128), other[0:3].reshape(192, 128)], axis=1))
    parted = jnp.dot(jnp.concatenate([high, low], axis=0).astype(BF16), parter, preferred_element_type=F32)
    parted = parted.reshape(2, 3, 8, 8, 256)
    pieces = []
    for x in range(4):
        near = parted[:, :, 2 * x : 2 * x + 2].reshape(2, 48, 256)
        pieces.append(
            jnp.concatenate([near[0, :, :128], near[0, :, 128:], near[1, :, :128], near[1, :, 128:]], axis=0)
        )
    stacked = jnp.concatenate(pieces, axis=1).astype(BF16)
    out_ref[0:96, :] = jnp.dot(shuffle, stacked, preferred_element_type=F32)

    levels = jnp.concatenate([raw[3, 0:4].reshape(32, 128), other[3, 0:4].reshape(32, 128)], axis=1)
    ratio = jnp.dot(levels.astype(BF16), widen, preferred_element_type=F32) / (DENSITY_LEVELS - 1)
    moduli = 0.05 + 0.95 * ratio * ratio * ratio
    for x in range(4):
        out_ref[96:104, 128 * x : 128 * x + 128] = moduli[8 * x : 8 * x + 8]
    half_ref[...] = out_ref[pl.ds(pl.multiple_of((PACK - PART) * gz, 8), PART), :]


def split(values):
    high = values.astype(BF16).astype(F32)
    return jnp.concatenate([high, values - high], axis=0).astype(BF16)


def roll_tiles(values, step):
    tiles = []
    for t in range(values.shape[1] // 128):
        tile = values[:, 128 * t : 128 * t + 128]
        lane = lax.broadcasted_iota(jnp.int32, tile.shape, 1)
        if step == 1:
            tiles.append(jnp.where(lane < 127, pltpu.roll(tile, 127, 1), 0.0))
        else:
            tiles.append(jnp.where(lane > 0, pltpu.roll(tile, 1, 1), 0.0))
    return tiles[0] if len(tiles) == 1 else jnp.concatenate(tiles, axis=1)


def hi_lo_weights(matrix, left, right):
    high, low = halves(matrix)
    col = lax.broadcasted_iota(jnp.int32, right.shape, 1)
    right_high = jnp.where(col % 16 < 8, right.astype(F32), 0.0).astype(BF16)
    rows = [
        jnp.dot(jnp.dot(left, part.astype(BF16), preferred_element_type=F32).astype(BF16), to, preferred_element_type=F32)
        for part, to in ((high, right), (low, right_high))
    ]
    return jnp.concatenate(rows, axis=0).astype(BF16)


def weights_kernel(fine_ref, coarse_ref, cards_ref, *book_refs):
    def card(name):
        return Part(cards_ref, CARDS, name)[...]

    matrices = {name: card(name) for name in ("restrict", "prolong", "shuffle")}
    for name, ref in (("fine", fine_ref), ("coarse", coarse_ref)):
        matrix = ref[...]
        row = lax.broadcasted_iota(jnp.int32, matrix.shape, 0)
        col = lax.broadcasted_iota(jnp.int32, matrix.shape, 1)
        diagonal = jnp.where(row == col, matrix, 0.0)
        matrices[name] = hi_lo_weights(matrix, card(name + "_out"), card(name + "_in"))
        matrices[name + "_diag"] = hi_lo_weights(diagonal, card(name + "_rows"), card(name + "_at"))
    for (places, _), book_ref in zip(BOOKS, book_refs, strict=True):
        for name in places:
            Part(book_ref, places, name)[...] = matrices[name]


def scaled(values, moduli):
    rows, lanes = values.shape
    return (values.reshape(rows // 8, 8, lanes) * moduli[None]).reshape(rows, lanes)


def schedules():
    sigma = MID / HALF
    rhos = [1.0 / sigma]
    for _ in range(DEG - 1):
        rhos.append(1.0 / (2.0 * sigma - rhos[-1]))
    smooth = [(rhos[s + 1] * rhos[s], 2.0 * rhos[s + 1] / HALF) for s in range(DEG - 1)]
    o, c = SIDE, FAR
    return {
        "start": ([(0, ROWS, 0.0, 0.0, 0.0)], 3),
        "before": ([(o - 3 + s, o + 7 - s, *smooth[s], 0.0) for s in range(DEG - 1)], 6),
        "leave": ([(o, o + 4, 0.0, 0.0, 0.0)], 4),
        "coarse_start": ([(c - 7, c + 11, 0.0, 0.0, 0.0)], 3),
        "coarse": ([(c - 7 + s, c + 10 - s, *smooth[s], float(s == DEG - 2)) for s in range(DEG - 1)], 9),
        "correct": ([(o - 4, o + 8, 0.0, 0.0, 0.0)], 3),
        "after": (
            [(o - 4, o + 7, 0.0, 1.0 / MID, 0.0)]
            + [(o - 3 + s, o + 6 - s + (s == DEG - 2), *smooth[s], 0.0) for s in range(DEG - 1)],
            3,
        ),
    }


def row_at(name, t):
    at, row = 0, None
    for first, last, *_ in schedules()[name][0]:
        here = t + (first - at)
        row = here if row is None else jnp.where(t >= at, here, row)
        at += last - first
    return jnp.where(t >= at, SIDE, row).astype(jnp.int32)


def factor_at(name, t, which):
    at, factor = 0, None
    for first, last, *factors in schedules()[name][0]:
        here = jnp.float32(factors[which])
        factor = here if factor is None else jnp.where(t >= at, here, factor)
        at += last - first
    return factor


CHUNKS = [(256 * n, slice(256 * n, 256 * n + 256)) for n in range(4)]


def pushed(before, values):
    return jnp.concatenate([before, values[:, :128]], axis=1)


def store_fine(fine_x, y, lanes, values):
    for g in range(3):
        part = values[8 * g : 8 * g + 8]
        fine_x[y, 32 * g : 32 * g + 16, lanes] = split(part)
        fine_x[y, 32 * g + 16 : 32 * g + 32, lanes] = split(roll_tiles(part, 1))


def store_coarse(coarse_x, y, lanes, values):
    row = lax.broadcasted_iota(jnp.int32, values.shape, 0)
    further = pltpu.roll(roll_tiles(values, 1), 3, 0)
    coarse_x[y, :, lanes] = split(jnp.where(row < 3, values, jnp.where(row < 6, further, 0.0)))


def pipeline(prods, name, issue, finish):
    sweeps, together = schedules()[name]
    count = sum(last - first for first, last, *_ in sweeps)
    assert count % together == 0
    assert together % (AHEAD + 1) == 0 or count == together
    for u in range(AHEAD):
        issue(row_at(name, jnp.int32(u)), prods[u])

    def some(i, _):
        t = together * i
        for u in range(together):
            issue(row_at(name, t + u + AHEAD), prods[(u + AHEAD) % len(prods)])
            finish(t + u, row_at(name, t + u), prods[u % len(prods)])
        return 0

    lax.fori_loop(0, count // together, some, 0)


def fine_issue(fine_w, fine_x):
    def issue(y, prod):
        for low, lanes in CHUNKS:
            there = slice(low + 128, low + 384)
            operand = jnp.concatenate(
                [
                    fine_x[y, :, lanes],
                    fine_x[y, 0:32, there],
                    fine_x[y, 64:96, there],
                    fine_x[y + 1, 0:64, lanes],
                    fine_x[y + 1, 0:32, there],
                ],
                axis=0,
            )
            products = jnp.dot(fine_w[...], operand, preferred_element_type=F32)
            prod[:, lanes] = products[:128] + products[128:]

    return issue


def fine_finish(moduli, carry, use):
    def finish(t, y, prod):
        before = [(jnp.zeros((16, 128), F32), jnp.zeros((8, 128), F32))] * 2
        for low, lanes in CHUNKS:
            m = moduli[y, :, lanes]
            sums = []
            for z in range(2):
                v = scaled(prod[64 * z : 64 * z + 64, lanes], m)
                old = carry[16 * z : 16 * z + 16, lanes]
                along_x = pushed(before[z][0], v[24:40])
                along_xy = pushed(before[z][1], v[56:64])
                before[z] = (v[24:40, 128:], v[56:64, 128:])
                sums.append(
                    jnp.concatenate(
                        [v[0:8] + along_x[0:8] + old[0:8], v[8:16] + old[8:16], v[16:24] + along_x[8:16]], axis=0
                    )
                )
                carry[16 * z : 16 * z + 16, lanes] = jnp.concatenate([v[40:48] + along_xy, v[48:56]], axis=0)
            use(t, y, lanes, sums[0] + roll_tiles(sums[1], -1))

    return finish


def coarse_finish(moduli, carry, use):
    def finish(t, y, prod):
        before = (jnp.zeros((8, 128), F32), jnp.zeros((8, 128), F32))
        for low, lanes in CHUNKS:
            v = prod[0:32, lanes]
            if moduli is not None:
                v = scaled(v, moduli[y, :, lanes])
            sums = v[0:8] + pushed(before[0], v[8:16]) + carry[:, lanes]
            carry[:, lanes] = v[16:24] + pushed(before[1], v[24:32])
            before = (v[8:16, 128:], v[24:32, 128:])
            use(t, y, lanes, sums + roll_tiles(pltpu.roll(sums, 5, 0), -1))

    return finish


def smooth_fine(name, inverse, res, step, total, fine_x):
    def use(t, y, lanes, sums):
        keep, gain = factor_at(name, t, 0), factor_at(name, t, 1)
        r = res[y, :, lanes] - sums
        d = keep * step[y, :, lanes] + gain * (inverse[y, :, lanes] * r)
        res[y, :, lanes] = r
        step[y, :, lanes] = d
        total[y, :, lanes] = total[y, :, lanes] + d
        store_fine(fine_x, y, lanes, d)

    return use


def diag_issue(diag_w, moduli, count):
    def issue(y, prod):
        spot = lax.broadcasted_iota(jnp.int32, (8, 256), 0)
        before = jnp.zeros((8, 128), F32)
        for low, lanes in CHUNKS:
            near = jnp.where(spot < 4, moduli[y, :, lanes], moduli[jnp.maximum(y - 1, 0), :, lanes])
            moved = pushed(before, near)
            before = near[:, 128:]
            around = jnp.where(spot % 4 < 2, near, moved)
            around = jnp.where(spot % 2 < 1, around, roll_tiles(around, -1))
            products = jnp.dot(diag_w[...], split(around), preferred_element_type=F32)
            prod[0:count, lanes] = products[:count] + products[count:]

    return issue


def clear_tail(ref, rows):
    def clear(y, _):
        ref[y, :, LANES:] = jnp.zeros((ref.shape[1], 128), BF16)
        return 0

    lax.fori_loop(0, rows, clear, 0)


def validity(place_ref, ahead):
    first, count = place_ref[1] * OWN - ahead, place_ref[3] * OWN

    def valid(y):
        return jnp.where((first + y >= 0) & (first + y < count), 1.0, 0.0).astype(F32)

    return valid


def before_kernel(place_ref, *refs):
    blocks = refs[:7]
    book_ref, outs = refs[7], refs[8:13]
    (book, res, step, total, fine_x, carry, load, moduli, inverse, note, moduli_rows, c_carry, sems, out_sems, *prods) = refs[13:]
    gx, gz = place_ref[0], place_ref[2]
    valid = validity(place_ref, SIDE)
    o = SIDE

    own, a, ax, za, zax, half, half_other = blocks
    lanes_of = [pl.ds(pl.multiple_of(x * 512, 512), 512) for x in (gx, 1 - gx)]
    side = 1 - 2 * gz
    spots = [(own, 0, 0), (a, -side, 0), (ax, -side, 1), (za, side, 0), (zax, side, 1)]
    fine_w, diag_w, restrict_w = [Part(book, BOOKS[0][0], name) for name in BOOKS[0][0]]
    copies = [(book_ref, book)]
    for i, (ref, offset, across) in enumerate(spots):
        copies.append((ref.at[96:104, :], moduli_rows.at[i]))
        for y in range(OWN):
            copies.append((ref.at[24 * y : 24 * y + 24, :], load.at[o + OWN * offset + y, :, lanes_of[across]]))
    for i, (ref, core) in enumerate([(half, gz), (half_other, 1 - gz)]):
        copies.append((ref.at[PART - 8 : PART, :], moduli_rows.at[5 + i]))
        for y in range(2):
            first = pl.multiple_of(24 * y + (PACK - PART - 48) * core, 8)
            copies.append((ref.at[pl.ds(first, 24), :], load.at[o + 2 * core + y, :, lanes_of[1]]))
    copies = fetched(copies, sems)
    clear_tail(fine_x, ROWS)
    carry[...] = jnp.zeros_like(carry)
    wait_for(copies)
    own_rows = jnp.where(jnp.full((8, 512), gz) == 1, moduli_rows[5], moduli_rows[6])
    for rows, offset, across in [(moduli_rows[i], *spot[1:]) for i, spot in enumerate(spots)] + [(own_rows, 0, 1)]:
        for y in range(OWN):
            moduli[o + OWN * offset + y, :, lanes_of[across]] = jnp.broadcast_to(rows[y : y + 1], (8, 512))
    leaving = fetched([(load, outs[0]), (moduli, outs[1])], out_sems)

    def start(t, y, prod):
        ok = valid(y)
        for low, lanes in CHUNKS:
            inv = ok / (prod[0:24, lanes] + (1.0 - ok))
            r = load[y, :, lanes]
            d = inv * r * (1.0 / MID)
            inverse[y, :, lanes] = inv
            res[y, :, lanes] = r
            step[y, :, lanes] = d
            total[y, :, lanes] = d
            store_fine(fine_x, y, lanes, d)

    pipeline(prods, "start", diag_issue(diag_w, moduli, 24), start)
    leaving += fetched([(inverse, outs[2])], out_sems, len(leaving))
    issue = fine_issue(fine_w, fine_x)
    use = smooth_fine("before", inverse, res, step, total, fine_x)
    pipeline(prods, "before", issue, fine_finish(moduli, carry, use))
    rows = [(total.at[o + y], outs[3].at[24 * y : 24 * y + 24, :]) for y in range(OWN)]
    leaving += fetched(rows, out_sems, len(leaving))

    carry[...] = jnp.zeros_like(carry)

    def store_left(y, lanes, left):
        for g in range(3):
            fine_x[y, 16 * g : 16 * g + 16, lanes] = split(left[8 * g : 8 * g + 8])

    def leave(t, y, lanes, sums):
        store_left(y, lanes, res[y, :, lanes] - sums)

    pipeline(prods, "leave", issue, fine_finish(moduli, carry, leave))
    for low, lanes in CHUNKS:
        last = carry[0:16, lanes] + roll_tiles(carry[16:32, lanes], -1)
        last = jnp.concatenate([last, jnp.zeros((8, 256), F32)], axis=0)
        store_left(o + OWN, lanes, -last * valid(o + OWN))

    c_carry[...] = jnp.zeros_like(c_carry)
    for j in range(OWN + 1):
        prod = prods[j % len(prods)]
        for low, lanes in CHUNKS:
            prod[0:32, lanes] = jnp.dot(restrict_w[...], fine_x[o + j, 0:48, lanes], preferred_element_type=F32)

        def keep(t, y, lanes, sums, j=j):
            note[3 * j : 3 * j + 3, lanes] = sums[0:3]

        coarse_finish(None, c_carry, keep)(0, o + j, prod)
    for y in range(OWN):
        note[16 + y : 17 + y, :] = moduli[o + y, 0:1, :]
    leaving += fetched([(note, outs[4])], out_sems, len(leaving))
    wait_for(leaving)


def coarse_operand(coarse_x, y, low, lanes):
    there = slice(low + 128, low + 384)
    return jnp.concatenate(
        [coarse_x[y, :, lanes], coarse_x[y, :, there], coarse_x[y + 1, :, lanes], coarse_x[y + 1, :, there]], axis=0
    )


def coarse_kernel(place_ref, *refs):
    note, m1, zm1, m2, zm2, near_moduli, book_ref, fix = refs[:8]
    book, moduli, notes, c_inverse, c_res, c_step, c_total, coarse_x, c_carry, sems, *prods = refs[8:]
    gz = place_ref[2]
    o, c = SIDE, FAR
    valid = validity(place_ref, FAR)
    side = 1 - 2 * gz

    spots = [(note, 0), (m1, -side), (zm1, side), (m2, -2 * side), (zm2, 2 * side)]
    copies = [(ref, notes.at[i]) for i, (ref, _) in enumerate(spots)]
    copies.append((near_moduli, moduli.at[c - o : c - o + ROWS]))
    copies.append((book_ref, book))
    coarse_w, diag_w = [Part(book, BOOKS[1][0], name) for name in BOOKS[1][0]]
    copies = fetched(copies, sems)
    clear_tail(coarse_x, C_ROWS)
    c_carry[...] = jnp.zeros_like(c_carry)
    c_res[...] = jnp.zeros_like(c_res)
    wait_for(copies)
    for i, (_, offset) in enumerate(spots):
        at = c + OWN * offset
        if i >= 3:
            for y in range(OWN):
                moduli[at + y] = jnp.broadcast_to(notes[i, 16 + y : 17 + y, :], (8, LANES))
        for y in range(OWN + 1):
            c_res[at + y, 0:3, :] = c_res[at + y, 0:3, :] + notes[i, 3 * y : 3 * y + 3, :]

    def start(t, y, prod):
        ok = valid(y)
        for low, lanes in CHUNKS:
            used = lax.broadcasted_iota(jnp.int32, (8, 256), 0) < 3
            inv = jnp.where(used, ok / (prod[0:8, lanes] + (1.0 - ok)), 0.0)
            d = inv * c_res[y, :, lanes] * (1.0 / MID)
            c_inverse[y, :, lanes] = inv
            c_step[y, :, lanes] = d
            c_total[y, :, lanes] = d
            store_coarse(coarse_x, y, lanes, d)

    pipeline(prods, "coarse_start", diag_issue(diag_w, moduli, 8), start)

    def issue(y, prod):
        for low, lanes in CHUNKS:
            products = jnp.dot(coarse_w[...], coarse_operand(coarse_x, y, low, lanes), preferred_element_type=F32)
            prod[0:32, lanes] = products[:32] + products[32:]

    def smooth(t, y, lanes, sums):
        keep, gain, last = [factor_at("coarse", t, which) for which in range(3)]
        r = c_res[y, :, lanes] - sums
        d = keep * c_step[y, :, lanes] + gain * (c_inverse[y, :, lanes] * r)
        so_far = c_total[y, :, lanes]
        c_res[y, :, lanes] = r
        c_step[y, :, lanes] = d
        c_total[y, :, lanes] = so_far + d
        store_coarse(coarse_x, y, lanes, d + last * so_far)

    pipeline(prods, "coarse", issue, coarse_finish(moduli, c_carry, smooth))
    wait_for(fetched([(coarse_x.at[c - o : c - o + ROWS + 1], fix)], sems))


def after_kernel(place_ref, *refs):
    fix_sent, s0, s1, zs1, load_sent, moduli_sent, inverse_sent, book_ref, out_ref = refs[:9]
    (book, res, step, total, fine_x, carry, load, moduli, inverse, fix, sems, *prods) = refs[9:]
    gx, gz = place_ref[0], place_ref[2]
    o = SIDE
    side = 1 - 2 * gz

    fine_w, prolong_w, shuffle = [Part(book, BOOKS[2][0], name) for name in BOOKS[2][0]]
    copies = [(fix_sent, fix), (load_sent, load), (book_ref, book)]
    for ref, offset in [(s0, 0), (s1, -side), (zs1, side)]:
        for y in range(OWN):
            copies.append((ref.at[24 * y : 24 * y + 24, :], total.at[o + OWN * offset + y]))
    first = fetched(copies, sems)
    second = fetched([(inverse_sent, inverse), (moduli_sent, moduli)], sems, len(first))
    clear_tail(fine_x, ROWS)
    carry[...] = jnp.zeros_like(carry)
    wait_for(first)

    def correct_issue(y, prod):
        for low, lanes in CHUNKS:
            prod[0:24, lanes] = jnp.dot(
                prolong_w[...], coarse_operand(fix, y, low, lanes), preferred_element_type=F32
            )

    def correct(t, y, prod):
        for low, lanes in CHUNKS:
            corrected = total[y, :, lanes] + prod[0:24, lanes]
            total[y, :, lanes] = corrected
            res[y, :, lanes] = load[y, :, lanes]
            step[y, :, lanes] = jnp.zeros((24, 256), F32)
            store_fine(fine_x, y, lanes, corrected)

    pipeline(prods, "correct", correct_issue, correct)
    wait_for(second)
    use = smooth_fine("after", inverse, res, step, total, fine_x)
    pipeline(prods, "after", fine_issue(fine_w, fine_x), fine_finish(moduli, carry, use))

    row = lax.broadcasted_iota(jnp.int32, (256, 128), 0)
    col = lax.broadcasted_iota(jnp.int32, (256, 128), 1)
    weave = (row == 128 * (col % 2) + 64 * gz + col // 2).astype(F32).astype(BF16)
    lanes = pl.ds(pl.multiple_of(gx * 512, 512), 512)
    high, low = halves(total[o : o + OWN, :, lanes].reshape(96, 512))
    pieces = []
    for part in (high, low):
        back = lax.dot_general(
            shuffle[...][:, 0:96], part.astype(BF16), (((0,), (0,)), ((), ())), preferred_element_type=F32
        )
        for x in range(4):
            near = back[:, 128 * x : 128 * x + 128]
            pieces.append(jnp.concatenate([near[0:48], near[48:96]], axis=1))
    woven = jnp.dot(jnp.concatenate(pieces, axis=0).astype(BF16), weave, preferred_element_type=F32)
    woven = woven[:192] + woven[192:]
    for x in range(4):
        out_ref[:, 2 * x : 2 * x + 2] = woven[48 * x : 48 * x + 48].reshape(3, 2, 8, 128)


def per_device(adjoint_load, levels, fine_stiffness, coarse_stiffness):
    count = lax.axis_size("gy")
    place = jnp.stack(
        [lax.axis_index("gx"), lax.axis_index("gy"), lax.axis_index("gz"), jnp.int32(count)]
    ).astype(jnp.int32)

    def swap(value, axis):
        return lax.ppermute(value, axis, [(0, 1), (1, 0)])

    def sided(value, steps, across=False):
        pairs = []
        for gx in range(2):
            for i in range(count - steps):
                low, high = 2 * (gx * count + i), 2 * (gx * count + i + steps)
                other = 2 * count * (1 - 2 * gx) if across else 0
                pairs += [(low, high + other), (high + 1, low + other + 1)]
        return lax.ppermute(value, ("gx", "gy", "gz"), pairs)

    whole = pl.BlockSpec(memory_space=pltpu.VMEM)
    there = pl.BlockSpec(memory_space=pl.ANY)
    scalars = pl.BlockSpec(memory_space=pltpu.SMEM)

    def pack(raw, other):
        return pl.pallas_call(
            pack_kernel,
            out_shape=[jax.ShapeDtypeStruct((rows, 512), F32) for rows in (PACK, PART)],
            in_specs=[scalars, there, there],
            out_specs=[whole] * 2,
            scratch_shapes=[pltpu.VMEM(raw.shape, F32)] * 2 + [pltpu.SemaphoreType.DMA((2,))],
            compiler_params=pltpu.CompilerParams(vmem_limit_bytes=8 * 1024 * 1024),
            name="pack",
        )(place, raw, other)

    book, coarse_book, after_book = pl.pallas_call(
        weights_kernel,
        out_shape=[jax.ShapeDtypeStruct((rows, 256), BF16) for _, rows in BOOKS],
        in_specs=[whole] * 3,
        out_specs=[whole] * 3,
        compiler_params=pltpu.CompilerParams(vmem_limit_bytes=8 * 1024 * 1024),
        name="weights",
    )(fine_stiffness, coarse_stiffness, cards())

    _, x_nodes, y_nodes, z_nodes = adjoint_load.shape
    room = [(0, whole_size - size) for whole_size, size in zip((x_nodes, y_nodes, z_nodes), levels.shape, strict=True)]
    raw = jnp.concatenate([adjoint_load, jnp.pad(levels, room).astype(F32)[None]], axis=0)
    own, half = pack(raw, swap(raw, "gz"))
    a, ax = sided(own, 1), sided(own, 1, True)
    half_x = swap(half, "gx")
    blocks = [own, a, ax, swap(lax.optimization_barrier((a, book))[0], "gz"), swap(ax, "gz"), half_x, swap(half_x, "gz")]

    def held(count, height=24):
        return pltpu.VMEM((count, height, LANES), F32)

    fine_scratch = [
        held(ROWS),
        held(ROWS),
        held(ROWS),
        pltpu.VMEM((ROWS + 1, 96, WIDE), BF16),
        pltpu.VMEM((32, LANES), F32),
        held(ROWS),
    ]
    prods = [pltpu.VMEM((128, LANES), F32)] * (AHEAD + 1)
    limit = pltpu.CompilerParams(vmem_limit_bytes=24 * 1024 * 1024)
    load, moduli, inverse, smoothed, note = pl.pallas_call(
        before_kernel,
        out_shape=[
            jax.ShapeDtypeStruct(shape, F32)
            for shape in [(ROWS, 24, LANES), (ROWS, 8, LANES), (ROWS, 24, LANES), (24 * OWN, LANES), (NOTE, LANES)]
        ],
        in_specs=[scalars] + [there] * 8,
        out_specs=[there] * 5,
        scratch_shapes=[pltpu.VMEM(book.shape, BF16), *fine_scratch]
        + [
            held(ROWS, 8),
            held(ROWS),
            pltpu.VMEM((NOTE, LANES), F32),
            pltpu.VMEM((7, 8, 512), F32),
            pltpu.VMEM((8, LANES), F32),
            pltpu.SemaphoreType.DMA((5 * (OWN + 1) + 7,)),
            pltpu.SemaphoreType.DMA((OWN + 4,)),
            *prods,
        ],
        compiler_params=limit,
        name="before",
    )(place, *blocks, book)

    m1, m2 = sided(note, 1), sided(note, 2)
    s1 = sided(smoothed, 1)
    fix = pl.pallas_call(
        coarse_kernel,
        out_shape=jax.ShapeDtypeStruct((ROWS + 1, 16, WIDE), BF16),
        in_specs=[scalars] + [there] * 7,
        out_specs=there,
        scratch_shapes=[
            pltpu.VMEM(coarse_book.shape, BF16),
            held(C_ROWS, 8),
            pltpu.VMEM((5, NOTE, LANES), F32),
            held(C_ROWS, 8),
            held(C_ROWS + 1, 8),
            held(C_ROWS, 8),
            held(C_ROWS, 8),
            pltpu.VMEM((C_ROWS + 1, 16, WIDE), BF16),
            pltpu.VMEM((8, LANES), F32),
            pltpu.SemaphoreType.DMA((7,)),
            *prods,
        ],
        compiler_params=limit,
        cost_estimate=pl.CostEstimate(flops=4 * 10**9, bytes_accessed=4 * 10**7, transcendentals=0),
        name="coarse",
    )(place, note, m1, swap(m1, "gz"), m2, swap(m2, "gz"), moduli, coarse_book)
    return pl.pallas_call(
        after_kernel,
        out_shape=jax.ShapeDtypeStruct(adjoint_load.shape, F32),
        in_specs=[scalars] + [there] * 8,
        out_specs=whole,
        scratch_shapes=[
            pltpu.VMEM(after_book.shape, BF16),
            *fine_scratch,
            held(ROWS, 8),
            held(ROWS),
            pltpu.VMEM((ROWS + 1, 16, WIDE), BF16),
            pltpu.SemaphoreType.DMA((3 * OWN + 5,)),
            *prods,
        ],
        compiler_params=limit,
        name="after",
    )(place, fix, smoothed, s1, swap(s1, "gz"), load, moduli, inverse, after_book)


def solution(mesh):
    return jax.shard_map(
        per_device,
        mesh=mesh,
        in_specs=(P(None, "gx", "gy", "gz"), P("gx", "gy", "gz"), P(), P()),
        out_specs=P(None, "gx", "gy", "gz"),
        check_vma=False,
    )
```

time: 90 us -> 78.7 us (0.87)
  starting transfers between devices: 35.7 us -> 27 us
  waiting for transfers between devices: 3.62 us -> 9.08 us
  local copies, waits for them, and re-layouts: 7.24 us -> 2.46 us
  matrix products: 2.31 us -> 0 us
  Pallas kernels: 39.7 us -> 38 us
    pallas_call x1, Pallas kernels: 23.6 us -> 14.1 us  [per_device(): pl.pallas_call(after_kernel, out_shape=jax.ShapeDtypeStruct(adjoint_load....]
    ppermute x9 -> x8, starting transfers between devices: 19.5 us -> 11 us  [swap(): return lax.ppermute(value, axis, [(0, 1), (1, 0)])]
    pallas_call x1 -> x3, Pallas kernels: 3.82 us -> 11.9 us  [the longest x1 9.77 us: per_device(): pl.pallas_call(coarse_kernel, out_shape=jax.ShapeDtypeStruct((ROWS + 1, 1...]
    gather x2 -> x0, local copies, waits for them, and re-layouts: 3.2 us -> none  [the longest x1 1.68 us: per_device(): diag = jnp.sum(jnp.asarray(fine_at) * jnp.diagonal(fine_stiffness), axis=1)]
    ppermute x9 -> x8, waiting for transfers between devices: 0.22 us -> 2.97 us  [swap(): return lax.ppermute(value, axis, [(0, 1), (1, 0)])]
    ppermute x4 -> x5, waiting for transfers between devices: 3.4 us -> 6.11 us  [sided(): return lax.ppermute(value, ('gx', 'gy', 'gz'), pairs)]
    dot_general x4 -> x0, matrix products: 2.31 us -> none  [exact_dot(): return jnp.dot(a, b, precision=EXACT, preferred_element_type=F32)]
    unnamed x42 -> x6, local copies, waits for them, and re-layouts: 3.35 us -> 2.46 us
  transfers between devices with their start and end apart: 13 -> 13, of which waited for: 4 -> 6; matrix products, arithmetic and copies ran while one was open for 8% -> 0% of each run, Pallas kernels for 0% -> 13%
where the time goes in v2:
time: 78.7 us; the launch traced here: 78.3 us
  Pallas kernels  38 us (48%)
  starting transfers between devices  27 us (34%)
  waiting for transfers between devices  9.08 us (12%)
  local copies, waits for them, and re-layouts  2.46 us (3%)
  other arithmetic  1.68 us (2%)
    ppermute x5, starting transfers between devices, sided(): return lax.ppermute(value, ('gx', 'gy', 'gz'), pairs)  16 us
    pallas_call x1, Pallas kernels, per_device(): pl.pallas_call(after_kernel, out_shape=jax.ShapeDtypeStruct(adjoint_load....  14.1 us
    pallas_call x1, Pallas kernels, per_device(): pl.pallas_call(before_kernel, out_shape=[jax.ShapeDtypeStruct(shape, F32)...  12 us
    ppermute x8, starting transfers between devices, swap(): return lax.ppermute(value, axis, [(0, 1), (1, 0)])  11 us
    pallas_call x1, Pallas kernels, per_device(): pl.pallas_call(coarse_kernel, out_shape=jax.ShapeDtypeStruct((ROWS + 1, 1...  9.77 us
    ppermute x5, waiting for transfers between devices, sided(): return lax.ppermute(value, ('gx', 'gy', 'gz'), pairs)  6.11 us
    ppermute x8, waiting for transfers between devices, swap(): return lax.ppermute(value, axis, [(0, 1), (1, 0)])  2.97 us
    unnamed x6, local copies, waits for them, and re-layouts  2.46 us
  transfers between devices with their start and end apart: 13, of which 6 were waited for; matrix products, arithmetic and copies ran while one was open for 0% of the time, Pallas kernels for 13%

profile of v2, /device:TPU:129, one launch (start us, length us, event | category | flops | bytes accessed | tf_op | source)
XLA Modules:
  0.0 78.3 jit_solution(17707651214058858123)
XLA Ops:
  0.0 0.7 convert_bitcast_fusion
  0.7 0.9 %pad_maximum_fusion.raw_sent = f32[4,8,8,128]{3,2,1,0:T(8,128)S(1)} fusion(f32[1,8,8,128]{3,2,1,0:T(8,128)S(1)} %convert_bitcast_fusion, f32[3,8,8,128]{3,2,1,0:T(8,128)} %param.5), kind=kLoop, calls=%fused_computation | loop fusion | flops 32768 | bytes 262144 | tf_op jit(solution)/shard_map/concatenate | solution.py:727
  1.6 0.8 collective-permute-start
  2.4 0.1 pad_add_fusion.place_ref
  2.4 0.9 %collective-permute-done.other_sent = f32[4,8,8,128]{3,2,1,0:T(8,128)S(1)} collective-permute-done((f32[4,8,8,128]{3,2,1,0:T(8,128)S(1)}, f32[4,8,8,128]{3,2,1,0:T(8,128)S(1)}, u32[]{:S(2)}, u32[]{:S(2)}) %collective-permute-start) | collective-permute-done | bytes 131104 | tf_op jit(solution)/shard_map/ppermute | solution.py:690
  3.4 1.4 %pack.1 = (f32[104,512]{1,0:T(8,128)S(1)}, f32[56,512]{1,0:T(8,128)S(1)}) custom-call(s32[4]{0:T(128)S(1)} %pad_add_fusion.place_ref, f32[4,8,8,128]{3,2,1,0:T(8,128)S(1)} %pad_maximum_fusion.raw_sent, f32[4,8,8,128]{3,2,1,0:T(8,128)S(1)} %collective-permute-done.other_sent), custom_call_target="tpu_custom_call" | custom-call | tf_op jit(solution)/shard_map/pack/pallas_call | solution.py:706
  4.8 5.1 %collective-permute-start.1 = (f32[104,512]{1,0:T(8,128)S(1)}, f32[104,512]{1,0:T(8,128)S(1)}, u32[]{:S(2)}, u32[]{:S(2)}) collective-permute-start(f32[104,512]{1,0:T(8,128)S(1)} %get-tuple-element.16.refs_0_), channel_id=1, source_target_pairs={{0,2},{3,1},{2,4},{5,3},{4,6},{7,5},{6,8},{9,7},{8,10},{11,9},{10,... | collective-permute-start | bytes 638984 | tf_op jit(solution)/shard_map/ppermute | solution.py:699
  9.9 3.7 %collective-permute-start.2 = (f32[104,512]{1,0:T(8,128)S(1)}, f32[104,512]{1,0:T(8,128)S(1)}, u32[]{:S(2)}, u32[]{:S(2)}) collective-permute-start(f32[104,512]{1,0:T(8,128)S(1)} %get-tuple-element.16.refs_0_), channel_id=1, source_target_pairs={{0,130},{3,129},{2,132},{5,131},{4,134},{7,133},{6,136},{9,135},{8... | collective-permute-start | bytes 638984 | tf_op jit(solution)/shard_map/ppermute | solution.py:699
  13.7 0.7 collective-permute-start.5
  14.4 0.0 copy-start
  14.4 1.0 %copy-done = bf16[624,256]{1,0:T(8,128)(2,1)S(1)} copy-done((bf16[624,256]{1,0:T(8,128)(2,1)S(1)}, bf16[624,256]{1,0:T(8,128)(2,1)}, u32[]{:S(2)}) %copy-start) | copy-done | bytes 319512
  15.4 0.0 copy-start.1
  15.4 0.8 %copy-done.1 = f32[81,81]{1,0:T(8,128)S(1)} copy-done((f32[81,81]{1,0:T(8,128)S(1)}, f32[81,81]{1,0:T(8,128)}, u32[]{:S(2)}) %copy-start.1) | copy-done | bytes 26268
  16.1 0.0 copy-start.2
  16.1 0.7 copy-done.2
  16.9 0.6 weights.1
  17.5 0.0 collective-permute-done.1.refs_1_
  17.5 4.8 %collective-permute-done.2.refs_2_ = f32[104,512]{1,0:T(8,128)S(1)} collective-permute-done((f32[104,512]{1,0:T(8,128)S(1)}, f32[104,512]{1,0:T(8,128)S(1)}, u32[]{:S(2)}, u32[]{:S(2)}) %collective-permute-start.2) | collective-permute-done | bytes 213024 | tf_op jit(solution)/shard_map/ppermute | solution.py:699
  22.3 1.1 %collective-permute-start.4 = (f32[104,512]{1,0:T(8,128)S(1)}, f32[104,512]{1,0:T(8,128)S(1)}, u32[]{:S(2)}, u32[]{:S(2)}) collective-permute-start(f32[104,512]{1,0:T(8,128)S(1)} %collective-permute-done.2.refs_2_), channel_id=1, source_target_pairs={{0,1},{1,0},{2,3},{3,2},{4,5},{5,4},{6,7},{7,6},{8,9},{9,8},{10,11... | collective-permute-start | bytes 638984 | tf_op jit(solution)/shard_map/ppermute | solution.py:690
  23.4 0.0 collective-permute-start.3
  23.4 0.0 collective-permute-done.5.refs_5_
  23.4 0.5 collective-permute-start.6
  23.9 1.1 %collective-permute-done.6.refs_6_ = f32[56,512]{1,0:T(8,128)S(1)} collective-permute-done((f32[56,512]{1,0:T(8,128)S(1)}, f32[56,512]{1,0:T(8,128)S(1)}, u32[]{:S(2)}, u32[]{:S(2)}) %collective-permute-start.6) | collective-permute-done | bytes 114720 | tf_op jit(solution)/shard_map/ppermute | solution.py:690
  25.0 0.0 collective-permute-done.4.refs_4_
  25.0 0.0 collective-permute-done.3.refs_3_
  25.0 12.0 %before.1 = (f32[12,24,1024]{2,1,0:T(8,128)S(1)}, f32[12,8,1024]{2,1,0:T(8,128)S(1)}, f32[12,24,1024]{2,1,0:T(8,128)S(1)}, f32[96,1024]{1,0:T(8,128)S(1)}, f32[24,1024]{1,0:T(8,128)S(1)}) custom-call(s32[4]{0:T(128)S(1)} %pad_add_fusion.place_ref, f32[104,512]{1,0:T(8,128)S(1)} %get-tuple-element.16.refs_0_, f32[104,512]{1,0:T(8,128)S(1)} %collective-permute-done.1.refs_1_, ...), custom_call_target="tpu_custom_call" | custom-call | tf_op jit(solution)/shard_map/before/pallas_call | solution.py:746
  37.0 2.1 %collective-permute-start.11 = (f32[96,1024]{1,0:T(8,128)S(1)}, f32[96,1024]{1,0:T(8,128)S(1)}, u32[]{:S(2)}, u32[]{:S(2)}) collective-permute-start(f32[96,1024]{1,0:T(8,128)S(1)} %get-tuple-element.23.refs_1_), channel_id=1, source_target_pairs={{0,2},{3,1},{2,4},{5,3},{4,6},{7,5},{6,8},{9,7},{8,10},{11,9},{10,... | collective-permute-start | bytes 1179656 | tf_op jit(solution)/shard_map/ppermute | solution.py:699
  39.2 1.9 %collective-permute-start.9 = (f32[24,1024]{1,0:T(8,128)S(1)}, f32[24,1024]{1,0:T(8,128)S(1)}, u32[]{:S(2)}, u32[]{:S(2)}) collective-permute-start(f32[24,1024]{1,0:T(8,128)S(1)} %get-tuple-element.20.refs_0_), channel_id=1, source_target_pairs={{0,4},{5,1},{2,6},{7,3},{4,8},{9,5},{6,10},{11,7},{8,12},{13,9},{1... | collective-permute-start | bytes 294920 | tf_op jit(solution)/shard_map/ppermute | solution.py:699
  41.1 3.1 %collective-permute-start.7 = (f32[24,1024]{1,0:T(8,128)S(1)}, f32[24,1024]{1,0:T(8,128)S(1)}, u32[]{:S(2)}, u32[]{:S(2)}) collective-permute-start(f32[24,1024]{1,0:T(8,128)S(1)} %get-tuple-element.20.refs_0_), channel_id=1, source_target_pairs={{0,2},{3,1},{2,4},{5,3},{4,6},{7,5},{6,8},{9,7},{8,10},{11,9},{10,... | collective-permute-start | bytes 294920 | tf_op jit(solution)/shard_map/ppermute | solution.py:699
  44.2 0.7 collective-permute-done.9.refs_3_
  45.0 5.2 %collective-permute-start.10 = (f32[24,1024]{1,0:T(8,128)S(1)}, f32[24,1024]{1,0:T(8,128)S(1)}, u32[]{:S(2)}, u32[]{:S(2)}) collective-permute-start(f32[24,1024]{1,0:T(8,128)S(1)} %collective-permute-done.9.refs_3_), channel_id=1, source_target_pairs={{0,1},{1,0},{2,3},{3,2},{4,5},{5,4},{6,7},{7,6},{8,9},{9,8},{10,11... | collective-permute-start | bytes 294920 | tf_op jit(solution)/shard_map/ppermute | solution.py:690
  50.2 0.5 collective-permute-done.7.refs_1_
  50.7 2.7 %collective-permute-start.8 = (f32[24,1024]{1,0:T(8,128)S(1)}, f32[24,1024]{1,0:T(8,128)S(1)}, u32[]{:S(2)}, u32[]{:S(2)}) collective-permute-start(f32[24,1024]{1,0:T(8,128)S(1)} %collective-permute-done.7.refs_1_), channel_id=1, source_target_pairs={{0,1},{1,0},{2,3},{3,2},{4,5},{5,4},{6,7},{7,6},{8,9},{9,8},{10,11... | collective-permute-start | bytes 294920 | tf_op jit(solution)/shard_map/ppermute | solution.py:690
  53.4 0.0 collective-permute-done.11.refs_2_
  53.4 0.0 collective-permute-start.12
  53.4 0.0 collective-permute-done.10.refs_4_
  53.5 0.9 %collective-permute-done.8.refs_2_ = f32[24,1024]{1,0:T(8,128)S(1)} collective-permute-done((f32[24,1024]{1,0:T(8,128)S(1)}, f32[24,1024]{1,0:T(8,128)S(1)}, u32[]{:S(2)}, u32[]{:S(2)}) %collective-permute-start.8) | collective-permute-done | bytes 98336 | tf_op jit(solution)/shard_map/ppermute | solution.py:690
  54.4 9.8 %coarse.1.refs_0_ = bf16[13,16,1152]{2,1,0:T(8,128)(2,1)S(1)} custom-call(s32[4]{0:T(128)S(1)} %pad_add_fusion.place_ref, f32[24,1024]{1,0:T(8,128)S(1)} %get-tuple-element.20.refs_0_, f32[24,1024]{1,0:T(8,128)S(1)} %collective-permute-done.7.refs_1_, f32[24,1024]{1,0:T(8,128)S(1)} %collective-permute-done.8.refs_2_, ...), custom_call_target="tpu_custom_call" | custom-call | flops 4000000000 | bytes 40000000 | tf_op jit(solution)/shard_map/coarse/pallas_call | solution.py:771
  64.2 0.0 collective-permute-done.12.refs_3_
  64.2 14.1 %after.1 = f32[3,8,8,128]{3,2,1,0:T(8,128)} custom-call(s32[4]{0:T(128)S(1)} %pad_add_fusion.place_ref, bf16[13,16,1152]{2,1,0:T(8,128)(2,1)S(1)} %coarse.1.refs_0_, f32[96,1024]{1,0:T(8,128)S(1)} %get-tuple-element.23.refs_1_, f32[96,1024]{1,0:T(8,128)S(1)} %collective-permute-done.11.refs_2_, f32[96,1024]{1,0:T(8,128)S(1)} %collective-permute-done.12.refs_3_, ...), custom_call_target="tpu_custom_call" | custom-call | tf_op jit(solution)/shard_map/after/pallas_call | solution.py:793
Async XLA Ops:
  1.6 1.7 %collective-permute-start = (f32[4,8,8,128]{3,2,1,0:T(8,128)S(1)}, f32[4,8,8,128]{3,2,1,0:T(8,128)S(1)}, u32[]{:S(2)}, u32[]{:S(2)}) collective-permute-start(f32[4,8,8,128]{3,2,1,0:T(8,128)S(1)} %pad_maximum_fusion.raw_sent), channel_id=1, source_target_pairs={{0,1},{1,0},{2,3},{3,2},{4,5},{5,4},{6,7},{7,6},{8,9},{9,8},{10,11... | collective-permute-start | bytes 393224 | tf_op jit(solution)/shard_map/ppermute | solution.py:690
  4.8 12.7 %collective-permute-start.1 = (f32[104,512]{1,0:T(8,128)S(1)}, f32[104,512]{1,0:T(8,128)S(1)}, u32[]{:S(2)}, u32[]{:S(2)}) collective-permute-start(f32[104,512]{1,0:T(8,128)S(1)} %get-tuple-element.16.refs_0_), channel_id=1, source_target_pairs={{0,2},{3,1},{2,4},{5,3},{4,6},{7,5},{6,8},{9,7},{8,10},{11,9},{10,... | collective-permute-start | bytes 638984 | tf_op jit(solution)/shard_map/ppermute | solution.py:699
  9.9 12.4 %collective-permute-start.2 = (f32[104,512]{1,0:T(8,128)S(1)}, f32[104,512]{1,0:T(8,128)S(1)}, u32[]{:S(2)}, u32[]{:S(2)}) collective-permute-start(f32[104,512]{1,0:T(8,128)S(1)} %get-tuple-element.16.refs_0_), channel_id=1, source_target_pairs={{0,130},{3,129},{2,132},{5,131},{4,134},{7,133},{6,136},{9,135},{8... | collective-permute-start | bytes 638984 | tf_op jit(solution)/shard_map/ppermute | solution.py:699
  13.7 9.8 %collective-permute-start.5 = (f32[56,512]{1,0:T(8,128)S(1)}, f32[56,512]{1,0:T(8,128)S(1)}, u32[]{:S(2)}, u32[]{:S(2)}) collective-permute-start(f32[56,512]{1,0:T(8,128)S(1)} %get-tuple-element.19), channel_id=1, source_target_pairs={{0,128},{128,0},{1,129},{129,1},{2,130},{130,2},{3,131},{131,3},{4... | collective-permute-start | bytes 344072 | tf_op jit(solution)/shard_map/ppermute | solution.py:690
  14.4 1.0 %copy-start = (bf16[624,256]{1,0:T(8,128)(2,1)S(1)}, bf16[624,256]{1,0:T(8,128)(2,1)}, u32[]{:S(2)}) copy-start(bf16[624,256]{1,0:T(8,128)(2,1)} %constant.18.clone.cards_ref) | copy-start | bytes 958468
  15.4 0.8 %copy-start.1 = (f32[81,81]{1,0:T(8,128)S(1)}, f32[81,81]{1,0:T(8,128)}, u32[]{:S(2)}) copy-start(f32[81,81]{1,0:T(8,128)} %fine_ref.1) | copy-start | bytes 78736
  16.1 0.7 copy-start.2
  22.3 2.7 %collective-permute-start.4 = (f32[104,512]{1,0:T(8,128)S(1)}, f32[104,512]{1,0:T(8,128)S(1)}, u32[]{:S(2)}, u32[]{:S(2)}) collective-permute-start(f32[104,512]{1,0:T(8,128)S(1)} %collective-permute-done.2.refs_2_), channel_id=1, source_target_pairs={{0,1},{1,0},{2,3},{3,2},{4,5},{5,4},{6,7},{7,6},{8,9},{9,8},{10,11... | collective-permute-start | bytes 638984 | tf_op jit(solution)/shard_map/ppermute | solution.py:690
  23.4 1.6 %collective-permute-start.3 = (f32[104,512]{1,0:T(8,128)S(1)}, f32[104,512]{1,0:T(8,128)S(1)}, u32[]{:S(2)}, u32[]{:S(2)}) collective-permute-start(f32[104,512]{1,0:T(8,128)S(1)} %collective-permute-done.1.refs_1_), channel_id=1, source_target_pairs={{0,1},{1,0},{2,3},{3,2},{4,5},{5,4},{6,7},{7,6},{8,9},{9,8},{10,11... | collective-permute-start | bytes 638984 | tf_op jit(solution)/shard_map/ppermute | solution.py:690
  23.4 1.6 %collective-permute-start.6 = (f32[56,512]{1,0:T(8,128)S(1)}, f32[56,512]{1,0:T(8,128)S(1)}, u32[]{:S(2)}, u32[]{:S(2)}) collective-permute-start(f32[56,512]{1,0:T(8,128)S(1)} %collective-permute-done.5.refs_5_), channel_id=1, source_target_pairs={{0,1},{1,0},{2,3},{3,2},{4,5},{5,4},{6,7},{7,6},{8,9},{9,8},{10,11... | collective-permute-start | bytes 344072 | tf_op jit(solution)/shard_map/ppermute | solution.py:690
  37.0 16.4 %collective-permute-start.11 = (f32[96,1024]{1,0:T(8,128)S(1)}, f32[96,1024]{1,0:T(8,128)S(1)}, u32[]{:S(2)}, u32[]{:S(2)}) collective-permute-start(f32[96,1024]{1,0:T(8,128)S(1)} %get-tuple-element.23.refs_1_), channel_id=1, source_target_pairs={{0,2},{3,1},{2,4},{5,3},{4,6},{7,5},{6,8},{9,7},{8,10},{11,9},{10,... | collective-permute-start | bytes 1179656 | tf_op jit(solution)/shard_map/ppermute | solution.py:699
  39.2 5.8 %collective-permute-start.9 = (f32[24,1024]{1,0:T(8,128)S(1)}, f32[24,1024]{1,0:T(8,128)S(1)}, u32[]{:S(2)}, u32[]{:S(2)}) collective-permute-start(f32[24,1024]{1,0:T(8,128)S(1)} %get-tuple-element.20.refs_0_), channel_id=1, source_target_pairs={{0,4},{5,1},{2,6},{7,3},{4,8},{9,5},{6,10},{11,7},{8,12},{13,9},{1... | collective-permute-start | bytes 294920 | tf_op jit(solution)/shard_map/ppermute | solution.py:699
  41.1 9.6 %collective-permute-start.7 = (f32[24,1024]{1,0:T(8,128)S(1)}, f32[24,1024]{1,0:T(8,128)S(1)}, u32[]{:S(2)}, u32[]{:S(2)}) collective-permute-start(f32[24,1024]{1,0:T(8,128)S(1)} %get-tuple-element.20.refs_0_), channel_id=1, source_target_pairs={{0,2},{3,1},{2,4},{5,3},{4,6},{7,5},{6,8},{9,7},{8,10},{11,9},{10,... | collective-permute-start | bytes 294920 | tf_op jit(solution)/shard_map/ppermute | solution.py:699
  45.0 8.5 %collective-permute-start.10 = (f32[24,1024]{1,0:T(8,128)S(1)}, f32[24,1024]{1,0:T(8,128)S(1)}, u32[]{:S(2)}, u32[]{:S(2)}) collective-permute-start(f32[24,1024]{1,0:T(8,128)S(1)} %collective-permute-done.9.refs_3_), channel_id=1, source_target_pairs={{0,1},{1,0},{2,3},{3,2},{4,5},{5,4},{6,7},{7,6},{8,9},{9,8},{10,11... | collective-permute-start | bytes 294920 | tf_op jit(solution)/shard_map/ppermute | solution.py:690
  50.7 3.7 %collective-permute-start.8 = (f32[24,1024]{1,0:T(8,128)S(1)}, f32[24,1024]{1,0:T(8,128)S(1)}, u32[]{:S(2)}, u32[]{:S(2)}) collective-permute-start(f32[24,1024]{1,0:T(8,128)S(1)} %collective-permute-done.7.refs_1_), channel_id=1, source_target_pairs={{0,1},{1,0},{2,3},{3,2},{4,5},{5,4},{6,7},{7,6},{8,9},{9,8},{10,11... | collective-permute-start | bytes 294920 | tf_op jit(solution)/shard_map/ppermute | solution.py:690
  53.4 10.7 %collective-permute-start.12 = (f32[96,1024]{1,0:T(8,128)S(1)}, f32[96,1024]{1,0:T(8,128)S(1)}, u32[]{:S(2)}, u32[]{:S(2)}) collective-permute-start(f32[96,1024]{1,0:T(8,128)S(1)} %collective-permute-done.11.refs_2_), channel_id=1, source_target_pairs={{0,1},{1,0},{2,3},{3,2},{4,5},{5,4},{6,7},{7,6},{8,9},{9,8},{10,11... | collective-permute-start | bytes 1179656 | tf_op jit(solution)/shard_map/ppermute | solution.py:690

commit v3 on v2

--- a/solution.py
+++ b/solution.py
@@ -1,3 +1,5 @@
+from typing import NamedTuple
+
 import jax
 import jax.numpy as jnp
 import numpy as np
@@ -293,6 +295,17 @@
     return (values.reshape(rows // 8, 8, lanes) * moduli[None]).reshape(rows, lanes)
 
 
+class Step(NamedTuple):
+    row: int
+    keep: float = 0.0
+    gain: float = 0.0
+    last: bool = False
+    lead: bool = False
+    tail: bool = False
+    operand: bool = True
+    residual: bool = True
+
+
 def schedules():
     sigma = MID / HALF
     rhos = [1.0 / sigma]
@@ -300,37 +313,37 @@
         rhos.append(1.0 / (2.0 * sigma - rhos[-1]))
     smooth = [(rhos[s + 1] * rhos[s], 2.0 * rhos[s + 1] / HALF) for s in range(DEG - 1)]
     o, c = SIDE, FAR
+
+    def smoothing(sweeps, operand, residual):
+        steps = []
+        for at, (first, last, keep, gain) in enumerate(sweeps):
+            final = at == len(sweeps) - 1
+            reads = operand if final else range(sweeps[at + 1][0], sweeps[at + 1][1] + 1)
+            sums = residual if final else range(sweeps[at + 1][0] + 1, sweeps[at + 1][1])
+            for row in range(first, last):
+                steps.append(Step(row, keep, gain, final, row == first, row == last - 1, row in reads, row in sums))
+        return steps
+
     return {
-        "start": ([(0, ROWS, 0.0, 0.0, 0.0)], 3),
-        "before": ([(o - 3 + s, o + 7 - s, *smooth[s], 0.0) for s in range(DEG - 1)], 6),
-        "leave": ([(o, o + 4, 0.0, 0.0, 0.0)], 4),
-        "coarse_start": ([(c - 7, c + 11, 0.0, 0.0, 0.0)], 3),
-        "coarse": ([(c - 7 + s, c + 10 - s, *smooth[s], float(s == DEG - 2)) for s in range(DEG - 1)], 9),
-        "correct": ([(o - 4, o + 8, 0.0, 0.0, 0.0)], 3),
-        "after": (
-            [(o - 4, o + 7, 0.0, 1.0 / MID, 0.0)]
-            + [(o - 3 + s, o + 6 - s + (s == DEG - 2), *smooth[s], 0.0) for s in range(DEG - 1)],
-            3,
+        "start": [Step(row) for row in range(o - 3, o + 8)],
+        "before": smoothing(
+            [(o - 3 + s, o + 7 - s, *smooth[s]) for s in range(DEG - 1)], range(o, o + 5), range(o, o + 4)
+        ),
+        "leave": [Step(row) for row in range(o, o + 4)],
+        "coarse_start": [Step(row) for row in range(c - 7, c + 11)],
+        "coarse": smoothing(
+            [(c - 7 + s, c + 10 - s, *smooth[s]) for s in range(DEG - 1)], range(c - 4, c + 8), range(0)
+        ),
+        "correct": [Step(row) for row in range(o - 4, o + 8)],
+        "after": smoothing(
+            [(o - 4, o + 7, 0.0, 1.0 / MID)] + [(o - 3 + s, o + 6 - s, *smooth[s]) for s in range(DEG - 1)],
+            range(0),
+            range(0),
         ),
     }
 
 
-def row_at(name, t):
-    at, row = 0, None
-    for first, last, *_ in schedules()[name][0]:
-        here = t + (first - at)
-        row = here if row is None else jnp.where(t >= at, here, row)
-        at += last - first
-    return jnp.where(t >= at, SIDE, row).astype(jnp.int32)
-
-
-def factor_at(name, t, which):
-    at, factor = 0, None
-    for first, last, *factors in schedules()[name][0]:
-        here = jnp.float32(factors[which])
-        factor = here if factor is None else jnp.where(t >= at, here, factor)
-        at += last - first
-    return factor
+OWN_ROWS = range(SIDE, SIDE + OWN)
 
 
 CHUNKS = [(256 * n, slice(256 * n, 256 * n + 256)) for n in range(4)]
@@ -354,21 +367,12 @@
 
 
 def pipeline(prods, name, issue, finish):
-    sweeps, together = schedules()[name]
-    count = sum(last - first for first, last, *_ in sweeps)
-    assert count % together == 0
-    assert together % (AHEAD + 1) == 0 or count == together
-    for u in range(AHEAD):
-        issue(row_at(name, jnp.int32(u)), prods[u])
-
-    def some(i, _):
-        t = together * i
-        for u in range(together):
-            issue(row_at(name, t + u + AHEAD), prods[(u + AHEAD) % len(prods)])
-            finish(t + u, row_at(name, t + u), prods[u % len(prods)])
-        return 0
-
-    lax.fori_loop(0, count // together, some, 0)
+    steps = schedules()[name]
+    for t in range(len(steps) + AHEAD):
+        if t < len(steps):
+            issue(steps[t].row, prods[t % len(prods)])
+        if t >= AHEAD:
+            finish(steps[t - AHEAD], prods[(t - AHEAD) % len(prods)])
 
 
 def fine_issue(fine_w, fine_x):
@@ -392,52 +396,66 @@
 
 
 def fine_finish(moduli, carry, use):
-    def finish(t, y, prod):
+    def finish(now, prod):
+        y = now.row
         before = [(jnp.zeros((16, 128), F32), jnp.zeros((8, 128), F32))] * 2
         for low, lanes in CHUNKS:
             m = moduli[y, :, lanes]
             sums = []
             for z in range(2):
                 v = scaled(prod[64 * z : 64 * z + 64, lanes], m)
-                old = carry[16 * z : 16 * z + 16, lanes]
-                along_x = pushed(before[z][0], v[24:40])
-                along_xy = pushed(before[z][1], v[56:64])
+                if not now.lead:
+                    old = carry[16 * z : 16 * z + 16, lanes]
+                    along_x = pushed(before[z][0], v[24:40])
+                    sums.append(
+                        jnp.concatenate(
+                            [v[0:8] + along_x[0:8] + old[0:8], v[8:16] + old[8:16], v[16:24] + along_x[8:16]], axis=0
+                        )
+                    )
+                if not now.tail:
+                    along_xy = pushed(before[z][1], v[56:64])
+                    carry[16 * z : 16 * z + 16, lanes] = jnp.concatenate([v[40:48] + along_xy, v[48:56]], axis=0)
                 before[z] = (v[24:40, 128:], v[56:64, 128:])
-                sums.append(
-                    jnp.concatenate(
-                        [v[0:8] + along_x[0:8] + old[0:8], v[8:16] + old[8:16], v[16:24] + along_x[8:16]], axis=0
-                    )
-                )
-                carry[16 * z : 16 * z + 16, lanes] = jnp.concatenate([v[40:48] + along_xy, v[48:56]], axis=0)
-            use(t, y, lanes, sums[0] + roll_tiles(sums[1], -1))
+            if not now.lead:
+                use(now, y, lanes, sums[0] + roll_tiles(sums[1], -1))
 
     return finish
 
 
 def coarse_finish(moduli, carry, use):
-    def finish(t, y, prod):
+    def finish(now, prod):
+        y = now.row
         before = (jnp.zeros((8, 128), F32), jnp.zeros((8, 128), F32))
         for low, lanes in CHUNKS:
             v = prod[0:32, lanes]
             if moduli is not None:
                 v = scaled(v, moduli[y, :, lanes])
-            sums = v[0:8] + pushed(before[0], v[8:16]) + carry[:, lanes]
-            carry[:, lanes] = v[16:24] + pushed(before[1], v[24:32])
+            if not now.lead:
+                sums = v[0:8] + pushed(before[0], v[8:16]) + carry[:, lanes]
+            if not now.tail:
+                carry[:, lanes] = v[16:24] + pushed(before[1], v[24:32])
             before = (v[8:16, 128:], v[24:32, 128:])
-            use(t, y, lanes, sums + roll_tiles(pltpu.roll(sums, 5, 0), -1))
+            if not now.lead:
+                use(now, y, lanes, sums + roll_tiles(pltpu.roll(sums, 5, 0), -1))
 
     return finish
 
 
-def smooth_fine(name, inverse, res, step, total, fine_x):
-    def use(t, y, lanes, sums):
-        keep, gain = factor_at(name, t, 0), factor_at(name, t, 1)
+def smooth_fine(inverse, res, step, total, fine_x):
+    def use(now, y, lanes, sums):
+        if not (now.operand or now.residual or y in OWN_ROWS):
+            return
         r = res[y, :, lanes] - sums
-        d = keep * step[y, :, lanes] + gain * (inverse[y, :, lanes] * r)
-        res[y, :, lanes] = r
-        step[y, :, lanes] = d
-        total[y, :, lanes] = total[y, :, lanes] + d
-        store_fine(fine_x, y, lanes, d)
+        d = now.gain * (inverse[y, :, lanes] * r)
+        if now.keep:
+            d = now.keep * step[y, :, lanes] + d
+        if now.residual:
+            res[y, :, lanes] = r
+            step[y, :, lanes] = d
+        if y in OWN_ROWS:
+            total[y, :, lanes] = total[y, :, lanes] + d
+        if now.operand:
+            store_fine(fine_x, y, lanes, d)
 
     return use
 
@@ -447,7 +465,7 @@
         spot = lax.broadcasted_iota(jnp.int32, (8, 256), 0)
         before = jnp.zeros((8, 128), F32)
         for low, lanes in CHUNKS:
-            near = jnp.where(spot < 4, moduli[y, :, lanes], moduli[jnp.maximum(y - 1, 0), :, lanes])
+            near = jnp.where(spot < 4, moduli[y, :, lanes], moduli[max(y - 1, 0), :, lanes])
             moved = pushed(before, near)
             before = near[:, 128:]
             around = jnp.where(spot % 4 < 2, near, moved)
@@ -508,7 +526,8 @@
             moduli[o + OWN * offset + y, :, lanes_of[across]] = jnp.broadcast_to(rows[y : y + 1], (8, 512))
     leaving = fetched([(load, outs[0]), (moduli, outs[1])], out_sems)
 
-    def start(t, y, prod):
+    def start(now, prod):
+        y = now.row
         ok = valid(y)
         for low, lanes in CHUNKS:
             inv = ok / (prod[0:24, lanes] + (1.0 - ok))
@@ -517,13 +536,14 @@
             inverse[y, :, lanes] = inv
             res[y, :, lanes] = r
             step[y, :, lanes] = d
-            total[y, :, lanes] = d
+            if y in OWN_ROWS:
+                total[y, :, lanes] = d
             store_fine(fine_x, y, lanes, d)
 
     pipeline(prods, "start", diag_issue(diag_w, moduli, 24), start)
     leaving += fetched([(inverse, outs[2])], out_sems, len(leaving))
     issue = fine_issue(fine_w, fine_x)
-    use = smooth_fine("before", inverse, res, step, total, fine_x)
+    use = smooth_fine(inverse, res, step, total, fine_x)
     pipeline(prods, "before", issue, fine_finish(moduli, carry, use))
     rows = [(total.at[o + y], outs[3].at[24 * y : 24 * y + 24, :]) for y in range(OWN)]
     leaving += fetched(rows, out_sems, len(leaving))
@@ -534,7 +554,7 @@
         for g in range(3):
             fine_x[y, 16 * g : 16 * g + 16, lanes] = split(left[8 * g : 8 * g + 8])
 
-    def leave(t, y, lanes, sums):
+    def leave(now, y, lanes, sums):
         store_left(y, lanes, res[y, :, lanes] - sums)
 
     pipeline(prods, "leave", issue, fine_finish(moduli, carry, leave))
@@ -549,10 +569,10 @@
         for low, lanes in CHUNKS:
             prod[0:32, lanes] = jnp.dot(restrict_w[...], fine_x[o + j, 0:48, lanes], preferred_element_type=F32)
 
-        def keep(t, y, lanes, sums, j=j):
+        def keep(now, y, lanes, sums, j=j):
             note[3 * j : 3 * j + 3, lanes] = sums[0:3]
 
-        coarse_finish(None, c_carry, keep)(0, o + j, prod)
+        coarse_finish(None, c_carry, keep)(Step(o + j), prod)
     for y in range(OWN):
         note[16 + y : 17 + y, :] = moduli[o + y, 0:1, :]
     leaving += fetched([(note, outs[4])], out_sems, len(leaving))
@@ -592,7 +612,8 @@
         for y in range(OWN + 1):
             c_res[at + y, 0:3, :] = c_res[at + y, 0:3, :] + notes[i, 3 * y : 3 * y + 3, :]
 
-    def start(t, y, prod):
+    def start(now, prod):
+        y = now.row
         ok = valid(y)
         for low, lanes in CHUNKS:
             used = lax.broadcasted_iota(jnp.int32, (8, 256), 0) < 3
@@ -610,15 +631,17 @@
             products = jnp.dot(coarse_w[...], coarse_operand(coarse_x, y, low, lanes), preferred_element_type=F32)
             prod[0:32, lanes] = products[:32] + products[32:]
 
-    def smooth(t, y, lanes, sums):
-        keep, gain, last = [factor_at("coarse", t, which) for which in range(3)]
+    def smooth(now, y, lanes, sums):
+        if not (now.operand or now.residual):
+            return
         r = c_res[y, :, lanes] - sums
-        d = keep * c_step[y, :, lanes] + gain * (c_inverse[y, :, lanes] * r)
-        so_far = c_total[y, :, lanes]
-        c_res[y, :, lanes] = r
-        c_step[y, :, lanes] = d
-        c_total[y, :, lanes] = so_far + d
-        store_coarse(coarse_x, y, lanes, d + last * so_far)
+        d = now.keep * c_step[y, :, lanes] + now.gain * (c_inverse[y, :, lanes] * r)
+        so_far = c_total[y, :, lanes] + d
+        if now.residual:
+            c_res[y, :, lanes] = r
+            c_step[y, :, lanes] = d
+            c_total[y, :, lanes] = so_far
+        store_coarse(coarse_x, y, lanes, so_far if now.last else d)
 
     pipeline(prods, "coarse", issue, coarse_finish(moduli, c_carry, smooth))
     wait_for(fetched([(coarse_x.at[c - o : c - o + ROWS + 1], fix)], sems))
@@ -626,13 +649,13 @@
 
 def after_kernel(place_ref, *refs):
     fix_sent, s0, s1, zs1, load_sent, moduli_sent, inverse_sent, book_ref, out_ref = refs[:9]
-    (book, res, step, total, fine_x, carry, load, moduli, inverse, fix, sems, *prods) = refs[9:]
+    (book, res, step, total, fine_x, carry, moduli, inverse, fix, sems, *prods) = refs[9:]
     gx, gz = place_ref[0], place_ref[2]
     o = SIDE
     side = 1 - 2 * gz
 
     fine_w, prolong_w, shuffle = [Part(book, BOOKS[2][0], name) for name in BOOKS[2][0]]
-    copies = [(fix_sent, fix), (load_sent, load), (book_ref, book)]
+    copies = [(fix_sent, fix), (load_sent, res), (book_ref, book)]
     for ref, offset in [(s0, 0), (s1, -side), (zs1, side)]:
         for y in range(OWN):
             copies.append((ref.at[24 * y : 24 * y + 24, :], total.at[o + OWN * offset + y]))
@@ -648,17 +671,17 @@
                 prolong_w[...], coarse_operand(fix, y, low, lanes), preferred_element_type=F32
             )
 
-    def correct(t, y, prod):
+    def correct(now, prod):
+        y = now.row
         for low, lanes in CHUNKS:
             corrected = total[y, :, lanes] + prod[0:24, lanes]
-            total[y, :, lanes] = corrected
-            res[y, :, lanes] = load[y, :, lanes]
-            step[y, :, lanes] = jnp.zeros((24, 256), F32)
+            if y in OWN_ROWS:
+                total[y, :, lanes] = corrected
             store_fine(fine_x, y, lanes, corrected)
 
     pipeline(prods, "correct", correct_issue, correct)
     wait_for(second)
-    use = smooth_fine("after", inverse, res, step, total, fine_x)
+    use = smooth_fine(inverse, res, step, total, fine_x)
     pipeline(prods, "after", fine_issue(fine_w, fine_x), fine_finish(moduli, carry, use))
 
     row = lax.broadcasted_iota(jnp.int32, (256, 128), 0)
@@ -739,7 +762,6 @@
         held(ROWS),
         pltpu.VMEM((ROWS + 1, 96, WIDE), BF16),
         pltpu.VMEM((32, LANES), F32),
-        held(ROWS),
     ]
     prods = [pltpu.VMEM((128, LANES), F32)] * (AHEAD + 1)
     limit = pltpu.CompilerParams(vmem_limit_bytes=24 * 1024 * 1024)
@@ -753,6 +775,7 @@
         out_specs=[there] * 5,
         scratch_shapes=[pltpu.VMEM(book.shape, BF16), *fine_scratch]
         + [
+            held(ROWS),
             held(ROWS, 8),
             held(ROWS),
             pltpu.VMEM((NOTE, LANES), F32),

time: 78.7 us -> 67.9 us (0.86)
  Pallas kernels: 38 us -> 27 us
    pallas_call x1, Pallas kernels: 9.77 us -> 4.92 us  [per_device(): pl.pallas_call(coarse_kernel, out_shape=jax.ShapeDtypeStruct((ROWS + 1, 1...]
    pallas_call x1, Pallas kernels: 14.1 us -> 10.3 us  [per_device(): pl.pallas_call(after_kernel, out_shape=jax.ShapeDtypeStruct(adjoint_load....]
    pallas_call x1, Pallas kernels: 12 us -> 9.77 us  [per_device(): pl.pallas_call(before_kernel, out_shape=[jax.ShapeDtypeStruct(shape, F32)...]
  transfers between devices with their start and end apart: 13 -> 13, of which waited for: 6 -> 6; matrix products, arithmetic and copies ran while one was open for 0% -> 0% of each run, Pallas kernels for 13% -> 8%
where the time goes in v3:
time: 67.9 us; the launch traced here: 67.5 us
  starting transfers between devices  27.1 us (40%)
  Pallas kernels  27 us (40%)
  waiting for transfers between devices  9.05 us (13%)
  local copies, waits for them, and re-layouts  2.46 us (4%)
  other arithmetic  1.68 us (2%)
    ppermute x5, starting transfers between devices, sided(): return lax.ppermute(value, ('gx', 'gy', 'gz'), pairs)  16 us
    ppermute x8, starting transfers between devices, swap(): return lax.ppermute(value, axis, [(0, 1), (1, 0)])  11 us
    pallas_call x1, Pallas kernels, per_device(): pl.pallas_call(after_kernel, out_shape=jax.ShapeDtypeStruct(adjoint_load....  10.3 us
    pallas_call x1, Pallas kernels, per_device(): pl.pallas_call(before_kernel, out_shape=[jax.ShapeDtypeStruct(shape, F32)...  9.77 us
    ppermute x5, waiting for transfers between devices, sided(): return lax.ppermute(value, ('gx', 'gy', 'gz'), pairs)  6.08 us
    pallas_call x1, Pallas kernels, per_device(): pl.pallas_call(coarse_kernel, out_shape=jax.ShapeDtypeStruct((ROWS + 1, 1...  4.92 us
    ppermute x8, waiting for transfers between devices, swap(): return lax.ppermute(value, axis, [(0, 1), (1, 0)])  2.97 us
    unnamed x6, local copies, waits for them, and re-layouts  2.46 us
  transfers between devices with their start and end apart: 13, of which 6 were waited for; matrix products, arithmetic and copies ran while one was open for 0% of the time, Pallas kernels for 8%

profile of v3, /device:TPU:129, one launch (start us, length us, event | category | flops | bytes accessed | tf_op | source)
XLA Modules:
  0.0 67.5 jit_solution(1439929564957028583)
XLA Ops:
  0.0 0.7 %convert_bitcast_fusion = f32[1,8,8,128]{3,2,1,0:T(8,128)S(1)} fusion(s32[4,4,64]{2,1,0:T(4,128)} %param.6), kind=kLoop, calls=%fused_computation.1 | loop fusion | flops 8192 | bytes 36864 | tf_op jit(solution)/shard_map/broadcast_in_dim | solution.py:750
  0.7 0.9 %pad_maximum_fusion.raw_sent = f32[4,8,8,128]{3,2,1,0:T(8,128)S(1)} fusion(f32[1,8,8,128]{3,2,1,0:T(8,128)S(1)} %convert_bitcast_fusion, f32[3,8,8,128]{3,2,1,0:T(8,128)} %param.5), kind=kLoop, calls=%fused_computation | loop fusion | flops 32768 | bytes 262144 | tf_op jit(solution)/shard_map/concatenate | solution.py:750
  1.6 0.8 %collective-permute-start = (f32[4,8,8,128]{3,2,1,0:T(8,128)S(1)}, f32[4,8,8,128]{3,2,1,0:T(8,128)S(1)}, u32[]{:S(2)}, u32[]{:S(2)}) collective-permute-start(f32[4,8,8,128]{3,2,1,0:T(8,128)S(1)} %pad_maximum_fusion.raw_sent), channel_id=1, source_target_pairs={{0,1},{1,0},{2,3},{3,2},{4,5},{5,4},{6,7},{7,6},{8,9},{9,8},{10,11... | collective-permute-start | bytes 393224 | tf_op jit(solution)/shard_map/ppermute | solution.py:713
  2.4 0.1 pad_add_fusion.place_ref
  2.4 0.9 %collective-permute-done.other_sent = f32[4,8,8,128]{3,2,1,0:T(8,128)S(1)} collective-permute-done((f32[4,8,8,128]{3,2,1,0:T(8,128)S(1)}, f32[4,8,8,128]{3,2,1,0:T(8,128)S(1)}, u32[]{:S(2)}, u32[]{:S(2)}) %collective-permute-start) | collective-permute-done | bytes 131104 | tf_op jit(solution)/shard_map/ppermute | solution.py:713
  3.4 1.4 %pack.1 = (f32[104,512]{1,0:T(8,128)S(1)}, f32[56,512]{1,0:T(8,128)S(1)}) custom-call(s32[4]{0:T(128)S(1)} %pad_add_fusion.place_ref, f32[4,8,8,128]{3,2,1,0:T(8,128)S(1)} %pad_maximum_fusion.raw_sent, f32[4,8,8,128]{3,2,1,0:T(8,128)S(1)} %collective-permute-done.other_sent), custom_call_target="tpu_custom_call" | custom-call | tf_op jit(solution)/shard_map/pack/pallas_call | solution.py:729
  4.8 5.1 %collective-permute-start.1 = (f32[104,512]{1,0:T(8,128)S(1)}, f32[104,512]{1,0:T(8,128)S(1)}, u32[]{:S(2)}, u32[]{:S(2)}) collective-permute-start(f32[104,512]{1,0:T(8,128)S(1)} %get-tuple-element.16.refs_0_), channel_id=1, source_target_pairs={{0,2},{3,1},{2,4},{5,3},{4,6},{7,5},{6,8},{9,7},{8,10},{11,9},{10,... | collective-permute-start | bytes 638984 | tf_op jit(solution)/shard_map/ppermute | solution.py:722
  9.9 3.7 %collective-permute-start.2 = (f32[104,512]{1,0:T(8,128)S(1)}, f32[104,512]{1,0:T(8,128)S(1)}, u32[]{:S(2)}, u32[]{:S(2)}) collective-permute-start(f32[104,512]{1,0:T(8,128)S(1)} %get-tuple-element.16.refs_0_), channel_id=1, source_target_pairs={{0,130},{3,129},{2,132},{5,131},{4,134},{7,133},{6,136},{9,135},{8... | collective-permute-start | bytes 638984 | tf_op jit(solution)/shard_map/ppermute | solution.py:722
  13.7 0.7 %collective-permute-start.5 = (f32[56,512]{1,0:T(8,128)S(1)}, f32[56,512]{1,0:T(8,128)S(1)}, u32[]{:S(2)}, u32[]{:S(2)}) collective-permute-start(f32[56,512]{1,0:T(8,128)S(1)} %get-tuple-element.19), channel_id=1, source_target_pairs={{0,128},{128,0},{1,129},{129,1},{2,130},{130,2},{3,131},{131,3},{4... | collective-permute-start | bytes 344072 | tf_op jit(solution)/shard_map/ppermute | solution.py:713
  14.4 0.0 copy-start
  14.4 1.0 %copy-done = bf16[624,256]{1,0:T(8,128)(2,1)S(1)} copy-done((bf16[624,256]{1,0:T(8,128)(2,1)S(1)}, bf16[624,256]{1,0:T(8,128)(2,1)}, u32[]{:S(2)}) %copy-start) | copy-done | bytes 319512
  15.4 0.0 copy-start.1
  15.4 0.8 %copy-done.1 = f32[81,81]{1,0:T(8,128)S(1)} copy-done((f32[81,81]{1,0:T(8,128)S(1)}, f32[81,81]{1,0:T(8,128)}, u32[]{:S(2)}) %copy-start.1) | copy-done | bytes 26268
  16.1 0.0 copy-start.2
  16.1 0.7 %copy-done.2 = f32[24,24]{1,0:T(8,128)S(1)} copy-done((f32[24,24]{1,0:T(8,128)S(1)}, f32[24,24]{1,0:T(8,128)}, u32[]{:S(2)}) %copy-start.2) | copy-done | bytes 2328
  16.9 0.6 weights.1
  17.5 0.0 collective-permute-done.1.refs_1_
  17.5 4.8 %collective-permute-done.2.refs_2_ = f32[104,512]{1,0:T(8,128)S(1)} collective-permute-done((f32[104,512]{1,0:T(8,128)S(1)}, f32[104,512]{1,0:T(8,128)S(1)}, u32[]{:S(2)}, u32[]{:S(2)}) %collective-permute-start.2) | collective-permute-done | bytes 213024 | tf_op jit(solution)/shard_map/ppermute | solution.py:722
  22.3 1.1 %collective-permute-start.4 = (f32[104,512]{1,0:T(8,128)S(1)}, f32[104,512]{1,0:T(8,128)S(1)}, u32[]{:S(2)}, u32[]{:S(2)}) collective-permute-start(f32[104,512]{1,0:T(8,128)S(1)} %collective-permute-done.2.refs_2_), channel_id=1, source_target_pairs={{0,1},{1,0},{2,3},{3,2},{4,5},{5,4},{6,7},{7,6},{8,9},{9,8},{10,11... | collective-permute-start | bytes 638984 | tf_op jit(solution)/shard_map/ppermute | solution.py:713
  23.4 0.0 collective-permute-start.3
  23.4 0.0 collective-permute-done.5.refs_5_
  23.4 0.5 collective-permute-start.6
  23.9 1.1 %collective-permute-done.6.refs_6_ = f32[56,512]{1,0:T(8,128)S(1)} collective-permute-done((f32[56,512]{1,0:T(8,128)S(1)}, f32[56,512]{1,0:T(8,128)S(1)}, u32[]{:S(2)}, u32[]{:S(2)}) %collective-permute-start.6) | collective-permute-done | bytes 114720 | tf_op jit(solution)/shard_map/ppermute | solution.py:713
  25.0 0.0 collective-permute-done.4.refs_4_
  25.0 0.0 collective-permute-done.3.refs_3_
  25.0 9.8 %before.1 = (f32[12,24,1024]{2,1,0:T(8,128)S(1)}, f32[12,8,1024]{2,1,0:T(8,128)S(1)}, f32[12,24,1024]{2,1,0:T(8,128)S(1)}, f32[96,1024]{1,0:T(8,128)S(1)}, f32[24,1024]{1,0:T(8,128)S(1)}) custom-call(s32[4]{0:T(128)S(1)} %pad_add_fusion.place_ref, f32[104,512]{1,0:T(8,128)S(1)} %get-tuple-element.16.refs_0_, f32[104,512]{1,0:T(8,128)S(1)} %collective-permute-done.1.refs_1_, ...), custom_call_target="tpu_custom_call" | custom-call | tf_op jit(solution)/shard_map/before/pallas_call | solution.py:768
  34.8 2.1 %collective-permute-start.11 = (f32[96,1024]{1,0:T(8,128)S(1)}, f32[96,1024]{1,0:T(8,128)S(1)}, u32[]{:S(2)}, u32[]{:S(2)}) collective-permute-start(f32[96,1024]{1,0:T(8,128)S(1)} %get-tuple-element.23.refs_1_), channel_id=1, source_target_pairs={{0,2},{3,1},{2,4},{5,3},{4,6},{7,5},{6,8},{9,7},{8,10},{11,9},{10,... | collective-permute-start | bytes 1179656 | tf_op jit(solution)/shard_map/ppermute | solution.py:722
  37.0 1.9 %collective-permute-start.9 = (f32[24,1024]{1,0:T(8,128)S(1)}, f32[24,1024]{1,0:T(8,128)S(1)}, u32[]{:S(2)}, u32[]{:S(2)}) collective-permute-start(f32[24,1024]{1,0:T(8,128)S(1)} %get-tuple-element.20.refs_0_), channel_id=1, source_target_pairs={{0,4},{5,1},{2,6},{7,3},{4,8},{9,5},{6,10},{11,7},{8,12},{13,9},{1... | collective-permute-start | bytes 294920 | tf_op jit(solution)/shard_map/ppermute | solution.py:722
  38.9 3.1 %collective-permute-start.7 = (f32[24,1024]{1,0:T(8,128)S(1)}, f32[24,1024]{1,0:T(8,128)S(1)}, u32[]{:S(2)}, u32[]{:S(2)}) collective-permute-start(f32[24,1024]{1,0:T(8,128)S(1)} %get-tuple-element.20.refs_0_), channel_id=1, source_target_pairs={{0,2},{3,1},{2,4},{5,3},{4,6},{7,5},{6,8},{9,7},{8,10},{11,9},{10,... | collective-permute-start | bytes 294920 | tf_op jit(solution)/shard_map/ppermute | solution.py:722
  42.0 0.7 %collective-permute-done.9.refs_3_ = f32[24,1024]{1,0:T(8,128)S(1)} collective-permute-done((f32[24,1024]{1,0:T(8,128)S(1)}, f32[24,1024]{1,0:T(8,128)S(1)}, u32[]{:S(2)}, u32[]{:S(2)}) %collective-permute-start.9) | collective-permute-done | bytes 98336 | tf_op jit(solution)/shard_map/ppermute | solution.py:722
  42.8 5.2 %collective-permute-start.10 = (f32[24,1024]{1,0:T(8,128)S(1)}, f32[24,1024]{1,0:T(8,128)S(1)}, u32[]{:S(2)}, u32[]{:S(2)}) collective-permute-start(f32[24,1024]{1,0:T(8,128)S(1)} %collective-permute-done.9.refs_3_), channel_id=1, source_target_pairs={{0,1},{1,0},{2,3},{3,2},{4,5},{5,4},{6,7},{7,6},{8,9},{9,8},{10,11... | collective-permute-start | bytes 294920 | tf_op jit(solution)/shard_map/ppermute | solution.py:713
  48.0 0.5 collective-permute-done.7.refs_1_
  48.5 2.7 %collective-permute-start.8 = (f32[24,1024]{1,0:T(8,128)S(1)}, f32[24,1024]{1,0:T(8,128)S(1)}, u32[]{:S(2)}, u32[]{:S(2)}) collective-permute-start(f32[24,1024]{1,0:T(8,128)S(1)} %collective-permute-done.7.refs_1_), channel_id=1, source_target_pairs={{0,1},{1,0},{2,3},{3,2},{4,5},{5,4},{6,7},{7,6},{8,9},{9,8},{10,11... | collective-permute-start | bytes 294920 | tf_op jit(solution)/shard_map/ppermute | solution.py:713
  51.2 0.0 collective-permute-done.11.refs_2_
  51.2 0.0 collective-permute-start.12
  51.2 0.0 collective-permute-done.10.refs_4_
  51.2 0.9 %collective-permute-done.8.refs_2_ = f32[24,1024]{1,0:T(8,128)S(1)} collective-permute-done((f32[24,1024]{1,0:T(8,128)S(1)}, f32[24,1024]{1,0:T(8,128)S(1)}, u32[]{:S(2)}, u32[]{:S(2)}) %collective-permute-start.8) | collective-permute-done | bytes 98336 | tf_op jit(solution)/shard_map/ppermute | solution.py:713
  52.2 4.9 %coarse.1.refs_0_ = bf16[13,16,1152]{2,1,0:T(8,128)(2,1)S(1)} custom-call(s32[4]{0:T(128)S(1)} %pad_add_fusion.place_ref, f32[24,1024]{1,0:T(8,128)S(1)} %get-tuple-element.20.refs_0_, f32[24,1024]{1,0:T(8,128)S(1)} %collective-permute-done.7.refs_1_, f32[24,1024]{1,0:T(8,128)S(1)} %collective-permute-done.8.refs_2_, ...), custom_call_target="tpu_custom_call" | custom-call | flops 4000000000 | bytes 40000000 | tf_op jit(solution)/shard_map/coarse/pallas_call | solution.py:794
  57.1 0.0 collective-permute-done.12.refs_3_
  57.1 10.3 %after.1 = f32[3,8,8,128]{3,2,1,0:T(8,128)} custom-call(s32[4]{0:T(128)S(1)} %pad_add_fusion.place_ref, bf16[13,16,1152]{2,1,0:T(8,128)(2,1)S(1)} %coarse.1.refs_0_, f32[96,1024]{1,0:T(8,128)S(1)} %get-tuple-element.23.refs_1_, f32[96,1024]{1,0:T(8,128)S(1)} %collective-permute-done.11.refs_2_, f32[96,1024]{1,0:T(8,128)S(1)} %collective-permute-done.12.refs_3_, ...), custom_call_target="tpu_custom_call" | custom-call | tf_op jit(solution)/shard_map/after/pallas_call | solution.py:816
Async XLA Ops:
  1.6 1.7 %collective-permute-start = (f32[4,8,8,128]{3,2,1,0:T(8,128)S(1)}, f32[4,8,8,128]{3,2,1,0:T(8,128)S(1)}, u32[]{:S(2)}, u32[]{:S(2)}) collective-permute-start(f32[4,8,8,128]{3,2,1,0:T(8,128)S(1)} %pad_maximum_fusion.raw_sent), channel_id=1, source_target_pairs={{0,1},{1,0},{2,3},{3,2},{4,5},{5,4},{6,7},{7,6},{8,9},{9,8},{10,11... | collective-permute-start | bytes 393224 | tf_op jit(solution)/shard_map/ppermute | solution.py:713
  4.8 12.7 %collective-permute-start.1 = (f32[104,512]{1,0:T(8,128)S(1)}, f32[104,512]{1,0:T(8,128)S(1)}, u32[]{:S(2)}, u32[]{:S(2)}) collective-permute-start(f32[104,512]{1,0:T(8,128)S(1)} %get-tuple-element.16.refs_0_), channel_id=1, source_target_pairs={{0,2},{3,1},{2,4},{5,3},{4,6},{7,5},{6,8},{9,7},{8,10},{11,9},{10,... | collective-permute-start | bytes 638984 | tf_op jit(solution)/shard_map/ppermute | solution.py:722
  9.9 12.4 %collective-permute-start.2 = (f32[104,512]{1,0:T(8,128)S(1)}, f32[104,512]{1,0:T(8,128)S(1)}, u32[]{:S(2)}, u32[]{:S(2)}) collective-permute-start(f32[104,512]{1,0:T(8,128)S(1)} %get-tuple-element.16.refs_0_), channel_id=1, source_target_pairs={{0,130},{3,129},{2,132},{5,131},{4,134},{7,133},{6,136},{9,135},{8... | collective-permute-start | bytes 638984 | tf_op jit(solution)/shard_map/ppermute | solution.py:722
  13.7 9.8 %collective-permute-start.5 = (f32[56,512]{1,0:T(8,128)S(1)}, f32[56,512]{1,0:T(8,128)S(1)}, u32[]{:S(2)}, u32[]{:S(2)}) collective-permute-start(f32[56,512]{1,0:T(8,128)S(1)} %get-tuple-element.19), channel_id=1, source_target_pairs={{0,128},{128,0},{1,129},{129,1},{2,130},{130,2},{3,131},{131,3},{4... | collective-permute-start | bytes 344072 | tf_op jit(solution)/shard_map/ppermute | solution.py:713
  14.4 1.0 %copy-start = (bf16[624,256]{1,0:T(8,128)(2,1)S(1)}, bf16[624,256]{1,0:T(8,128)(2,1)}, u32[]{:S(2)}) copy-start(bf16[624,256]{1,0:T(8,128)(2,1)} %constant.18.clone.cards_ref) | copy-start | bytes 958468
  15.4 0.8 %copy-start.1 = (f32[81,81]{1,0:T(8,128)S(1)}, f32[81,81]{1,0:T(8,128)}, u32[]{:S(2)}) copy-start(f32[81,81]{1,0:T(8,128)} %fine_ref.1) | copy-start | bytes 78736
  16.1 0.7 %copy-start.2 = (f32[24,24]{1,0:T(8,128)S(1)}, f32[24,24]{1,0:T(8,128)}, u32[]{:S(2)}) copy-start(f32[24,24]{1,0:T(8,128)} %coarse_ref.1) | copy-start | bytes 6916
  22.3 2.7 %collective-permute-start.4 = (f32[104,512]{1,0:T(8,128)S(1)}, f32[104,512]{1,0:T(8,128)S(1)}, u32[]{:S(2)}, u32[]{:S(2)}) collective-permute-start(f32[104,512]{1,0:T(8,128)S(1)} %collective-permute-done.2.refs_2_), channel_id=1, source_target_pairs={{0,1},{1,0},{2,3},{3,2},{4,5},{5,4},{6,7},{7,6},{8,9},{9,8},{10,11... | collective-permute-start | bytes 638984 | tf_op jit(solution)/shard_map/ppermute | solution.py:713
  23.4 1.6 %collective-permute-start.3 = (f32[104,512]{1,0:T(8,128)S(1)}, f32[104,512]{1,0:T(8,128)S(1)}, u32[]{:S(2)}, u32[]{:S(2)}) collective-permute-start(f32[104,512]{1,0:T(8,128)S(1)} %collective-permute-done.1.refs_1_), channel_id=1, source_target_pairs={{0,1},{1,0},{2,3},{3,2},{4,5},{5,4},{6,7},{7,6},{8,9},{9,8},{10,11... | collective-permute-start | bytes 638984 | tf_op jit(solution)/shard_map/ppermute | solution.py:713
  23.4 1.6 %collective-permute-start.6 = (f32[56,512]{1,0:T(8,128)S(1)}, f32[56,512]{1,0:T(8,128)S(1)}, u32[]{:S(2)}, u32[]{:S(2)}) collective-permute-start(f32[56,512]{1,0:T(8,128)S(1)} %collective-permute-done.5.refs_5_), channel_id=1, source_target_pairs={{0,1},{1,0},{2,3},{3,2},{4,5},{5,4},{6,7},{7,6},{8,9},{9,8},{10,11... | collective-permute-start | bytes 344072 | tf_op jit(solution)/shard_map/ppermute | solution.py:713
  34.8 16.4 %collective-permute-start.11 = (f32[96,1024]{1,0:T(8,128)S(1)}, f32[96,1024]{1,0:T(8,128)S(1)}, u32[]{:S(2)}, u32[]{:S(2)}) collective-permute-start(f32[96,1024]{1,0:T(8,128)S(1)} %get-tuple-element.23.refs_1_), channel_id=1, source_target_pairs={{0,2},{3,1},{2,4},{5,3},{4,6},{7,5},{6,8},{9,7},{8,10},{11,9},{10,... | collective-permute-start | bytes 1179656 | tf_op jit(solution)/shard_map/ppermute | solution.py:722
  37.0 5.8 %collective-permute-start.9 = (f32[24,1024]{1,0:T(8,128)S(1)}, f32[24,1024]{1,0:T(8,128)S(1)}, u32[]{:S(2)}, u32[]{:S(2)}) collective-permute-start(f32[24,1024]{1,0:T(8,128)S(1)} %get-tuple-element.20.refs_0_), channel_id=1, source_target_pairs={{0,4},{5,1},{2,6},{7,3},{4,8},{9,5},{6,10},{11,7},{8,12},{13,9},{1... | collective-permute-start | bytes 294920 | tf_op jit(solution)/shard_map/ppermute | solution.py:722
  38.9 9.6 %collective-permute-start.7 = (f32[24,1024]{1,0:T(8,128)S(1)}, f32[24,1024]{1,0:T(8,128)S(1)}, u32[]{:S(2)}, u32[]{:S(2)}) collective-permute-start(f32[24,1024]{1,0:T(8,128)S(1)} %get-tuple-element.20.refs_0_), channel_id=1, source_target_pairs={{0,2},{3,1},{2,4},{5,3},{4,6},{7,5},{6,8},{9,7},{8,10},{11,9},{10,... | collective-permute-start | bytes 294920 | tf_op jit(solution)/shard_map/ppermute | solution.py:722
  42.8 8.5 %collective-permute-start.10 = (f32[24,1024]{1,0:T(8,128)S(1)}, f32[24,1024]{1,0:T(8,128)S(1)}, u32[]{:S(2)}, u32[]{:S(2)}) collective-permute-start(f32[24,1024]{1,0:T(8,128)S(1)} %collective-permute-done.9.refs_3_), channel_id=1, source_target_pairs={{0,1},{1,0},{2,3},{3,2},{4,5},{5,4},{6,7},{7,6},{8,9},{9,8},{10,11... | collective-permute-start | bytes 294920 | tf_op jit(solution)/shard_map/ppermute | solution.py:713
  48.5 3.7 %collective-permute-start.8 = (f32[24,1024]{1,0:T(8,128)S(1)}, f32[24,1024]{1,0:T(8,128)S(1)}, u32[]{:S(2)}, u32[]{:S(2)}) collective-permute-start(f32[24,1024]{1,0:T(8,128)S(1)} %collective-permute-done.7.refs_1_), channel_id=1, source_target_pairs={{0,1},{1,0},{2,3},{3,2},{4,5},{5,4},{6,7},{7,6},{8,9},{9,8},{10,11... | collective-permute-start | bytes 294920 | tf_op jit(solution)/shard_map/ppermute | solution.py:713
  51.2 5.9 %collective-permute-start.12 = (f32[96,1024]{1,0:T(8,128)S(1)}, f32[96,1024]{1,0:T(8,128)S(1)}, u32[]{:S(2)}, u32[]{:S(2)}) collective-permute-start(f32[96,1024]{1,0:T(8,128)S(1)} %collective-permute-done.11.refs_2_), channel_id=1, source_target_pairs={{0,1},{1,0},{2,3},{3,2},{4,5},{5,4},{6,7},{7,6},{8,9},{9,8},{10,11... | collective-permute-start | bytes 1179656 | tf_op jit(solution)/shard_map/ppermute | solution.py:713

commit v4 on v3

--- a/solution.py
+++ b/solution.py
@@ -545,8 +545,7 @@
     issue = fine_issue(fine_w, fine_x)
     use = smooth_fine(inverse, res, step, total, fine_x)
     pipeline(prods, "before", issue, fine_finish(moduli, carry, use))
-    rows = [(total.at[o + y], outs[3].at[24 * y : 24 * y + 24, :]) for y in range(OWN)]
-    leaving += fetched(rows, out_sems, len(leaving))
+    leaving += fetched([(total.at[o : o + OWN], outs[3])], out_sems, len(leaving))
 
     carry[...] = jnp.zeros_like(carry)
 
@@ -657,8 +656,7 @@
     fine_w, prolong_w, shuffle = [Part(book, BOOKS[2][0], name) for name in BOOKS[2][0]]
     copies = [(fix_sent, fix), (load_sent, res), (book_ref, book)]
     for ref, offset in [(s0, 0), (s1, -side), (zs1, side)]:
-        for y in range(OWN):
-            copies.append((ref.at[24 * y : 24 * y + 24, :], total.at[o + OWN * offset + y]))
+        copies.append((ref, total.at[pl.ds(o + OWN * offset, OWN)]))
     first = fetched(copies, sems)
     second = fetched([(inverse_sent, inverse), (moduli_sent, moduli)], sems, len(first))
     clear_tail(fine_x, ROWS)
@@ -769,7 +767,7 @@
         before_kernel,
         out_shape=[
             jax.ShapeDtypeStruct(shape, F32)
-            for shape in [(ROWS, 24, LANES), (ROWS, 8, LANES), (ROWS, 24, LANES), (24 * OWN, LANES), (NOTE, LANES)]
+            for shape in [(ROWS, 24, LANES), (ROWS, 8, LANES), (ROWS, 24, LANES), (OWN, 24, LANES), (NOTE, LANES)]
         ],
         in_specs=[scalars] + [there] * 8,
         out_specs=[there] * 5,
@@ -782,7 +780,7 @@
             pltpu.VMEM((7, 8, 512), F32),
             pltpu.VMEM((8, LANES), F32),
             pltpu.SemaphoreType.DMA((5 * (OWN + 1) + 7,)),
-            pltpu.SemaphoreType.DMA((OWN + 4,)),
+            pltpu.SemaphoreType.DMA((5,)),
             *prods,
         ],
         compiler_params=limit,
@@ -824,7 +822,7 @@
             held(ROWS, 8),
             held(ROWS),
             pltpu.VMEM((ROWS + 1, 16, WIDE), BF16),
-            pltpu.SemaphoreType.DMA((3 * OWN + 5,)),
+            pltpu.SemaphoreType.DMA((8,)),
             *prods,
         ],
         compiler_params=limit,

time: 67.9 us -> 66.5 us (0.979)
  Pallas kernels: 27 us -> 25.5 us
    pallas_call x1, Pallas kernels: 10.3 us -> 9.2 us  [per_device(): pl.pallas_call(after_kernel, out_shape=jax.ShapeDtypeStruct(adjoint_load....]
where the time goes in v4:
time: 66.5 us; the launch traced here: 66 us
  starting transfers between devices  27 us (41%)
  Pallas kernels  25.5 us (38%)
  waiting for transfers between devices  9.05 us (14%)
  local copies, waits for them, and re-layouts  2.46 us (4%)
  other arithmetic  1.68 us (3%)
    ppermute x5, starting transfers between devices, sided(): return lax.ppermute(value, ('gx', 'gy', 'gz'), pairs)  16 us
    ppermute x8, starting transfers between devices, swap(): return lax.ppermute(value, axis, [(0, 1), (1, 0)])  11 us
    pallas_call x1, Pallas kernels, per_device(): pl.pallas_call(before_kernel, out_shape=[jax.ShapeDtypeStruct(shape, F32)...  9.34 us
    pallas_call x1, Pallas kernels, per_device(): pl.pallas_call(after_kernel, out_shape=jax.ShapeDtypeStruct(adjoint_load....  9.2 us
    ppermute x5, waiting for transfers between devices, sided(): return lax.ppermute(value, ('gx', 'gy', 'gz'), pairs)  6.08 us
    pallas_call x1, Pallas kernels, per_device(): pl.pallas_call(coarse_kernel, out_shape=jax.ShapeDtypeStruct((ROWS + 1, 1...  4.92 us
    ppermute x8, waiting for transfers between devices, swap(): return lax.ppermute(value, axis, [(0, 1), (1, 0)])  2.97 us
    unnamed x6, local copies, waits for them, and re-layouts  2.46 us
  transfers between devices with their start and end apart: 13, of which 6 were waited for; matrix products, arithmetic and copies ran while one was open for 0% of the time, Pallas kernels for 8%

profile of v4, /device:TPU:129, one launch (start us, length us, event | category | flops | bytes accessed | tf_op | source)
XLA Modules:
  0.0 66.0 jit_solution(13848348586267665651)
XLA Ops:
  0.0 0.7 %convert_bitcast_fusion = f32[1,8,8,128]{3,2,1,0:T(8,128)S(1)} fusion(s32[4,4,64]{2,1,0:T(4,128)} %param.6), kind=kLoop, calls=%fused_computation.1 | loop fusion | flops 8192 | bytes 36864 | tf_op jit(solution)/shard_map/broadcast_in_dim | solution.py:748
  0.7 0.9 %pad_maximum_fusion.raw_sent = f32[4,8,8,128]{3,2,1,0:T(8,128)S(1)} fusion(f32[1,8,8,128]{3,2,1,0:T(8,128)S(1)} %convert_bitcast_fusion, f32[3,8,8,128]{3,2,1,0:T(8,128)} %param.5), kind=kLoop, calls=%fused_computation | loop fusion | flops 32768 | bytes 262144 | tf_op jit(solution)/shard_map/concatenate | solution.py:748
  1.6 0.8 %collective-permute-start = (f32[4,8,8,128]{3,2,1,0:T(8,128)S(1)}, f32[4,8,8,128]{3,2,1,0:T(8,128)S(1)}, u32[]{:S(2)}, u32[]{:S(2)}) collective-permute-start(f32[4,8,8,128]{3,2,1,0:T(8,128)S(1)} %pad_maximum_fusion.raw_sent), channel_id=1, source_target_pairs={{0,1},{1,0},{2,3},{3,2},{4,5},{5,4},{6,7},{7,6},{8,9},{9,8},{10,11... | collective-permute-start | bytes 393224 | tf_op jit(solution)/shard_map/ppermute | solution.py:711
  2.4 0.1 pad_add_fusion.place_ref
  2.4 0.9 %collective-permute-done.other_sent = f32[4,8,8,128]{3,2,1,0:T(8,128)S(1)} collective-permute-done((f32[4,8,8,128]{3,2,1,0:T(8,128)S(1)}, f32[4,8,8,128]{3,2,1,0:T(8,128)S(1)}, u32[]{:S(2)}, u32[]{:S(2)}) %collective-permute-start) | collective-permute-done | bytes 131104 | tf_op jit(solution)/shard_map/ppermute | solution.py:711
  3.4 1.4 %pack.1 = (f32[104,512]{1,0:T(8,128)S(1)}, f32[56,512]{1,0:T(8,128)S(1)}) custom-call(s32[4]{0:T(128)S(1)} %pad_add_fusion.place_ref, f32[4,8,8,128]{3,2,1,0:T(8,128)S(1)} %pad_maximum_fusion.raw_sent, f32[4,8,8,128]{3,2,1,0:T(8,128)S(1)} %collective-permute-done.other_sent), custom_call_target="tpu_custom_call" | custom-call | tf_op jit(solution)/shard_map/pack/pallas_call | solution.py:727
  4.8 5.1 %collective-permute-start.1 = (f32[104,512]{1,0:T(8,128)S(1)}, f32[104,512]{1,0:T(8,128)S(1)}, u32[]{:S(2)}, u32[]{:S(2)}) collective-permute-start(f32[104,512]{1,0:T(8,128)S(1)} %get-tuple-element.16.refs_0_), channel_id=1, source_target_pairs={{0,2},{3,1},{2,4},{5,3},{4,6},{7,5},{6,8},{9,7},{8,10},{11,9},{10,... | collective-permute-start | bytes 638984 | tf_op jit(solution)/shard_map/ppermute | solution.py:720
  9.9 3.7 %collective-permute-start.2 = (f32[104,512]{1,0:T(8,128)S(1)}, f32[104,512]{1,0:T(8,128)S(1)}, u32[]{:S(2)}, u32[]{:S(2)}) collective-permute-start(f32[104,512]{1,0:T(8,128)S(1)} %get-tuple-element.16.refs_0_), channel_id=1, source_target_pairs={{0,130},{3,129},{2,132},{5,131},{4,134},{7,133},{6,136},{9,135},{8... | collective-permute-start | bytes 638984 | tf_op jit(solution)/shard_map/ppermute | solution.py:720
  13.7 0.7 %collective-permute-start.5 = (f32[56,512]{1,0:T(8,128)S(1)}, f32[56,512]{1,0:T(8,128)S(1)}, u32[]{:S(2)}, u32[]{:S(2)}) collective-permute-start(f32[56,512]{1,0:T(8,128)S(1)} %get-tuple-element.19), channel_id=1, source_target_pairs={{0,128},{128,0},{1,129},{129,1},{2,130},{130,2},{3,131},{131,3},{4... | collective-permute-start | bytes 344072 | tf_op jit(solution)/shard_map/ppermute | solution.py:711
  14.4 0.0 copy-start
  14.4 1.0 %copy-done = bf16[624,256]{1,0:T(8,128)(2,1)S(1)} copy-done((bf16[624,256]{1,0:T(8,128)(2,1)S(1)}, bf16[624,256]{1,0:T(8,128)(2,1)}, u32[]{:S(2)}) %copy-start) | copy-done | bytes 319512
  15.4 0.0 copy-start.1
  15.4 0.8 %copy-done.1 = f32[81,81]{1,0:T(8,128)S(1)} copy-done((f32[81,81]{1,0:T(8,128)S(1)}, f32[81,81]{1,0:T(8,128)}, u32[]{:S(2)}) %copy-start.1) | copy-done | bytes 26268
  16.1 0.0 copy-start.2
  16.1 0.7 %copy-done.2 = f32[24,24]{1,0:T(8,128)S(1)} copy-done((f32[24,24]{1,0:T(8,128)S(1)}, f32[24,24]{1,0:T(8,128)}, u32[]{:S(2)}) %copy-start.2) | copy-done | bytes 2328
  16.9 0.6 weights.1
  17.5 0.0 collective-permute-done.1.refs_1_
  17.5 4.8 %collective-permute-done.2.refs_2_ = f32[104,512]{1,0:T(8,128)S(1)} collective-permute-done((f32[104,512]{1,0:T(8,128)S(1)}, f32[104,512]{1,0:T(8,128)S(1)}, u32[]{:S(2)}, u32[]{:S(2)}) %collective-permute-start.2) | collective-permute-done | bytes 213024 | tf_op jit(solution)/shard_map/ppermute | solution.py:720
  22.3 1.1 %collective-permute-start.4 = (f32[104,512]{1,0:T(8,128)S(1)}, f32[104,512]{1,0:T(8,128)S(1)}, u32[]{:S(2)}, u32[]{:S(2)}) collective-permute-start(f32[104,512]{1,0:T(8,128)S(1)} %collective-permute-done.2.refs_2_), channel_id=1, source_target_pairs={{0,1},{1,0},{2,3},{3,2},{4,5},{5,4},{6,7},{7,6},{8,9},{9,8},{10,11... | collective-permute-start | bytes 638984 | tf_op jit(solution)/shard_map/ppermute | solution.py:711
  23.4 0.0 collective-permute-start.3
  23.4 0.0 collective-permute-done.5.refs_5_
  23.4 0.5 collective-permute-start.6
  23.9 1.1 %collective-permute-done.6.refs_6_ = f32[56,512]{1,0:T(8,128)S(1)} collective-permute-done((f32[56,512]{1,0:T(8,128)S(1)}, f32[56,512]{1,0:T(8,128)S(1)}, u32[]{:S(2)}, u32[]{:S(2)}) %collective-permute-start.6) | collective-permute-done | bytes 114720 | tf_op jit(solution)/shard_map/ppermute | solution.py:711
  25.0 0.0 collective-permute-done.4.refs_4_
  25.0 0.0 collective-permute-done.3.refs_3_
  25.0 9.3 %before.1 = (f32[12,24,1024]{2,1,0:T(8,128)S(1)}, f32[12,8,1024]{2,1,0:T(8,128)S(1)}, f32[12,24,1024]{2,1,0:T(8,128)S(1)}, f32[4,24,1024]{2,1,0:T(8,128)S(1)}, f32[24,1024]{1,0:T(8,128)S(1)}) custom-call(s32[4]{0:T(128)S(1)} %pad_add_fusion.place_ref, f32[104,512]{1,0:T(8,128)S(1)} %get-tuple-element.16.refs_0_, ...), custom_call_target="tpu_custom_call" | custom-call | tf_op jit(solution)/shard_map/before/pallas_call | solution.py:766
  34.4 2.1 %collective-permute-start.11 = (f32[4,24,1024]{2,1,0:T(8,128)S(1)}, f32[4,24,1024]{2,1,0:T(8,128)S(1)}, u32[]{:S(2)}, u32[]{:S(2)}) collective-permute-start(f32[4,24,1024]{2,1,0:T(8,128)S(1)} %get-tuple-element.23.refs_1_), channel_id=1, source_target_pairs={{0,2},{3,1},{2,4},{5,3},{4,6},{7,5},{6,8},{9,7},{8,10},{11,9},{10,... | collective-permute-start | bytes 1179656 | tf_op jit(solution)/shard_map/ppermute | solution.py:720
  36.5 1.9 %collective-permute-start.9 = (f32[24,1024]{1,0:T(8,128)S(1)}, f32[24,1024]{1,0:T(8,128)S(1)}, u32[]{:S(2)}, u32[]{:S(2)}) collective-permute-start(f32[24,1024]{1,0:T(8,128)S(1)} %get-tuple-element.20.refs_0_), channel_id=1, source_target_pairs={{0,4},{5,1},{2,6},{7,3},{4,8},{9,5},{6,10},{11,7},{8,12},{13,9},{1... | collective-permute-start | bytes 294920 | tf_op jit(solution)/shard_map/ppermute | solution.py:720
  38.5 3.1 %collective-permute-start.7 = (f32[24,1024]{1,0:T(8,128)S(1)}, f32[24,1024]{1,0:T(8,128)S(1)}, u32[]{:S(2)}, u32[]{:S(2)}) collective-permute-start(f32[24,1024]{1,0:T(8,128)S(1)} %get-tuple-element.20.refs_0_), channel_id=1, source_target_pairs={{0,2},{3,1},{2,4},{5,3},{4,6},{7,5},{6,8},{9,7},{8,10},{11,9},{10,... | collective-permute-start | bytes 294920 | tf_op jit(solution)/shard_map/ppermute | solution.py:720
  41.6 0.7 %collective-permute-done.9.refs_3_ = f32[24,1024]{1,0:T(8,128)S(1)} collective-permute-done((f32[24,1024]{1,0:T(8,128)S(1)}, f32[24,1024]{1,0:T(8,128)S(1)}, u32[]{:S(2)}, u32[]{:S(2)}) %collective-permute-start.9) | collective-permute-done | bytes 98336 | tf_op jit(solution)/shard_map/ppermute | solution.py:720
  42.3 5.2 %collective-permute-start.10 = (f32[24,1024]{1,0:T(8,128)S(1)}, f32[24,1024]{1,0:T(8,128)S(1)}, u32[]{:S(2)}, u32[]{:S(2)}) collective-permute-start(f32[24,1024]{1,0:T(8,128)S(1)} %collective-permute-done.9.refs_3_), channel_id=1, source_target_pairs={{0,1},{1,0},{2,3},{3,2},{4,5},{5,4},{6,7},{7,6},{8,9},{9,8},{10,11... | collective-permute-start | bytes 294920 | tf_op jit(solution)/shard_map/ppermute | solution.py:711
  47.6 0.5 collective-permute-done.7.refs_1_
  48.1 2.7 %collective-permute-start.8 = (f32[24,1024]{1,0:T(8,128)S(1)}, f32[24,1024]{1,0:T(8,128)S(1)}, u32[]{:S(2)}, u32[]{:S(2)}) collective-permute-start(f32[24,1024]{1,0:T(8,128)S(1)} %collective-permute-done.7.refs_1_), channel_id=1, source_target_pairs={{0,1},{1,0},{2,3},{3,2},{4,5},{5,4},{6,7},{7,6},{8,9},{9,8},{10,11... | collective-permute-start | bytes 294920 | tf_op jit(solution)/shard_map/ppermute | solution.py:711
  50.8 0.0 collective-permute-done.11.refs_2_
  50.8 0.0 collective-permute-start.12
  50.8 0.0 collective-permute-done.10.refs_4_
  50.8 0.9 %collective-permute-done.8.refs_2_ = f32[24,1024]{1,0:T(8,128)S(1)} collective-permute-done((f32[24,1024]{1,0:T(8,128)S(1)}, f32[24,1024]{1,0:T(8,128)S(1)}, u32[]{:S(2)}, u32[]{:S(2)}) %collective-permute-start.8) | collective-permute-done | bytes 98336 | tf_op jit(solution)/shard_map/ppermute | solution.py:711
  51.7 4.9 %coarse.1.refs_0_ = bf16[13,16,1152]{2,1,0:T(8,128)(2,1)S(1)} custom-call(s32[4]{0:T(128)S(1)} %pad_add_fusion.place_ref, f32[24,1024]{1,0:T(8,128)S(1)} %get-tuple-element.20.refs_0_, f32[24,1024]{1,0:T(8,128)S(1)} %collective-permute-done.7.refs_1_, f32[24,1024]{1,0:T(8,128)S(1)} %collective-permute-done.8.refs_2_, ...), custom_call_target="tpu_custom_call" | custom-call | flops 4000000000 | bytes 40000000 | tf_op jit(solution)/shard_map/coarse/pallas_call | solution.py:792
  56.7 0.0 collective-permute-done.12.refs_3_
  56.7 9.2 %after.1 = f32[3,8,8,128]{3,2,1,0:T(8,128)} custom-call(s32[4]{0:T(128)S(1)} %pad_add_fusion.place_ref, bf16[13,16,1152]{2,1,0:T(8,128)(2,1)S(1)} %coarse.1.refs_0_, f32[4,24,1024]{2,1,0:T(8,128)S(1)} %get-tuple-element.23.refs_1_, f32[4,24,1024]{2,1,0:T(8,128)S(1)} %collective-permute-done.11.refs_2_, f32[4,24,1024]{2,1,0:T(8,128)S(1)} %collective-permute-done.12.refs_3_, ...), custom_call_target="tpu_custom_call" | custom-call | tf_op jit(solution)/shard_map/after/pallas_call | solution.py:814
Async XLA Ops:
  1.6 1.7 %collective-permute-start = (f32[4,8,8,128]{3,2,1,0:T(8,128)S(1)}, f32[4,8,8,128]{3,2,1,0:T(8,128)S(1)}, u32[]{:S(2)}, u32[]{:S(2)}) collective-permute-start(f32[4,8,8,128]{3,2,1,0:T(8,128)S(1)} %pad_maximum_fusion.raw_sent), channel_id=1, source_target_pairs={{0,1},{1,0},{2,3},{3,2},{4,5},{5,4},{6,7},{7,6},{8,9},{9,8},{10,11... | collective-permute-start | bytes 393224 | tf_op jit(solution)/shard_map/ppermute | solution.py:711
  4.8 12.7 %collective-permute-start.1 = (f32[104,512]{1,0:T(8,128)S(1)}, f32[104,512]{1,0:T(8,128)S(1)}, u32[]{:S(2)}, u32[]{:S(2)}) collective-permute-start(f32[104,512]{1,0:T(8,128)S(1)} %get-tuple-element.16.refs_0_), channel_id=1, source_target_pairs={{0,2},{3,1},{2,4},{5,3},{4,6},{7,5},{6,8},{9,7},{8,10},{11,9},{10,... | collective-permute-start | bytes 638984 | tf_op jit(solution)/shard_map/ppermute | solution.py:720
  9.9 12.4 %collective-permute-start.2 = (f32[104,512]{1,0:T(8,128)S(1)}, f32[104,512]{1,0:T(8,128)S(1)}, u32[]{:S(2)}, u32[]{:S(2)}) collective-permute-start(f32[104,512]{1,0:T(8,128)S(1)} %get-tuple-element.16.refs_0_), channel_id=1, source_target_pairs={{0,130},{3,129},{2,132},{5,131},{4,134},{7,133},{6,136},{9,135},{8... | collective-permute-start | bytes 638984 | tf_op jit(solution)/shard_map/ppermute | solution.py:720
  13.7 9.8 %collective-permute-start.5 = (f32[56,512]{1,0:T(8,128)S(1)}, f32[56,512]{1,0:T(8,128)S(1)}, u32[]{:S(2)}, u32[]{:S(2)}) collective-permute-start(f32[56,512]{1,0:T(8,128)S(1)} %get-tuple-element.19), channel_id=1, source_target_pairs={{0,128},{128,0},{1,129},{129,1},{2,130},{130,2},{3,131},{131,3},{4... | collective-permute-start | bytes 344072 | tf_op jit(solution)/shard_map/ppermute | solution.py:711
  14.4 1.0 %copy-start = (bf16[624,256]{1,0:T(8,128)(2,1)S(1)}, bf16[624,256]{1,0:T(8,128)(2,1)}, u32[]{:S(2)}) copy-start(bf16[624,256]{1,0:T(8,128)(2,1)} %constant.18.clone.cards_ref) | copy-start | bytes 958468
  15.4 0.8 %copy-start.1 = (f32[81,81]{1,0:T(8,128)S(1)}, f32[81,81]{1,0:T(8,128)}, u32[]{:S(2)}) copy-start(f32[81,81]{1,0:T(8,128)} %fine_ref.1) | copy-start | bytes 78736
  16.1 0.7 %copy-start.2 = (f32[24,24]{1,0:T(8,128)S(1)}, f32[24,24]{1,0:T(8,128)}, u32[]{:S(2)}) copy-start(f32[24,24]{1,0:T(8,128)} %coarse_ref.1) | copy-start | bytes 6916
  22.3 2.7 %collective-permute-start.4 = (f32[104,512]{1,0:T(8,128)S(1)}, f32[104,512]{1,0:T(8,128)S(1)}, u32[]{:S(2)}, u32[]{:S(2)}) collective-permute-start(f32[104,512]{1,0:T(8,128)S(1)} %collective-permute-done.2.refs_2_), channel_id=1, source_target_pairs={{0,1},{1,0},{2,3},{3,2},{4,5},{5,4},{6,7},{7,6},{8,9},{9,8},{10,11... | collective-permute-start | bytes 638984 | tf_op jit(solution)/shard_map/ppermute | solution.py:711
  23.4 1.6 %collective-permute-start.3 = (f32[104,512]{1,0:T(8,128)S(1)}, f32[104,512]{1,0:T(8,128)S(1)}, u32[]{:S(2)}, u32[]{:S(2)}) collective-permute-start(f32[104,512]{1,0:T(8,128)S(1)} %collective-permute-done.1.refs_1_), channel_id=1, source_target_pairs={{0,1},{1,0},{2,3},{3,2},{4,5},{5,4},{6,7},{7,6},{8,9},{9,8},{10,11... | collective-permute-start | bytes 638984 | tf_op jit(solution)/shard_map/ppermute | solution.py:711
  23.4 1.6 %collective-permute-start.6 = (f32[56,512]{1,0:T(8,128)S(1)}, f32[56,512]{1,0:T(8,128)S(1)}, u32[]{:S(2)}, u32[]{:S(2)}) collective-permute-start(f32[56,512]{1,0:T(8,128)S(1)} %collective-permute-done.5.refs_5_), channel_id=1, source_target_pairs={{0,1},{1,0},{2,3},{3,2},{4,5},{5,4},{6,7},{7,6},{8,9},{9,8},{10,11... | collective-permute-start | bytes 344072 | tf_op jit(solution)/shard_map/ppermute | solution.py:711
  34.4 16.4 %collective-permute-start.11 = (f32[4,24,1024]{2,1,0:T(8,128)S(1)}, f32[4,24,1024]{2,1,0:T(8,128)S(1)}, u32[]{:S(2)}, u32[]{:S(2)}) collective-permute-start(f32[4,24,1024]{2,1,0:T(8,128)S(1)} %get-tuple-element.23.refs_1_), channel_id=1, source_target_pairs={{0,2},{3,1},{2,4},{5,3},{4,6},{7,5},{6,8},{9,7},{8,10},{11,9},{10,... | collective-permute-start | bytes 1179656 | tf_op jit(solution)/shard_map/ppermute | solution.py:720
  36.5 5.8 %collective-permute-start.9 = (f32[24,1024]{1,0:T(8,128)S(1)}, f32[24,1024]{1,0:T(8,128)S(1)}, u32[]{:S(2)}, u32[]{:S(2)}) collective-permute-start(f32[24,1024]{1,0:T(8,128)S(1)} %get-tuple-element.20.refs_0_), channel_id=1, source_target_pairs={{0,4},{5,1},{2,6},{7,3},{4,8},{9,5},{6,10},{11,7},{8,12},{13,9},{1... | collective-permute-start | bytes 294920 | tf_op jit(solution)/shard_map/ppermute | solution.py:720
  38.5 9.6 %collective-permute-start.7 = (f32[24,1024]{1,0:T(8,128)S(1)}, f32[24,1024]{1,0:T(8,128)S(1)}, u32[]{:S(2)}, u32[]{:S(2)}) collective-permute-start(f32[24,1024]{1,0:T(8,128)S(1)} %get-tuple-element.20.refs_0_), channel_id=1, source_target_pairs={{0,2},{3,1},{2,4},{5,3},{4,6},{7,5},{6,8},{9,7},{8,10},{11,9},{10,... | collective-permute-start | bytes 294920 | tf_op jit(solution)/shard_map/ppermute | solution.py:720
  42.3 8.5 %collective-permute-start.10 = (f32[24,1024]{1,0:T(8,128)S(1)}, f32[24,1024]{1,0:T(8,128)S(1)}, u32[]{:S(2)}, u32[]{:S(2)}) collective-permute-start(f32[24,1024]{1,0:T(8,128)S(1)} %collective-permute-done.9.refs_3_), channel_id=1, source_target_pairs={{0,1},{1,0},{2,3},{3,2},{4,5},{5,4},{6,7},{7,6},{8,9},{9,8},{10,11... | collective-permute-start | bytes 294920 | tf_op jit(solution)/shard_map/ppermute | solution.py:711
  48.1 3.7 %collective-permute-start.8 = (f32[24,1024]{1,0:T(8,128)S(1)}, f32[24,1024]{1,0:T(8,128)S(1)}, u32[]{:S(2)}, u32[]{:S(2)}) collective-permute-start(f32[24,1024]{1,0:T(8,128)S(1)} %collective-permute-done.7.refs_1_), channel_id=1, source_target_pairs={{0,1},{1,0},{2,3},{3,2},{4,5},{5,4},{6,7},{7,6},{8,9},{9,8},{10,11... | collective-permute-start | bytes 294920 | tf_op jit(solution)/shard_map/ppermute | solution.py:711
  50.8 5.9 %collective-permute-start.12 = (f32[4,24,1024]{2,1,0:T(8,128)S(1)}, f32[4,24,1024]{2,1,0:T(8,128)S(1)}, u32[]{:S(2)}, u32[]{:S(2)}) collective-permute-start(f32[4,24,1024]{2,1,0:T(8,128)S(1)} %collective-permute-done.11.refs_2_), channel_id=1, source_target_pairs={{0,1},{1,0},{2,3},{3,2},{4,5},{5,4},{6,7},{7,6},{8,9},{9,8},{10,11... | collective-permute-start | bytes 1179656 | tf_op jit(solution)/shard_map/ppermute | solution.py:711

commit v5 on v4

--- a/solution.py
+++ b/solution.py
@@ -370,13 +370,13 @@
     steps = schedules()[name]
     for t in range(len(steps) + AHEAD):
         if t < len(steps):
-            issue(steps[t].row, prods[t % len(prods)])
+            issue(steps[t].row, prods[t % len(prods)], steps[t].lead)
         if t >= AHEAD:
             finish(steps[t - AHEAD], prods[(t - AHEAD) % len(prods)])
 
 
 def fine_issue(fine_w, fine_x):
-    def issue(y, prod):
+    def issue(y, prod, lead):
         for low, lanes in CHUNKS:
             there = slice(low + 128, low + 384)
             operand = jnp.concatenate(
@@ -389,6 +389,13 @@
                 ],
                 axis=0,
             )
+            if lead:
+                weights = fine_w[...]
+                weights = jnp.concatenate([weights[at : at + 32] for at in (32, 96, 160, 224)], axis=0)
+                products = jnp.dot(weights, operand, preferred_element_type=F32)
+                prod[32:64, lanes] = products[0:32] + products[64:96]
+                prod[96:128, lanes] = products[32:64] + products[96:128]
+                continue
             products = jnp.dot(fine_w[...], operand, preferred_element_type=F32)
             prod[:, lanes] = products[:128] + products[128:]
 
@@ -403,7 +410,9 @@
             m = moduli[y, :, lanes]
             sums = []
             for z in range(2):
-                v = scaled(prod[64 * z : 64 * z + 64, lanes], m)
+                v = scaled(prod[64 * z + 32 * now.lead : 64 * z + 64, lanes], m)
+                if now.lead:
+                    v = jnp.concatenate([jnp.zeros((32, 256), F32), v], axis=0)
                 if not now.lead:
                     old = carry[16 * z : 16 * z + 16, lanes]
                     along_x = pushed(before[z][0], v[24:40])
@@ -461,7 +470,7 @@
 
 
 def diag_issue(diag_w, moduli, count):
-    def issue(y, prod):
+    def issue(y, prod, lead):
         spot = lax.broadcasted_iota(jnp.int32, (8, 256), 0)
         before = jnp.zeros((8, 128), F32)
         for low, lanes in CHUNKS:
@@ -625,7 +634,7 @@
 
     pipeline(prods, "coarse_start", diag_issue(diag_w, moduli, 8), start)
 
-    def issue(y, prod):
+    def issue(y, prod, lead):
         for low, lanes in CHUNKS:
             products = jnp.dot(coarse_w[...], coarse_operand(coarse_x, y, low, lanes), preferred_element_type=F32)
             prod[0:32, lanes] = products[:32] + products[32:]
@@ -663,7 +672,7 @@
     carry[...] = jnp.zeros_like(carry)
     wait_for(first)
 
-    def correct_issue(y, prod):
+    def correct_issue(y, prod, lead):
         for low, lanes in CHUNKS:
             prod[0:24, lanes] = jnp.dot(
                 prolong_w[...], coarse_operand(fix, y, low, lanes), preferred_element_type=F32

time: 66.5 us -> 66.1 us (level)
  no operation moved by 1% of the time
where the time goes in v5:
time: 66.1 us; the launch traced here: 65.7 us
  starting transfers between devices  27 us (41%)
  Pallas kernels  25.2 us (38%)
  waiting for transfers between devices  9.06 us (14%)
  local copies, waits for them, and re-layouts  2.46 us (4%)
  other arithmetic  1.68 us (3%)
    ppermute x5, starting transfers between devices, sided(): return lax.ppermute(value, ('gx', 'gy', 'gz'), pairs)  16 us
    ppermute x8, starting transfers between devices, swap(): return lax.ppermute(value, axis, [(0, 1), (1, 0)])  11 us
    pallas_call x1, Pallas kernels, per_device(): pl.pallas_call(before_kernel, out_shape=[jax.ShapeDtypeStruct(shape, F32)...  9.22 us
    pallas_call x1, Pallas kernels, per_device(): pl.pallas_call(after_kernel, out_shape=jax.ShapeDtypeStruct(adjoint_load....  8.96 us
    ppermute x5, waiting for transfers between devices, sided(): return lax.ppermute(value, ('gx', 'gy', 'gz'), pairs)  6.09 us
    pallas_call x1, Pallas kernels, per_device(): pl.pallas_call(coarse_kernel, out_shape=jax.ShapeDtypeStruct((ROWS + 1, 1...  4.92 us
    ppermute x8, waiting for transfers between devices, swap(): return lax.ppermute(value, axis, [(0, 1), (1, 0)])  2.97 us
    unnamed x6, local copies, waits for them, and re-layouts  2.46 us
  transfers between devices with their start and end apart: 13, of which 6 were waited for; matrix products, arithmetic and copies ran while one was open for 0% of the time, Pallas kernels for 8%

profile of v5, /device:TPU:129, one launch (start us, length us, event | category | flops | bytes accessed | tf_op | source)
XLA Modules:
  0.0 65.7 jit_solution(5714422710050088666)
XLA Ops:
  0.0 0.7 %convert_bitcast_fusion = f32[1,8,8,128]{3,2,1,0:T(8,128)S(1)} fusion(s32[4,4,64]{2,1,0:T(4,128)} %param.6), kind=kLoop, calls=%fused_computation.1 | loop fusion | flops 8192 | bytes 36864 | tf_op jit(solution)/shard_map/broadcast_in_dim | solution.py:757
  0.7 0.9 %pad_maximum_fusion.raw_sent = f32[4,8,8,128]{3,2,1,0:T(8,128)S(1)} fusion(f32[1,8,8,128]{3,2,1,0:T(8,128)S(1)} %convert_bitcast_fusion, f32[3,8,8,128]{3,2,1,0:T(8,128)} %param.5), kind=kLoop, calls=%fused_computation | loop fusion | flops 32768 | bytes 262144 | tf_op jit(solution)/shard_map/concatenate | solution.py:757
  1.6 0.8 %collective-permute-start = (f32[4,8,8,128]{3,2,1,0:T(8,128)S(1)}, f32[4,8,8,128]{3,2,1,0:T(8,128)S(1)}, u32[]{:S(2)}, u32[]{:S(2)}) collective-permute-start(f32[4,8,8,128]{3,2,1,0:T(8,128)S(1)} %pad_maximum_fusion.raw_sent), channel_id=1, source_target_pairs={{0,1},{1,0},{2,3},{3,2},{4,5},{5,4},{6,7},{7,6},{8,9},{9,8},{10,11... | collective-permute-start | bytes 393224 | tf_op jit(solution)/shard_map/ppermute | solution.py:720
  2.4 0.1 pad_add_fusion.place_ref
  2.4 0.9 %collective-permute-done.other_sent = f32[4,8,8,128]{3,2,1,0:T(8,128)S(1)} collective-permute-done((f32[4,8,8,128]{3,2,1,0:T(8,128)S(1)}, f32[4,8,8,128]{3,2,1,0:T(8,128)S(1)}, u32[]{:S(2)}, u32[]{:S(2)}) %collective-permute-start) | collective-permute-done | bytes 131104 | tf_op jit(solution)/shard_map/ppermute | solution.py:720
  3.4 1.4 %pack.1 = (f32[104,512]{1,0:T(8,128)S(1)}, f32[56,512]{1,0:T(8,128)S(1)}) custom-call(s32[4]{0:T(128)S(1)} %pad_add_fusion.place_ref, f32[4,8,8,128]{3,2,1,0:T(8,128)S(1)} %pad_maximum_fusion.raw_sent, f32[4,8,8,128]{3,2,1,0:T(8,128)S(1)} %collective-permute-done.other_sent), custom_call_target="tpu_custom_call" | custom-call | tf_op jit(solution)/shard_map/pack/pallas_call | solution.py:736
  4.8 5.1 %collective-permute-start.1 = (f32[104,512]{1,0:T(8,128)S(1)}, f32[104,512]{1,0:T(8,128)S(1)}, u32[]{:S(2)}, u32[]{:S(2)}) collective-permute-start(f32[104,512]{1,0:T(8,128)S(1)} %get-tuple-element.16.refs_0_), channel_id=1, source_target_pairs={{0,2},{3,1},{2,4},{5,3},{4,6},{7,5},{6,8},{9,7},{8,10},{11,9},{10,... | collective-permute-start | bytes 638984 | tf_op jit(solution)/shard_map/ppermute | solution.py:729
  9.9 3.7 %collective-permute-start.2 = (f32[104,512]{1,0:T(8,128)S(1)}, f32[104,512]{1,0:T(8,128)S(1)}, u32[]{:S(2)}, u32[]{:S(2)}) collective-permute-start(f32[104,512]{1,0:T(8,128)S(1)} %get-tuple-element.16.refs_0_), channel_id=1, source_target_pairs={{0,130},{3,129},{2,132},{5,131},{4,134},{7,133},{6,136},{9,135},{8... | collective-permute-start | bytes 638984 | tf_op jit(solution)/shard_map/ppermute | solution.py:729
  13.7 0.7 %collective-permute-start.5 = (f32[56,512]{1,0:T(8,128)S(1)}, f32[56,512]{1,0:T(8,128)S(1)}, u32[]{:S(2)}, u32[]{:S(2)}) collective-permute-start(f32[56,512]{1,0:T(8,128)S(1)} %get-tuple-element.19), channel_id=1, source_target_pairs={{0,128},{128,0},{1,129},{129,1},{2,130},{130,2},{3,131},{131,3},{4... | collective-permute-start | bytes 344072 | tf_op jit(solution)/shard_map/ppermute | solution.py:720
  14.4 0.0 copy-start
  14.4 1.0 %copy-done = bf16[624,256]{1,0:T(8,128)(2,1)S(1)} copy-done((bf16[624,256]{1,0:T(8,128)(2,1)S(1)}, bf16[624,256]{1,0:T(8,128)(2,1)}, u32[]{:S(2)}) %copy-start) | copy-done | bytes 319512
  15.4 0.0 copy-start.1
  15.4 0.8 %copy-done.1 = f32[81,81]{1,0:T(8,128)S(1)} copy-done((f32[81,81]{1,0:T(8,128)S(1)}, f32[81,81]{1,0:T(8,128)}, u32[]{:S(2)}) %copy-start.1) | copy-done | bytes 26268
  16.1 0.0 copy-start.2
  16.1 0.7 %copy-done.2 = f32[24,24]{1,0:T(8,128)S(1)} copy-done((f32[24,24]{1,0:T(8,128)S(1)}, f32[24,24]{1,0:T(8,128)}, u32[]{:S(2)}) %copy-start.2) | copy-done | bytes 2328
  16.9 0.6 weights.1
  17.5 0.0 collective-permute-done.1.refs_1_
  17.5 4.8 %collective-permute-done.2.refs_2_ = f32[104,512]{1,0:T(8,128)S(1)} collective-permute-done((f32[104,512]{1,0:T(8,128)S(1)}, f32[104,512]{1,0:T(8,128)S(1)}, u32[]{:S(2)}, u32[]{:S(2)}) %collective-permute-start.2) | collective-permute-done | bytes 213024 | tf_op jit(solution)/shard_map/ppermute | solution.py:729
  22.3 1.1 %collective-permute-start.4 = (f32[104,512]{1,0:T(8,128)S(1)}, f32[104,512]{1,0:T(8,128)S(1)}, u32[]{:S(2)}, u32[]{:S(2)}) collective-permute-start(f32[104,512]{1,0:T(8,128)S(1)} %collective-permute-done.2.refs_2_), channel_id=1, source_target_pairs={{0,1},{1,0},{2,3},{3,2},{4,5},{5,4},{6,7},{7,6},{8,9},{9,8},{10,11... | collective-permute-start | bytes 638984 | tf_op jit(solution)/shard_map/ppermute | solution.py:720
  23.4 0.0 collective-permute-start.3
  23.4 0.0 collective-permute-done.5.refs_5_
  23.4 0.5 collective-permute-start.6
  23.9 1.1 %collective-permute-done.6.refs_6_ = f32[56,512]{1,0:T(8,128)S(1)} collective-permute-done((f32[56,512]{1,0:T(8,128)S(1)}, f32[56,512]{1,0:T(8,128)S(1)}, u32[]{:S(2)}, u32[]{:S(2)}) %collective-permute-start.6) | collective-permute-done | bytes 114720 | tf_op jit(solution)/shard_map/ppermute | solution.py:720
  25.0 0.0 collective-permute-done.4.refs_4_
  25.0 0.0 collective-permute-done.3.refs_3_
  25.0 9.2 %before.1 = (f32[12,24,1024]{2,1,0:T(8,128)S(1)}, f32[12,8,1024]{2,1,0:T(8,128)S(1)}, f32[12,24,1024]{2,1,0:T(8,128)S(1)}, f32[4,24,1024]{2,1,0:T(8,128)S(1)}, f32[24,1024]{1,0:T(8,128)S(1)}) custom-call(s32[4]{0:T(128)S(1)} %pad_add_fusion.place_ref, f32[104,512]{1,0:T(8,128)S(1)} %get-tuple-element.16.refs_0_, ...), custom_call_target="tpu_custom_call" | custom-call | tf_op jit(solution)/shard_map/before/pallas_call | solution.py:775
  34.3 2.1 %collective-permute-start.11 = (f32[4,24,1024]{2,1,0:T(8,128)S(1)}, f32[4,24,1024]{2,1,0:T(8,128)S(1)}, u32[]{:S(2)}, u32[]{:S(2)}) collective-permute-start(f32[4,24,1024]{2,1,0:T(8,128)S(1)} %get-tuple-element.23.refs_1_), channel_id=1, source_target_pairs={{0,2},{3,1},{2,4},{5,3},{4,6},{7,5},{6,8},{9,7},{8,10},{11,9},{10,... | collective-permute-start | bytes 1179656 | tf_op jit(solution)/shard_map/ppermute | solution.py:729
  36.4 1.9 %collective-permute-start.9 = (f32[24,1024]{1,0:T(8,128)S(1)}, f32[24,1024]{1,0:T(8,128)S(1)}, u32[]{:S(2)}, u32[]{:S(2)}) collective-permute-start(f32[24,1024]{1,0:T(8,128)S(1)} %get-tuple-element.20.refs_0_), channel_id=1, source_target_pairs={{0,4},{5,1},{2,6},{7,3},{4,8},{9,5},{6,10},{11,7},{8,12},{13,9},{1... | collective-permute-start | bytes 294920 | tf_op jit(solution)/shard_map/ppermute | solution.py:729
  38.3 3.1 %collective-permute-start.7 = (f32[24,1024]{1,0:T(8,128)S(1)}, f32[24,1024]{1,0:T(8,128)S(1)}, u32[]{:S(2)}, u32[]{:S(2)}) collective-permute-start(f32[24,1024]{1,0:T(8,128)S(1)} %get-tuple-element.20.refs_0_), channel_id=1, source_target_pairs={{0,2},{3,1},{2,4},{5,3},{4,6},{7,5},{6,8},{9,7},{8,10},{11,9},{10,... | collective-permute-start | bytes 294920 | tf_op jit(solution)/shard_map/ppermute | solution.py:729
  41.5 0.7 %collective-permute-done.9.refs_3_ = f32[24,1024]{1,0:T(8,128)S(1)} collective-permute-done((f32[24,1024]{1,0:T(8,128)S(1)}, f32[24,1024]{1,0:T(8,128)S(1)}, u32[]{:S(2)}, u32[]{:S(2)}) %collective-permute-start.9) | collective-permute-done | bytes 98336 | tf_op jit(solution)/shard_map/ppermute | solution.py:729
  42.2 5.2 %collective-permute-start.10 = (f32[24,1024]{1,0:T(8,128)S(1)}, f32[24,1024]{1,0:T(8,128)S(1)}, u32[]{:S(2)}, u32[]{:S(2)}) collective-permute-start(f32[24,1024]{1,0:T(8,128)S(1)} %collective-permute-done.9.refs_3_), channel_id=1, source_target_pairs={{0,1},{1,0},{2,3},{3,2},{4,5},{5,4},{6,7},{7,6},{8,9},{9,8},{10,11... | collective-permute-start | bytes 294920 | tf_op jit(solution)/shard_map/ppermute | solution.py:720
  47.4 0.5 collective-permute-done.7.refs_1_
  48.0 2.7 %collective-permute-start.8 = (f32[24,1024]{1,0:T(8,128)S(1)}, f32[24,1024]{1,0:T(8,128)S(1)}, u32[]{:S(2)}, u32[]{:S(2)}) collective-permute-start(f32[24,1024]{1,0:T(8,128)S(1)} %collective-permute-done.7.refs_1_), channel_id=1, source_target_pairs={{0,1},{1,0},{2,3},{3,2},{4,5},{5,4},{6,7},{7,6},{8,9},{9,8},{10,11... | collective-permute-start | bytes 294920 | tf_op jit(solution)/shard_map/ppermute | solution.py:720
  50.7 0.0 collective-permute-done.11.refs_2_
  50.7 0.0 collective-permute-start.12
  50.7 0.0 collective-permute-done.10.refs_4_
  50.7 0.9 %collective-permute-done.8.refs_2_ = f32[24,1024]{1,0:T(8,128)S(1)} collective-permute-done((f32[24,1024]{1,0:T(8,128)S(1)}, f32[24,1024]{1,0:T(8,128)S(1)}, u32[]{:S(2)}, u32[]{:S(2)}) %collective-permute-start.8) | collective-permute-done | bytes 98336 | tf_op jit(solution)/shard_map/ppermute | solution.py:720
  51.6 4.9 %coarse.1.refs_0_ = bf16[13,16,1152]{2,1,0:T(8,128)(2,1)S(1)} custom-call(s32[4]{0:T(128)S(1)} %pad_add_fusion.place_ref, f32[24,1024]{1,0:T(8,128)S(1)} %get-tuple-element.20.refs_0_, f32[24,1024]{1,0:T(8,128)S(1)} %collective-permute-done.7.refs_1_, f32[24,1024]{1,0:T(8,128)S(1)} %collective-permute-done.8.refs_2_, ...), custom_call_target="tpu_custom_call" | custom-call | flops 4000000000 | bytes 40000000 | tf_op jit(solution)/shard_map/coarse/pallas_call | solution.py:801
  56.6 0.0 collective-permute-done.12.refs_3_
  56.6 9.0 %after.1 = f32[3,8,8,128]{3,2,1,0:T(8,128)} custom-call(s32[4]{0:T(128)S(1)} %pad_add_fusion.place_ref, bf16[13,16,1152]{2,1,0:T(8,128)(2,1)S(1)} %coarse.1.refs_0_, f32[4,24,1024]{2,1,0:T(8,128)S(1)} %get-tuple-element.23.refs_1_, f32[4,24,1024]{2,1,0:T(8,128)S(1)} %collective-permute-done.11.refs_2_, f32[4,24,1024]{2,1,0:T(8,128)S(1)} %collective-permute-done.12.refs_3_, ...), custom_call_target="tpu_custom_call" | custom-call | tf_op jit(solution)/shard_map/after/pallas_call | solution.py:823
Async XLA Ops:
  1.6 1.7 %collective-permute-start = (f32[4,8,8,128]{3,2,1,0:T(8,128)S(1)}, f32[4,8,8,128]{3,2,1,0:T(8,128)S(1)}, u32[]{:S(2)}, u32[]{:S(2)}) collective-permute-start(f32[4,8,8,128]{3,2,1,0:T(8,128)S(1)} %pad_maximum_fusion.raw_sent), channel_id=1, source_target_pairs={{0,1},{1,0},{2,3},{3,2},{4,5},{5,4},{6,7},{7,6},{8,9},{9,8},{10,11... | collective-permute-start | bytes 393224 | tf_op jit(solution)/shard_map/ppermute | solution.py:720
  4.8 12.7 %collective-permute-start.1 = (f32[104,512]{1,0:T(8,128)S(1)}, f32[104,512]{1,0:T(8,128)S(1)}, u32[]{:S(2)}, u32[]{:S(2)}) collective-permute-start(f32[104,512]{1,0:T(8,128)S(1)} %get-tuple-element.16.refs_0_), channel_id=1, source_target_pairs={{0,2},{3,1},{2,4},{5,3},{4,6},{7,5},{6,8},{9,7},{8,10},{11,9},{10,... | collective-permute-start | bytes 638984 | tf_op jit(solution)/shard_map/ppermute | solution.py:729
  9.9 12.4 %collective-permute-start.2 = (f32[104,512]{1,0:T(8,128)S(1)}, f32[104,512]{1,0:T(8,128)S(1)}, u32[]{:S(2)}, u32[]{:S(2)}) collective-permute-start(f32[104,512]{1,0:T(8,128)S(1)} %get-tuple-element.16.refs_0_), channel_id=1, source_target_pairs={{0,130},{3,129},{2,132},{5,131},{4,134},{7,133},{6,136},{9,135},{8... | collective-permute-start | bytes 638984 | tf_op jit(solution)/shard_map/ppermute | solution.py:729
  13.7 9.8 %collective-permute-start.5 = (f32[56,512]{1,0:T(8,128)S(1)}, f32[56,512]{1,0:T(8,128)S(1)}, u32[]{:S(2)}, u32[]{:S(2)}) collective-permute-start(f32[56,512]{1,0:T(8,128)S(1)} %get-tuple-element.19), channel_id=1, source_target_pairs={{0,128},{128,0},{1,129},{129,1},{2,130},{130,2},{3,131},{131,3},{4... | collective-permute-start | bytes 344072 | tf_op jit(solution)/shard_map/ppermute | solution.py:720
  14.4 1.0 %copy-start = (bf16[624,256]{1,0:T(8,128)(2,1)S(1)}, bf16[624,256]{1,0:T(8,128)(2,1)}, u32[]{:S(2)}) copy-start(bf16[624,256]{1,0:T(8,128)(2,1)} %constant.18.clone.cards_ref) | copy-start | bytes 958468
  15.4 0.8 %copy-start.1 = (f32[81,81]{1,0:T(8,128)S(1)}, f32[81,81]{1,0:T(8,128)}, u32[]{:S(2)}) copy-start(f32[81,81]{1,0:T(8,128)} %fine_ref.1) | copy-start | bytes 78736
  16.1 0.7 %copy-start.2 = (f32[24,24]{1,0:T(8,128)S(1)}, f32[24,24]{1,0:T(8,128)}, u32[]{:S(2)}) copy-start(f32[24,24]{1,0:T(8,128)} %coarse_ref.1) | copy-start | bytes 6916
  22.3 2.7 %collective-permute-start.4 = (f32[104,512]{1,0:T(8,128)S(1)}, f32[104,512]{1,0:T(8,128)S(1)}, u32[]{:S(2)}, u32[]{:S(2)}) collective-permute-start(f32[104,512]{1,0:T(8,128)S(1)} %collective-permute-done.2.refs_2_), channel_id=1, source_target_pairs={{0,1},{1,0},{2,3},{3,2},{4,5},{5,4},{6,7},{7,6},{8,9},{9,8},{10,11... | collective-permute-start | bytes 638984 | tf_op jit(solution)/shard_map/ppermute | solution.py:720
  23.4 1.6 %collective-permute-start.3 = (f32[104,512]{1,0:T(8,128)S(1)}, f32[104,512]{1,0:T(8,128)S(1)}, u32[]{:S(2)}, u32[]{:S(2)}) collective-permute-start(f32[104,512]{1,0:T(8,128)S(1)} %collective-permute-done.1.refs_1_), channel_id=1, source_target_pairs={{0,1},{1,0},{2,3},{3,2},{4,5},{5,4},{6,7},{7,6},{8,9},{9,8},{10,11... | collective-permute-start | bytes 638984 | tf_op jit(solution)/shard_map/ppermute | solution.py:720
  23.4 1.6 %collective-permute-start.6 = (f32[56,512]{1,0:T(8,128)S(1)}, f32[56,512]{1,0:T(8,128)S(1)}, u32[]{:S(2)}, u32[]{:S(2)}) collective-permute-start(f32[56,512]{1,0:T(8,128)S(1)} %collective-permute-done.5.refs_5_), channel_id=1, source_target_pairs={{0,1},{1,0},{2,3},{3,2},{4,5},{5,4},{6,7},{7,6},{8,9},{9,8},{10,11... | collective-permute-start | bytes 344072 | tf_op jit(solution)/shard_map/ppermute | solution.py:720
  34.3 16.4 %collective-permute-start.11 = (f32[4,24,1024]{2,1,0:T(8,128)S(1)}, f32[4,24,1024]{2,1,0:T(8,128)S(1)}, u32[]{:S(2)}, u32[]{:S(2)}) collective-permute-start(f32[4,24,1024]{2,1,0:T(8,128)S(1)} %get-tuple-element.23.refs_1_), channel_id=1, source_target_pairs={{0,2},{3,1},{2,4},{5,3},{4,6},{7,5},{6,8},{9,7},{8,10},{11,9},{10,... | collective-permute-start | bytes 1179656 | tf_op jit(solution)/shard_map/ppermute | solution.py:729
  36.4 5.8 %collective-permute-start.9 = (f32[24,1024]{1,0:T(8,128)S(1)}, f32[24,1024]{1,0:T(8,128)S(1)}, u32[]{:S(2)}, u32[]{:S(2)}) collective-permute-start(f32[24,1024]{1,0:T(8,128)S(1)} %get-tuple-element.20.refs_0_), channel_id=1, source_target_pairs={{0,4},{5,1},{2,6},{7,3},{4,8},{9,5},{6,10},{11,7},{8,12},{13,9},{1... | collective-permute-start | bytes 294920 | tf_op jit(solution)/shard_map/ppermute | solution.py:729
  38.3 9.6 %collective-permute-start.7 = (f32[24,1024]{1,0:T(8,128)S(1)}, f32[24,1024]{1,0:T(8,128)S(1)}, u32[]{:S(2)}, u32[]{:S(2)}) collective-permute-start(f32[24,1024]{1,0:T(8,128)S(1)} %get-tuple-element.20.refs_0_), channel_id=1, source_target_pairs={{0,2},{3,1},{2,4},{5,3},{4,6},{7,5},{6,8},{9,7},{8,10},{11,9},{10,... | collective-permute-start | bytes 294920 | tf_op jit(solution)/shard_map/ppermute | solution.py:729
  42.2 8.5 %collective-permute-start.10 = (f32[24,1024]{1,0:T(8,128)S(1)}, f32[24,1024]{1,0:T(8,128)S(1)}, u32[]{:S(2)}, u32[]{:S(2)}) collective-permute-start(f32[24,1024]{1,0:T(8,128)S(1)} %collective-permute-done.9.refs_3_), channel_id=1, source_target_pairs={{0,1},{1,0},{2,3},{3,2},{4,5},{5,4},{6,7},{7,6},{8,9},{9,8},{10,11... | collective-permute-start | bytes 294920 | tf_op jit(solution)/shard_map/ppermute | solution.py:720
  48.0 3.7 %collective-permute-start.8 = (f32[24,1024]{1,0:T(8,128)S(1)}, f32[24,1024]{1,0:T(8,128)S(1)}, u32[]{:S(2)}, u32[]{:S(2)}) collective-permute-start(f32[24,1024]{1,0:T(8,128)S(1)} %collective-permute-done.7.refs_1_), channel_id=1, source_target_pairs={{0,1},{1,0},{2,3},{3,2},{4,5},{5,4},{6,7},{7,6},{8,9},{9,8},{10,11... | collective-permute-start | bytes 294920 | tf_op jit(solution)/shard_map/ppermute | solution.py:720
  50.7 5.9 %collective-permute-start.12 = (f32[4,24,1024]{2,1,0:T(8,128)S(1)}, f32[4,24,1024]{2,1,0:T(8,128)S(1)}, u32[]{:S(2)}, u32[]{:S(2)}) collective-permute-start(f32[4,24,1024]{2,1,0:T(8,128)S(1)} %collective-permute-done.11.refs_2_), channel_id=1, source_target_pairs={{0,1},{1,0},{2,3},{3,2},{4,5},{5,4},{6,7},{7,6},{8,9},{9,8},{10,11... | collective-permute-start | bytes 1179656 | tf_op jit(solution)/shard_map/ppermute | solution.py:720
